TPU v7x, 128 devices: a whole 4x4x4 slice. The times are simulated.
128 devices in a mesh: visit: 8 (over y, core), region: 16 (over x, z).
Axes of the slice: x: 4, y: 4, z: 4, core: 2. Of those that a mesh axis runs over, the one named last changes fastest.
Arguments:
- image: bfloat16 [32, 4096, 2048], P('visit', 'region'), may hold values from -8 to 8
- variance: bfloat16 [32, 4096, 2048], P('visit', 'region'), may hold values from 0.25 to 24
- psf_coef: float32 [32, 3], P('visit'), may hold values from 0.2 to 1
- correlations: int32 [32, 2], replicated, may hold values from 0 to 7, all different within a row; in each aligned block of 4 rows (0 to 3, 4 to 7, ...) at most 2 rows name the same one
- row_start: int32 [32, 2, 1024], replicated, may hold values from -514 to 4614, as said below
- row_frac: float32 [32, 2, 1024], replicated, may hold values from 0 to 1
- col_start: int32 [32, 2, 4096], replicated, may hold values from -2050 to 4132, as said below
- col_frac: float32 [32, 2, 4096], replicated, may hold values from 0 to 1
Outputs:
- coadd: float32 [8, 1024, 4096], P('visit', None, 'region')
- weight_map: float32 [8, 1024, 4096], P('visit', None, 'region')
Inputs may be any that keep to these rules, and one draw needn't show every extreme that they name: `correlations`: each exposure names 2 different patches. Among the 4 exposures of one index of visit (aligned blocks of 4 rows) no patch is named more than 2 times, a bound that some block reaches. Along one correlation's patch rows, row_start never falls and rises by at most 2 from one row to the next. Along one correlation's patch columns, col_start never falls and rises by at most 2 from one column to the next.
All inputs are finite; a program needn't handle non-finite values.
Results may differ from a plain program's by a relative error of at most 0.0042.
Values may be sent and summed in bfloat16 or wider, within the bound.
No kernel may reach another device: no remote copies, remote signals or barrier semaphores. Data moves between devices by JAX's collectives and lax.ppermute only.
A program may use at most 192 MiB of HBM per device.

v0:
```python
import jax
import jax.numpy as jnp
from jax import lax
from jax.sharding import PartitionSpec as P

RADIUS = 10


tap_count = 6
block_rows = 128
sigma_list = (1.0, 2.0, 4.0)
floor_share = 0.5


def padded_2(block, sides, width):
    for axis, dim in sides:
        count = lax.axis_size(axis)
        forward = [(i, i + 1) for i in range(count - 1)]
        backward = [(target, source) for source, target in forward]
        low = lax.ppermute(
            lax.slice_in_dim(block, block.shape[dim] - width, None, axis=dim), axis, forward
        )
        high = lax.ppermute(lax.slice_in_dim(block, 0, width, axis=dim), axis, backward)
        block = jnp.concatenate([low, block, high], axis=dim)
    return block


def psf_kernel(coefficient):
    offsets = jnp.arange(-RADIUS, RADIUS + 1).astype(coefficient.dtype)
    sigmas = jnp.array(sigma_list, dtype=coefficient.dtype)
    gaussians = jnp.exp(
        -(offsets[None, :] * offsets[None, :]) / (2.0 * sigmas[:, None] * sigmas[:, None])
    )
    kernel = jnp.sum(coefficient[:, :, None] * gaussians[None, :, :], axis=1)
    return kernel / jnp.sum(kernel, axis=1, keepdims=True)


def lanczos_taps(fraction):
    tap_index = jnp.arange(tap_count).astype(fraction.dtype)
    distance = 2.0 + fraction[..., None, :] - tap_index[:, None]
    kernel_val = jnp.sinc(distance) * jnp.sinc(distance / 3.0)
    kernel_val = kernel_val / jnp.sum(kernel_val, axis=-2, keepdims=True)
    return kernel_val.astype(jnp.bfloat16)


def coverage(start_at, tap_weights, extent):
    running = jnp.zeros(start_at.shape, jnp.float32)
    for tap_at in range(tap_count):
        position = start_at + tap_at
        inside = (position >= 0) & (position < extent)
        running = running + jnp.where(inside, tap_weights[..., tap_at, :].astype(jnp.float32), 0.0)
    return running


def band_matrix(starts, tap_weights, first_row, window):
    offset = (
        first_row[:, None, None]
        + jnp.arange(window, dtype=jnp.int32)[None, :, None]
        - starts[:, None, :]
    )
    matrix = jnp.zeros(offset.shape, jnp.bfloat16)
    for tap_at in range(tap_count):
        matrix = jnp.where(offset == tap_at, tap_weights[tap_at][:, None, :], matrix)
    return matrix


def resample(source, start_at, tap_weights, along_axis):
    extent = source.shape[along_axis]
    out_count = start_at.shape[0]
    block_len = min(block_rows, out_count)
    block_num = out_count // block_len
    window = min(3 * block_rows, extent)
    starts = start_at.reshape(block_num, block_len)
    first_row = jnp.clip(starts[:, 0], 0, extent - window)
    pieces = jax.vmap(lambda row_at: lax.dynamic_slice_in_dim(source, row_at, window, along_axis))(
        first_row
    )
    matrix = band_matrix(
        starts, tap_weights.reshape(tap_count, block_num, block_len), first_row, window
    )
    if along_axis == 1:
        result = jnp.einsum("brw,bwq->rbq", pieces, matrix, preferred_element_type=jnp.float32)
        return result.reshape(source.shape[0], out_count)
    result = jnp.einsum("bwq,bwc->bqc", matrix, pieces, preferred_element_type=jnp.float32)
    return result.reshape(out_count, source.shape[1])


def local(image, variance, psf_coef, correlations, row_start, row_frac, col_start, col_frac):
    exp_dev, height, width = image.shape
    correlation_count = correlations.shape[1]
    patch_rows = row_start.shape[2]
    patch_cols = col_start.shape[2]
    patches = lax.axis_size("visit")
    rows_all = height * lax.axis_size("region")
    block_cols = patch_cols // lax.axis_size("region")
    visit_at = lax.axis_index("visit")
    col_first = lax.axis_index("region") * block_cols
    first_exp = visit_at * exp_dev
    slot_total = exp_dev * correlation_count

    def local_rows(table):
        return lax.dynamic_slice_in_dim(table, first_exp, exp_dev, 0)

    def column_block(table):
        return lax.dynamic_slice_in_dim(table, col_first, block_cols, table.ndim - 1)

    local_sums = jnp.sum(variance.astype(jnp.float32), axis=(1, 2))
    placed = lax.dynamic_update_slice(
        jnp.zeros((correlations.shape[0],), jnp.float32), local_sums, (first_exp,)
    )
    totals = lax.psum(placed, ("visit", "region"))
    weight = 1.0 / (totals / (rows_all * width))
    mean_weight = jnp.mean(weight)
    kernels = psf_kernel(psf_coef)
    padded = padded_2(image, (("region", 1),), RADIUS)
    running = jnp.zeros(image.shape, jnp.float32)
    for tap_at in range(2 * RADIUS + 1):
        running = running + kernels[:, tap_at, None, None] * padded[
            :, tap_at : tap_at + height, :
        ].astype(jnp.float32)
    widened = jnp.pad(running, ((0, 0), (0, 0), (RADIUS, RADIUS)))
    blurred = jnp.zeros(image.shape, jnp.float32)
    for tap_at in range(2 * RADIUS + 1):
        blurred = blurred + kernels[:, tap_at, None, None] * widened[:, :, tap_at : tap_at + width]
    matched = blurred.astype(jnp.bfloat16)
    col_taps = lanczos_taps(local_rows(col_frac))
    col_starts = local_rows(col_start)

    def warp_exposure(packed):
        matched_one, starts_one, taps_one = packed
        return jnp.stack(
            [
                resample(matched_one, starts_one[slot_at], taps_one[slot_at], 1).astype(
                    jnp.bfloat16
                )
                for slot_at in range(correlation_count)
            ]
        )

    warped_cols = lax.map(warp_exposure, (matched, col_starts, col_taps)).reshape(
        slot_total, height, patch_cols
    )
    slot_owner = local_rows(correlations).reshape(slot_total)
    slot_weight = jnp.repeat(local_rows(weight), correlation_count)
    strips = lax.all_to_all(warped_cols, "region", split_axis=2, concat_axis=1, tiled=True)
    slot_starts = local_rows(row_start).reshape(slot_total, patch_rows)
    slot_taps = lanczos_taps(local_rows(row_frac)).reshape(slot_total, tap_count, patch_rows)
    empty_sum = jnp.zeros((patches, patch_rows, block_cols), jnp.float32)
    slot_rows = coverage(slot_starts, slot_taps, rows_all)
    slot_cols = coverage(
        column_block(local_rows(col_start)).reshape(slot_total, block_cols),
        lanczos_taps(column_block(local_rows(col_frac))).reshape(slot_total, tap_count, block_cols),
        width,
    )

    def add_both(sums, packed):
        strip, starts_one, taps_one, owner_one, weight_one, rows_one, cols_one = packed
        summed_part = (
            sums[0].at[owner_one].add(weight_one * resample(strip, starts_one, taps_one, 0))
        )
        scaled = weight_one * rows_one[:, None]
        cover_part = sums[1].at[owner_one].add(scaled * cols_one[None, :])
        return ((summed_part, cover_part), None)

    (summed, weight_sum), unused = lax.scan(
        add_both,
        (empty_sum, empty_sum),
        (strips, slot_starts, slot_taps, slot_owner, slot_weight, slot_rows, slot_cols),
    )
    summed, weight_map = (
        lax.psum_scatter(summed, "visit", scatter_dimension=0, tiled=True),
        lax.psum_scatter(weight_sum, "visit", scatter_dimension=0, tiled=True),
    )
    coadd = summed / jnp.maximum(weight_map, floor_share * mean_weight)
    return (coadd, weight_map)


def solution(mesh):
    placed = (
        P("visit", "region", None),
        P("visit", "region", None),
        P("visit", None),
        P(),
        P(),
        P(),
        P(),
        P(),
    )
    return jax.shard_map(
        local,
        mesh=mesh,
        in_specs=placed,
        out_specs=(P("visit", None, "region"), P("visit", None, "region")),
        check_vma=False,
    )
```

profile of v0, /device:TPU:4, one launch (start us, length us, event | category | flops | bytes accessed | tf_op | source)
XLA Modules:
  0.0 1509.4 jit_solution(12444169609503189756)
XLA Ops:
  27.7 39.8 %multiply_add_fusion = f32[4,256,2048]{2,1,0:T(8,128)} fusion(bf16[4,256,2048]{2,1,0:T(8,128)(2,1)} %param.20, bf16[4,10,2048]{2,1,0:T(8,128)(2,1)S(1)} %collective-permute-done, bf16[4,266,2048]{2,1,0:T(8,128)(2,1)} %constant_dynamic-update-slice_fusion, f32[4]{0:T(128)S(1)} %get-tuple-element.217, f32[4]{0:T(128)S(1)} %get-tuple-element.218, ...), kind=kLoop, calls=%fused_computation.195 | loop fusion | flops 192937984 | bytes 54690128 | tf_op jit(solution)/shard_map/add | solution.py:118
  67.5 101.0 %add_convert_fusion = bf16[4,256,2048]{2,1,0:T(8,128)(2,1)} fusion(f32[4,256,2048]{2,1,0:T(8,128)} %multiply_add_fusion, f32[4]{0:T(128)S(1)} %get-tuple-element.217, f32[4]{0:T(128)S(1)} %get-tuple-element.218, f32[4]{0:T(128)S(1)} %get-tuple-element.219, f32[4]{0:T(128)S(1)} %get-tuple-element.220, f32[4]{0:T(128)S(1)} %get-tuple-element.221, ...), kind=kLoop, calls=%fused_computation.168 | loop fusion | flops 88080384 | bytes 12583248 | tf_op jit(solution)/shard_map/convert_element_type | solution.py:125
  168.5 645.8 %while.32 = (s32[]{:T(128)}, bf16[4,2,256,4096]{2,3,1,0:T(8,128)(2,1)}, s32[4,2,4096]{2,1,0:T(2,128)S(1)}, bf16[4,2,6,4096]{3,2,1,0:T(8,128)(2,1)S(1)}, bf16[4,2...) while((s32[]{:T(128)}, ...), condition=%wide.region_4.6_spmd, body=%wide.region_3.5_spmd.sunk | while | flops 1662017792 | bytes 45421432 | solution.py:140
  174.4 68.2 %while.36 = (s32[]{:T(128)}, bf16[256,2048]{1,0:T(8,128)(2,1)S(1)}, s32[32,2]{1,0:T(8,128)S(1)}, bf16[32,256,384]{2,1,0:T(8,128)(2,1)}, s32[]{:T(128)}) while((s32[]{:T(128)}, bf16[256,2048]{1,0:T(8,128)(2,1)S(1)}, s32[32,2]{1,0:T(8,128)S(1)}, bf16[32,256,384]{2,1,0:T(8,128)(2,1)}, s32[]{:T(128)}) %tuple.179), condition=%wide.while_cond.2, body=%wide.while_body.2.sunk | while | flops 2 | bytes 394329 | solution.py:75
  242.7 6.5 fusion.300
  253.0 68.2 %while.35 = (s32[]{:T(128)}, bf16[256,2048]{1,0:T(8,128)(2,1)S(1)}, s32[32,2]{1,0:T(8,128)S(1)}, bf16[32,256,384]{2,1,0:T(8,128)(2,1)}, s32[]{:T(128)}) while((s32[]{:T(128)}, bf16[256,2048]{1,0:T(8,128)(2,1)S(1)}, s32[32,2]{1,0:T(8,128)S(1)}, bf16[32,256,384]{2,1,0:T(8,128)(2,1)}, s32[]{:T(128)}) %tuple.192), condition=%wide.while_cond.3, body=%wide.while_body.3.sunk | while | flops 2 | bytes 394329 | solution.py:75
  321.3 6.6 fusion.298
  335.8 68.2 %while.36 = (s32[]{:T(128)}, bf16[256,2048]{1,0:T(8,128)(2,1)S(1)}, s32[32,2]{1,0:T(8,128)S(1)}, bf16[32,256,384]{2,1,0:T(8,128)(2,1)}, s32[]{:T(128)}) while((s32[]{:T(128)}, bf16[256,2048]{1,0:T(8,128)(2,1)S(1)}, s32[32,2]{1,0:T(8,128)S(1)}, bf16[32,256,384]{2,1,0:T(8,128)(2,1)}, s32[]{:T(128)}) %tuple.179), condition=%wide.while_cond.2, body=%wide.while_body.2.sunk | while | flops 2 | bytes 394329 | solution.py:75
  404.1 6.5 fusion.300
  414.4 68.2 %while.35 = (s32[]{:T(128)}, bf16[256,2048]{1,0:T(8,128)(2,1)S(1)}, s32[32,2]{1,0:T(8,128)S(1)}, bf16[32,256,384]{2,1,0:T(8,128)(2,1)}, s32[]{:T(128)}) while((s32[]{:T(128)}, bf16[256,2048]{1,0:T(8,128)(2,1)S(1)}, s32[32,2]{1,0:T(8,128)S(1)}, bf16[32,256,384]{2,1,0:T(8,128)(2,1)}, s32[]{:T(128)}) %tuple.192), condition=%wide.while_cond.3, body=%wide.while_body.3.sunk | while | flops 2 | bytes 394329 | solution.py:75
  482.7 6.5 fusion.298
  497.2 68.2 %while.36 = (s32[]{:T(128)}, bf16[256,2048]{1,0:T(8,128)(2,1)S(1)}, s32[32,2]{1,0:T(8,128)S(1)}, bf16[32,256,384]{2,1,0:T(8,128)(2,1)}, s32[]{:T(128)}) while((s32[]{:T(128)}, bf16[256,2048]{1,0:T(8,128)(2,1)S(1)}, s32[32,2]{1,0:T(8,128)S(1)}, bf16[32,256,384]{2,1,0:T(8,128)(2,1)}, s32[]{:T(128)}) %tuple.179), condition=%wide.while_cond.2, body=%wide.while_body.2.sunk | while | flops 2 | bytes 394329 | solution.py:75
  565.5 6.6 fusion.300
  575.8 68.2 %while.35 = (s32[]{:T(128)}, bf16[256,2048]{1,0:T(8,128)(2,1)S(1)}, s32[32,2]{1,0:T(8,128)S(1)}, bf16[32,256,384]{2,1,0:T(8,128)(2,1)}, s32[]{:T(128)}) while((s32[]{:T(128)}, bf16[256,2048]{1,0:T(8,128)(2,1)S(1)}, s32[32,2]{1,0:T(8,128)S(1)}, bf16[32,256,384]{2,1,0:T(8,128)(2,1)}, s32[]{:T(128)}) %tuple.192), condition=%wide.while_cond.3, body=%wide.while_body.3.sunk | while | flops 2 | bytes 394329 | solution.py:75
  644.1 6.6 fusion.298
  658.6 68.2 %while.36 = (s32[]{:T(128)}, bf16[256,2048]{1,0:T(8,128)(2,1)S(1)}, s32[32,2]{1,0:T(8,128)S(1)}, bf16[32,256,384]{2,1,0:T(8,128)(2,1)}, s32[]{:T(128)}) while((s32[]{:T(128)}, bf16[256,2048]{1,0:T(8,128)(2,1)S(1)}, s32[32,2]{1,0:T(8,128)S(1)}, bf16[32,256,384]{2,1,0:T(8,128)(2,1)}, s32[]{:T(128)}) %tuple.179), condition=%wide.while_cond.2, body=%wide.while_body.2.sunk | while | flops 2 | bytes 394329 | solution.py:75
  726.9 6.5 fusion.300
  737.2 68.2 %while.35 = (s32[]{:T(128)}, bf16[256,2048]{1,0:T(8,128)(2,1)S(1)}, s32[32,2]{1,0:T(8,128)S(1)}, bf16[32,256,384]{2,1,0:T(8,128)(2,1)}, s32[]{:T(128)}) while((s32[]{:T(128)}, bf16[256,2048]{1,0:T(8,128)(2,1)S(1)}, s32[32,2]{1,0:T(8,128)S(1)}, bf16[32,256,384]{2,1,0:T(8,128)(2,1)}, s32[]{:T(128)}) %tuple.192), condition=%wide.while_cond.3, body=%wide.while_body.3.sunk | while | flops 2 | bytes 394329 | solution.py:75
  805.5 6.5 fusion.298
  814.3 17.9 %copy.83 = bf16[8,256,4096]{1,0,2:T(8,128)(2,1)} copy(bf16[8,256,4096]{1,2,0:T(8,128)(2,1)} %bitcast.218) | data formatting | bytes 33554432 | tf_op jit(solution)/shard_map/reshape | solution.py:140
  832.2 8.5 all-to-all-start
  843.9 346.4 %psum.7 = f32[32]{0:T(128)S(1)} all-reduce(f32[32]{0:T(128)S(1)} %dynamic_update_slice.7), channel_id=1, replica_groups=mesh['visit'=8,'region'=16] {'visit','region'}, use_global_device_ids=true, to_apply=%region_7.10 | all-reduce | flops 32 | bytes 256 | tf_op jit(solution)/shard_map/psum | solution.py:111
  1196.1 23.3 %copy.76 = bf16[8,16,256,256]{3,2,1,0:T(8,128)(2,1)} copy(bf16[8,16,256,256]{2,0,3,1:T(8,128)(2,1)} %bitcast.20) | data formatting | bytes 33554432 | tf_op jit(solution)/shard_map/all_to_all | solution.py:145
  1227.3 165.7 %while.34 = (s32[]{:T(128)}, f32[8,1024,256]{2,1,0:T(8,128)}, f32[8,1024,256]{2,1,0:T(8,128)}, s32[8]{0:T(128)S(1)}, f32[8]{0:T(128)S(1)}, /*index=5*/s32[8,1024...) while((s32[]{:T(128)}, f32[8,1024,256]{2,1,0:T(8,128)}, ...), condition=%wide.region_11.15_spmd, body=%wide.region_9.14_spmd.sunk | while | flops 208015424 | bytes 12543201 | solution.py:165
  1229.2 6.2 while.37
  1249.9 6.2 while.37
  1312.0 6.2 while.37
  1332.7 6.2 while.37
  1353.4 6.2 while.37
  1374.2 6.2 while.37
  1394.4 50.5 %reduce-scatter.3.cloned.1.call-done = f32[1,1024,256]{2,1,0:T(8,128)} async-done(((f32[8,1024,256]{2,1,0:T(8,128)}), f32[1,1024,256]{2,1,0:T(8,128)}) %reduce-scatter.3.cloned.1.call-update) | async-done | bytes 1048592 | tf_op jit(solution)/shard_map/reduce_scatter | solution.py:171
  1444.9 55.0 %reduce-scatter.5.cloned.1.call-done = f32[1,1024,256]{2,1,0:T(8,128)} async-done(((f32[8,1024,256]{2,1,0:T(8,128)}), f32[1,1024,256]{2,1,0:T(8,128)}) %reduce-scatter.5.cloned.1.call-update) | async-done | bytes 1048592 | tf_op jit(solution)/shard_map/reduce_scatter | solution.py:172
  (1159 shorter events, 796.0 us)
Async XLA Ops:
  7.2 1183.1 %copy-start = (s32[32,2,1024]{2,1,0:T(2,128)S(1)}, s32[32,2,1024]{2,1,0:T(2,128)}, u32[]{:S(2)}) copy-start(s32[32,2,1024]{2,1,0:T(2,128)} %param.24) | copy-start | bytes 786436
  7.2 15.8 %copy-start.10 = (f32[3]{0:T(128)S(1)}, f32[3]{0:T(128)}, u32[]{:S(2)}) copy-start(f32[3]{0:T(128)} %constant.351) | copy-start | bytes 40
  7.2 13.8 copy-start.6
  8.4 18.6 %collective-permute-start.1 = (bf16[4,10,2048]{2,1,0:T(8,128)(2,1)S(1)}, bf16[4,10,2048]{2,1,0:T(8,128)(2,1)S(1)}, u32[]{:S(2)}, u32[]{:S(2)}) collective-permute-start(bf16[4,10,2048]{2,1,0:T(8,128)(2,1)S(1)} %get-tuple-element.303), channel_id=1, source_target_pairs={{1,0},{2,1},{3,2},{4,3},{5,4},{6,5},{7,6},{8,7},{9,8},{10,9},{11,1... | collective-permute-start | bytes 491528 | tf_op jit(solution)/shard_map/ppermute | solution.py:23
  14.3 13.4 collective-permute-start
  21.0 5.3 copy-start.7
  168.7 0.8 copy-start.1
  168.7 0.8 copy-start.3
  327.9 2.2 copy-start.2
  327.9 2.2 copy-start.4
  330.1 0.8 copy-start.1
  330.1 0.8 copy-start.3
  489.2 2.3 copy-start.2
  489.2 2.3 copy-start.4
  491.5 0.8 copy-start.1
  491.5 0.8 copy-start.3
  650.6 2.3 copy-start.2
  650.6 2.3 copy-start.4
  652.9 0.8 copy-start.1
  652.9 0.8 copy-start.3
  812.0 2.3 copy-start.2
  812.1 2.3 copy-start.4
  832.2 359.0 %copy-start.8 = (f32[6]{0:T(128)S(1)}, f32[6]{0:T(128)}, u32[]{:S(2)}) copy-start(f32[6]{0:T(128)} %copy-done.7) | copy-start | bytes 76
  832.2 361.9 %copy-start.9 = (s32[32,2]{0,1:T(2,128)S(1)}, s32[32,2]{0,1:T(2,128)}, u32[]{:S(2)}) copy-start(s32[32,2]{0,1:T(2,128)} %param.23) | copy-start | bytes 772
  832.2 363.9 %all-to-all-start = ((bf16[8,256,4096]{1,0,2:T(8,128)(2,1)}), bf16[8,256,4096]{1,0,2:T(8,128)(2,1)}, u32[]{:S(2)}, u32[]{:S(2)}) async-start(bf16[8,256,4096]{1,0,2:T(8,128)(2,1)} %copy.83), calls=%async_computation | async-start | bytes 33554432 | tf_op jit(solution)/shard_map/all_to_all | solution.py:145
  840.7 604.1 %reduce-scatter.3.cloned.1.call-start = ((), (), s32[]{:S(2)}) async-start(), calls=%async_computation.3 | async-start | bytes 9437184 | tf_op jit(solution)/shard_map/reduce_scatter | solution.py:171
  1219.4 7.9 copy-start.5
  1393.0 106.9 %reduce-scatter.5.cloned.1.call-start = ((), (), s32[]{:S(2)}) async-start(), calls=%async_computation.4 | async-start | bytes 9437184 | tf_op jit(solution)/shard_map/reduce_scatter | solution.py:172
Sparse Core Ops, SparseCore 0:
  1393.1 51.6 reduce-scatter.2
  1447.8 52.0 reduce-scatter.4
where the time goes:
time: 1520 us; the launch traced here: 1510 us
  local copies, waits for them, and re-layouts  715 us (47%)
  blocking collectives  346 us (23%)
  other arithmetic  209 us (14%)
  waiting for transfers between devices  106 us (7%)
  matrix products  86 us (6%)
  starting transfers between devices  16.5 us (1%)
  loops' own time  16 us (1%)
    gather x896, local copies, waits for them, and re-layouts  594 us
    psum x1, blocking collectives, local(): totals = lax.psum(placed, ('visit', 'region'))  346 us
    convert_element_type x1, other arithmetic, local(): matched = blurred.astype(jnp.bfloat16)  101 us
    reduce_scatter x1, waiting for transfers between devices, local(): lax.psum_scatter(weight_sum, 'visit', scatter_dimension=0, tiled=True)  55 us
    dot_general x8, matrix products, resample(): jnp.einsum('brw,bwq->rbq', pieces, matrix, preferred_element_type=jnp.flo...  52.4 us
    reduce_scatter x1, waiting for transfers between devices, local(): lax.psum_scatter(summed, 'visit', scatter_dimension=0, tiled=True)  50.5 us
    add x1, other arithmetic, local(): running + kernels[:, tap_at, None, None] * padded[:, tap_at:tap_at + heig...  39.8 us
    dot_general x8, matrix products, resample(): jnp.einsum('bwq,bwc->bqc', matrix, pieces, preferred_element_type=jnp.flo...  33.6 us
  transfers between devices with their start and end apart: 5, of which 2 were waited for; matrix products, arithmetic and copies ran while one was open for 1% of the time, Pallas kernels for 0%

commit v1 on v0

v1 whole, which is shorter than its diff:
```python
import functools
import math

import jax
import jax.numpy as jnp
from jax import lax
from jax.experimental import pallas as pl
from jax.experimental.pallas import tpu as pltpu
from jax.sharding import PartitionSpec as P

RADIUS = 10
TAPS = 6
SIGMAS = (1.0, 2.0, 4.0)
FLOOR_SHARE = 0.5
BF16 = jnp.bfloat16
F32 = jnp.float32

ROW_BLOCK = 128
ROW_STEP = 224
ROW_SPAN = 256
COL_BLOCK = 128
COL_STEP = 256
COL_GROUP = 4
BLUR_BLOCK = 256
BLUR_STEP = 512
BLUR_BAND = (112, 400)
LANES = 128
CHUNKS = 2


def psf_kernel(coefficient):
    offsets = jnp.arange(-RADIUS, RADIUS + 1).astype(coefficient.dtype)
    sigmas = jnp.array(SIGMAS, dtype=coefficient.dtype)
    gaussians = jnp.exp(
        -(offsets[None, :] * offsets[None, :]) / (2.0 * sigmas[:, None] * sigmas[:, None])
    )
    kernel = jnp.sum(coefficient[:, :, None] * gaussians[None, :, :], axis=1)
    return kernel / jnp.sum(kernel, axis=1, keepdims=True)


def lanczos_taps(f):
    g = 1.0 - f
    third = math.pi / 3.0
    tiny = 1e-6
    a = jnp.sin(third * f)
    b = jnp.sin(third * g)
    c = a + b
    fg = f * g
    a_over_f = jnp.where(f < tiny, third, a / jnp.maximum(f, tiny))
    b_over_g = jnp.where(g < tiny, third, b / jnp.maximum(g, tiny))
    values = [
        b * fg / ((f + 2.0) * (f + 2.0)),
        -c * fg / ((f + 1.0) * (f + 1.0)),
        a_over_f * g,
        b_over_g * f,
        -c * fg / ((2.0 - f) * (2.0 - f)),
        a * fg / ((3.0 - f) * (3.0 - f)),
    ]
    total = functools.reduce(jnp.add, values)
    return [lax.reduce_precision(value / total, 8, 7) for value in values]


def coverage(starts, taps, extent):
    running = jnp.zeros(starts.shape, F32)
    for tap_at, tap in enumerate(taps):
        position = starts + tap_at
        inside = (position >= 0) & (position < extent)
        running = running + jnp.where(inside, tap, 0.0)
    return running


def band_tables(starts, taps):
    place = jnp.arange(8, dtype=jnp.int32)[:, None]
    diff = place - starts[..., None, :]
    at = diff & 7
    turned = jnp.zeros(diff.shape, F32)
    for tap_at, tap in enumerate(taps):
        turned = turned + jnp.where(at == tap_at, tap[..., None, :], 0.0)
    return turned, diff - at


def toeplitz(kernels, rows, cols, shift):
    diff = (
        lax.broadcasted_iota(jnp.int32, (rows, cols), 0)
        - lax.broadcasted_iota(jnp.int32, (rows, cols), 1)
        + shift
    )
    full = jnp.zeros(kernels.shape[:-1] + (rows, cols), F32)
    for tap_at in range(2 * RADIUS + 1):
        full = full + jnp.where(diff == tap_at, kernels[..., tap_at, None, None], 0.0)
    return full


def dot(a, b):
    return jnp.dot(a, b, preferred_element_type=F32)


def dot_t(a, b):
    return lax.dot_general(a, b, (((0,), (0,)), ((), ())), preferred_element_type=F32)


def two_parts(value):
    high = value.astype(BF16)
    return high, (value - high.astype(F32)).astype(BF16)


def halves_sum(value, axis):
    half = value.shape[axis] // 2
    return lax.slice_in_dim(value, 0, half, axis=axis) + lax.slice_in_dim(
        value, half, 2 * half, axis=axis
    )


def row_body(slots, low_ref, num_ref, x_ref, blur_ref, turned_ref, key_ref, out_ref, blur):
    extent = x_ref.shape[0]
    owner_rows = out_ref.shape[2]
    blocks = turned_ref.shape[0] // slots
    last = extent - ROW_STEP
    groups = ROW_SPAN // 8
    blur_high, blur_rest = two_parts(blur_ref[...])
    blur[pl.ds(0, ROW_STEP), :] = blur_high
    blur[pl.ds(ROW_STEP, ROW_STEP), :] = blur_rest

    def part(index, start, masked):
        first = pl.multiple_of(jnp.minimum(start, last), 16)
        key = key_ref[index] + (first - 16)
        turned = turned_ref[index]
        pieces = []
        for g in range(groups):
            value = jnp.where(key == -8 * g, turned, 0.0)
            if g < 2:
                value = jnp.where(first > 0, value, 0.0)
            if g >= groups - 2:
                value = jnp.where(first < last, value, 0.0)
            pieces.append(value)
        band = jnp.concatenate(pieces, axis=0).astype(BF16)
        both = halves_sum(dot(blur[...], band), 0)
        if masked:
            row = lax.broadcasted_iota(jnp.int32, both.shape, 0) + first
            both = jnp.where(row >= start, both, 0.0)
        parts = jnp.concatenate(two_parts(both), axis=1)
        return halves_sum(dot_t(parts, x_ref[pl.ds(first, ROW_STEP), :]), 0)

    def block(at, carry):
        sums = [
            part(slot * blocks + at, low_ref[slot * blocks + at], False) for slot in range(slots)
        ]
        for slot in range(slots):
            index = slot * blocks + at

            def more(i, total, index=index):
                return total + part(index, low_ref[index] + i * ROW_STEP, True)

            total = lax.fori_loop(1, num_ref[index], more, sums[slot]).astype(BF16)
            for owner in range(ROW_BLOCK // owner_rows):
                out_ref[at * (ROW_BLOCK // owner_rows) + owner, slot] = total[
                    owner * owner_rows : (owner + 1) * owner_rows
                ]
        return carry

    lax.fori_loop(0, blocks, block, 0)


def row_warp(x, low, num, blur, turned, key, slots, owners):
    width = x.shape[1]
    owner_rows = turned.shape[0] // slots * ROW_BLOCK // owners
    vmem = pl.BlockSpec(memory_space=pltpu.VMEM)
    smem = pl.BlockSpec(memory_space=pltpu.SMEM)
    return pl.pallas_call(
        functools.partial(row_body, slots),
        out_shape=jax.ShapeDtypeStruct((owners, slots, owner_rows, width), BF16),
        in_specs=[smem, smem, vmem, vmem, vmem, vmem],
        out_specs=vmem,
        scratch_shapes=[pltpu.VMEM((2 * ROW_STEP, ROW_SPAN), BF16)],
        compiler_params=pltpu.CompilerParams(vmem_limit_bytes=40 * 1024 * 1024),
        cost_estimate=pl.CostEstimate(
            flops=8_000_000_000, bytes_accessed=8 * 1024 * 1024, transcendentals=0
        ),
        name="row_warp",
    )(low, num, x, blur, turned, key)


def col_body(cols, slots, count_ref, list_ref, low_ref, num_ref, any_ref, weight_ref, z_ref,
             blur_ref, turned_ref, key_ref, out_ref, padded, blur, blurred):
    rows = z_ref.shape[2]
    width = z_ref.shape[3]
    sources = cols // width
    exposures = z_ref.shape[0] // sources
    patch = pl.program_id(0)
    begin, end = BLUR_BAND

    @pl.when(patch == 0)
    def _():
        pad = jnp.zeros((slots * rows, LANES), BF16)
        padded[:, 0:LANES] = pad
        padded[:, LANES + cols : 2 * LANES + cols] = pad
        for n in range(2):
            blur[n, 0:begin] = jnp.zeros((begin, BLUR_BLOCK), BF16)
            blur[n, end:BLUR_STEP] = jnp.zeros((BLUR_STEP - end, BLUR_BLOCK), BF16)
        for e in range(exposures):
            blur_high, blur_rest = two_parts(blur_ref[e])
            blur[0, begin:end] = blur_high
            blur[1, begin:end] = blur_rest
            for s in range(sources):
                padded[:, LANES + s * width : LANES + (s + 1) * width] = z_ref[
                    e * sources + s
                ].reshape(slots * rows, width)
            windows = jnp.concatenate(
                [
                    padded[:, b * BLUR_BLOCK : b * BLUR_BLOCK + BLUR_STEP]
                    for b in range(cols // BLUR_BLOCK)
                ],
                axis=0,
            )
            high, rest = two_parts(dot(windows, blur[0]) + dot(windows, blur[1]))
            for b in range(cols // BLUR_BLOCK):
                for j in range(slots):
                    at = (b * slots + j) * rows
                    span = slice(b * BLUR_BLOCK, (b + 1) * BLUR_BLOCK)
                    blurred[e * slots + j, 0:rows, span] = high[at : at + rows]
                    blurred[e * slots + j, rows : 2 * rows, span] = rest[at : at + rows]
            for j in range(slots):
                blurred[e * slots + j, :, cols : cols + COL_STEP] = jnp.zeros(
                    (2 * rows, COL_STEP), BF16
                )

    def part(slot, b, start):
        first = pl.multiple_of(start, LANES)
        key = key_ref[slot, b] + first
        turned = turned_ref[slot, b]
        band = jnp.concatenate(
            [jnp.where(key == -8 * g, turned, 0.0) for g in range(COL_STEP // 8)], axis=0
        ).astype(BF16)
        return halves_sum(dot(blurred[slot, :, pl.ds(first, COL_STEP)], band), 0)

    def group(c, carry):
        def add_slot(i, totals):
            slot = list_ref[patch, i]

            def work(totals):
                blocks = [c * COL_GROUP + h for h in range(COL_GROUP)]
                sums = [part(slot, b, low_ref[slot, b]) for b in blocks]
                for h, b in enumerate(blocks):

                    def more(n, total, b=b):
                        return total + part(slot, b, low_ref[slot, b] + n * COL_STEP)

                    sums[h] = lax.fori_loop(1, num_ref[slot, b], more, sums[h])
                return tuple(t + weight_ref[slot] * s for t, s in zip(totals, sums))

            return lax.cond(any_ref[slot, c] > 0, work, lambda t: t, totals)

        zero = jnp.zeros((rows, COL_BLOCK), F32)
        totals = lax.fori_loop(0, count_ref[patch], add_slot, (zero,) * COL_GROUP)
        per_owner = out_ref.shape[3] // COL_BLOCK
        for h, total in enumerate(totals):
            out_ref[
                0,
                c * (COL_GROUP // per_owner) + h // per_owner,
                :,
                (h % per_owner) * COL_BLOCK : (h % per_owner + 1) * COL_BLOCK,
            ] = total.astype(BF16)
        return carry

    lax.fori_loop(0, turned_ref.shape[1] // COL_GROUP, group, 0)


def col_warp(z, count, listed, low, num, some, weight, blur, turned, key, cols, patches, owners):
    slots, rows = z.shape[1:3]
    slot_total, blocks = turned.shape[:2]
    own_cols = blocks * COL_BLOCK // owners
    vmem = pl.BlockSpec(memory_space=pltpu.VMEM)
    smem = pl.BlockSpec(memory_space=pltpu.SMEM)
    return pl.pallas_call(
        functools.partial(col_body, cols, slots),
        out_shape=jax.ShapeDtypeStruct((patches, owners, rows, own_cols), BF16),
        grid=(patches,),
        in_specs=[smem] * 6 + [vmem] * 4,
        out_specs=pl.BlockSpec((1, owners, rows, own_cols), lambda k: (k, 0, 0, 0)),
        scratch_shapes=[
            pltpu.VMEM((slots * rows, cols + 2 * LANES), BF16),
            pltpu.VMEM((2, BLUR_STEP, BLUR_BLOCK), BF16),
            pltpu.VMEM((slot_total, 2 * rows, cols + COL_STEP), BF16),
        ],
        compiler_params=pltpu.CompilerParams(
            dimension_semantics=("arbitrary",), vmem_limit_bytes=40 * 1024 * 1024
        ),
        cost_estimate=pl.CostEstimate(
            flops=8_000_000_000, bytes_accessed=8 * 1024 * 1024, transcendentals=0
        ),
        name="col_warp",
    )(count, listed, low, num, some, weight, z, blur, turned, key)


def local(image, variance, psf_coef, correlations, row_start, row_frac, col_start, col_frac):
    exp_dev, height, width = image.shape
    exposures, slots = correlations.shape
    patch_rows = row_start.shape[2]
    patch_cols = col_start.shape[2]
    visits = lax.axis_size("visit")
    regions = lax.axis_size("region")
    extent = height * regions
    parts = regions // exp_dev
    part_cols = width // parts
    own_cols = patch_cols // regions
    visit_at = lax.axis_index("visit")
    region_at = lax.axis_index("region")
    first_exp = visit_at * exp_dev
    own_exp = region_at // parts

    sent = image.reshape(exp_dev, height, parts, part_cols).transpose(0, 2, 1, 3)
    sent = sent.reshape(regions, height, part_cols)
    columns = lax.all_to_all(sent, "region", split_axis=0, concat_axis=0, tiled=True)
    columns = columns.reshape(extent, part_cols)

    local_sums = jnp.sum(variance.astype(F32), axis=(1, 2))
    tile = jnp.zeros((8, LANES), F32).at[0, :exp_dev].set(local_sums)
    gathered = lax.all_gather(tile, ("visit", "region"), axis=0, tiled=False)
    gathered = gathered[:, 0, :exp_dev].reshape(visits, regions, exp_dev)
    totals = jnp.sum(gathered, axis=1).reshape(exposures)
    weight = 1.0 / (totals / (extent * width))
    mean_weight = jnp.mean(weight)
    own_weight = lax.dynamic_slice_in_dim(weight, first_exp, exp_dev, 0)

    kernels = psf_kernel(psf_coef)

    starts = lax.dynamic_index_in_dim(row_start, first_exp + own_exp, 0, keepdims=False)
    fracs = lax.dynamic_index_in_dim(row_frac, first_exp + own_exp, 0, keepdims=False)
    blocks = patch_rows // ROW_BLOCK // CHUNKS
    chunked = (slots, CHUNKS, blocks, ROW_BLOCK)
    starts = starts.reshape(chunked).transpose(1, 0, 2, 3).reshape(CHUNKS, slots * blocks, ROW_BLOCK)
    fracs = fracs.reshape(chunked).transpose(1, 0, 2, 3).reshape(CHUNKS, slots * blocks, ROW_BLOCK)
    row_turned, row_key = band_tables(starts, lanczos_taps(fracs))
    row_low = jnp.clip(starts[..., 0] - RADIUS, 0, extent - ROW_STEP) // 16 * 16
    row_end = jnp.minimum(starts[..., -1] + TAPS + RADIUS, extent)
    row_num = jnp.maximum(row_end - row_low + ROW_STEP - 1, 0) // ROW_STEP
    row_blur = toeplitz(
        lax.dynamic_index_in_dim(kernels, own_exp, 0, keepdims=False),
        ROW_STEP, ROW_SPAN, 16 + RADIUS,
    )

    slot_total = exp_dev * slots
    col_blocks = patch_cols // COL_BLOCK
    own_starts = lax.dynamic_slice_in_dim(col_start, first_exp, exp_dev, 0)
    own_fracs = lax.dynamic_slice_in_dim(col_frac, first_exp, exp_dev, 0)
    own_starts = own_starts.reshape(slot_total, col_blocks, COL_BLOCK)
    own_fracs = own_fracs.reshape(slot_total, col_blocks, COL_BLOCK)
    col_turned, col_key = band_tables(own_starts, lanczos_taps(own_fracs))
    col_low = jnp.clip(own_starts[:, :, 0], 0, width) // LANES * LANES
    col_end = jnp.minimum(own_starts[:, :, -1] + TAPS, width)
    col_num = jnp.maximum(col_end - col_low + COL_STEP - 1, 0) // COL_STEP
    col_some = jnp.sum(col_num.reshape(slot_total, col_blocks // COL_GROUP, COL_GROUP), axis=2)
    col_blur = toeplitz(
        kernels, BLUR_BAND[1] - BLUR_BAND[0], BLUR_BLOCK, BLUR_BAND[0] - LANES + RADIUS
    )
    owners = lax.dynamic_slice_in_dim(correlations, first_exp, exp_dev, 0).reshape(slot_total)
    named = owners[None, :] == jnp.arange(visits, dtype=jnp.int32)[:, None]
    count = jnp.sum(named.astype(jnp.int32), axis=1)
    rank = jnp.cumsum(named.astype(jnp.int32), axis=1) - 1
    slot_ids = jnp.arange(slot_total, dtype=jnp.int32)
    listed = jnp.stack(
        [
            jnp.sum(jnp.where(named & (rank == i), slot_ids[None, :], 0), axis=1)
            for i in range(slot_total)
        ],
        axis=1,
    ).astype(jnp.int32)
    slot_weight = jnp.repeat(own_weight, slots)

    pieces = []
    for h in range(CHUNKS):
        row_warped = row_warp(
            columns, row_low[h], row_num[h], row_blur, row_turned[h], row_key[h], slots, regions
        )
        rows = lax.all_to_all(row_warped, "region", split_axis=0, concat_axis=0, tiled=True)
        partial = col_warp(
            rows, count, listed, col_low, col_num, col_some, slot_weight, col_blur,
            col_turned, col_key, width, visits, regions,
        )
        summed = lax.psum_scatter(partial, "visit", scatter_dimension=0, tiled=True)
        summed = lax.all_to_all(summed[0], "region", split_axis=0, concat_axis=0, tiled=True)
        pieces.append(summed.reshape(1, patch_rows // CHUNKS, own_cols))
    summed = jnp.concatenate(pieces, axis=1).astype(F32)

    total_slots = exposures * slots
    row_cover = coverage(
        row_start.reshape(total_slots, patch_rows),
        lanczos_taps(row_frac.reshape(total_slots, patch_rows)),
        extent,
    )
    at = region_at * own_cols
    col_cover = coverage(
        lax.dynamic_slice_in_dim(col_start, at, own_cols, 2).reshape(total_slots, own_cols),
        lanczos_taps(
            lax.dynamic_slice_in_dim(col_frac, at, own_cols, 2).reshape(total_slots, own_cols)
        ),
        width,
    )
    scale = jnp.where(
        correlations.reshape(total_slots) == visit_at, jnp.repeat(weight, slots), 0.0
    )
    weight_map = lax.dot_general(
        row_cover,
        col_cover * scale[:, None],
        (((0,), (0,)), ((), ())),
        precision=lax.Precision.HIGHEST,
        preferred_element_type=F32,
    ).reshape(1, patch_rows, own_cols)
    coadd = summed / jnp.maximum(weight_map, FLOOR_SHARE * mean_weight)
    return coadd, weight_map


def solution(mesh):
    placed = (
        P("visit", "region", None),
        P("visit", "region", None),
        P("visit", None),
        P(),
        P(),
        P(),
        P(),
        P(),
    )
    return jax.shard_map(
        local,
        mesh=mesh,
        in_specs=placed,
        out_specs=(P("visit", None, "region"), P("visit", None, "region")),
        check_vma=False,
    )
```

time: 1520 us -> 295 us (0.19)
  local copies, waits for them, and re-layouts: 715 us -> 17.7 us
  blocking collectives: 346 us -> 110 us
  other arithmetic: 209 us -> 50.9 us
  matrix products: 86 us -> 1.03 us
  waiting for transfers between devices: 106 us -> 22.6 us
  Pallas kernels: 0 us -> 47 us
  loops' own time: 16 us -> 0 us
    gather x896 -> x0, local copies, waits for them, and re-layouts: 594 us -> none
    psum x1 -> x0, blocking collectives: 346 us -> none  [local(): totals = lax.psum(placed, ('visit', 'region'))]
    convert_element_type x3 -> x1, other arithmetic: 102 us -> 0.01 us  [local(): count = jnp.sum(named.astype(jnp.int32), axis=1)]
    reduce_scatter x2, waiting for transfers between devices: 105 us -> 10 us  [local(): summed = lax.psum_scatter(partial, 'visit', scatter_dimension=0, tiled=True)]
    all_gather x0 -> x1, blocking collectives: none -> 92.2 us  [local(): gathered = lax.all_gather(tile, ('visit', 'region'), axis=0, tiled=False)]
    dot_general x16 -> x1, matrix products: 86 us -> 1.03 us  [local(): lax.dot_general(row_cover, col_cover * scale[:, None], (((0,), (0,)), (()...]
    pallas_call x0 -> x4, Pallas kernels: none -> 47 us  [the longest x2 35.7 us: col_warp(): pl.pallas_call(functools.partial(col_body, cols, slots), out_shape=jax.Sh...]
    scatter-add x8 -> x0, other arithmetic: 29.7 us -> none  [add_both(): sums[0].at[owner_one]]
  transfers between devices with their start and end apart: 5 -> 6, of which waited for: 2 -> 3; matrix products, arithmetic and copies ran while one was open for 1% -> 20% of each run, Pallas kernels for 0% -> 8%
where the time goes in v1:
time: 295 us; the launch traced here: 294 us
  blocking collectives  110 us (37%)
  other arithmetic  50.9 us (17%)
  Pallas kernels  47 us (16%)
  starting transfers between devices  29.6 us (10%)
  waiting for transfers between devices  22.6 us (8%)
  local copies, waits for them, and re-layouts  17.7 us (6%)
  between operations  15 us (5%)
    all_gather x1, blocking collectives, local(): gathered = lax.all_gather(tile, ('visit', 'region'), axis=0, tiled=False)  92.2 us
    pallas_call x2, Pallas kernels, col_warp(): pl.pallas_call(functools.partial(col_body, cols, slots), out_shape=jax.Sh...  35.7 us
    all_to_all x1, blocking collectives, local(): lax.all_to_all(row_warped, 'region', split_axis=0, concat_axis=0, tiled=T...  18.2 us
    add x2, other arithmetic, toeplitz(): full + jnp.where(diff == tap_at, kernels[..., tap_at, None, None], 0.0)  17 us
    all_to_all x2, starting transfers between devices, local(): lax.all_to_all(summed[0], 'region', split_axis=0, concat_axis=0, tiled=True)  13.2 us
    pallas_call x2, Pallas kernels, row_warp(): pl.pallas_call(functools.partial(row_body, slots), out_shape=jax.ShapeDty...  11.3 us
    add x1, other arithmetic, coverage(): running = running + jnp.where(inside, tap, 0.0)  10.2 us
    reduce_scatter x2, waiting for transfers between devices, local(): summed = lax.psum_scatter(partial, 'visit', scatter_dimension=0, tiled=True)  10 us
  transfers between devices with their start and end apart: 6, of which 3 were waited for; matrix products, arithmetic and copies ran while one was open for 20% of the time, Pallas kernels for 8%

profile of v1, /device:TPU:4, one launch (start us, length us, event | category | flops | bytes accessed | tf_op | source)
XLA Modules:
  0.0 294.4 jit_solution(12602051877420144195)
XLA Ops:
  7.2 2.6 fusion.112
  9.7 2.1 pad_maximum_fusion
  11.9 8.4 %all-to-all-start = ((bf16[16,256,512]{2,1,0:T(8,128)(2,1)}), bf16[16,256,512]{2,1,0:T(8,128)(2,1)}, u32[]{:S(2)}, u32[]{:S(2)}) async-start(bf16[16,256,512]{2,1,0:T(8,128)(2,1)} %bitcast.96), calls=%async_computation | async-start | bytes 8388608 | tf_op jit(solution)/shard_map/all_to_all | solution.py:313
  20.3 0.7 fusion.2
  24.3 1.1 slice_reduce_fusion.20
  28.2 0.8 select_reduce_fusion
  28.9 0.9 constant_dynamic-slice_fusion
  29.9 0.9 constant_dynamic-slice_fusion.4
  31.3 2.9 convert_reduce_fusion
  34.1 92.2 %all_gather.7 = f32[128,8,128]{2,1,0:T(8,128)S(1)} all-gather(f32[1,8,128]{2,1,0:T(8,128)S(1)} %scatter.4), channel_id=1, replica_groups=mesh['visit'=8,'region'=16] {'visit','region'}, dimensions={0}, use_global_device_ids=true | all-gather | bytes 528384 | tf_op jit(solution)/shard_map/all_gather | solution.py:318
  131.7 13.2 %select_add_fusion.2.blur_ref = f32[224,256]{1,0:T(8,128)S(1)} fusion(f32[]{:T(128)} %bitcast.40, f32[]{:T(128)} %bitcast.39, f32[]{:T(128)} %bitcast.38, f32[]{:T(128)} %bitcast.37, f32[]{:T(128)} %bitcast.36, f32[]{:T(128)} %bitcast.35, f32[]{:T(128)} %bitcast.34, f32[]{:T(128)} %bitcast.33, f32[]{:T(128)} %bitcast.32, f32[]{:T(128)} %bitcast.31, ...), kind=kLoop, calls=%fused_computation.72 | loop fusion | flops 3670016 | bytes 229460 | tf_op jit(solution)/shard_map/add | solution.py:90
  147.1 1.0 divide_reduce-precision_fusion.5
  148.2 1.0 divide_reduce-precision_fusion.4
  149.3 6.1 %row_warp.2 = bf16[16,2,32,512]{3,2,1,0:T(8,128)(2,1)} custom-call(s32[8]{0:T(128)S(1)} %get-tuple-element.104.low_ref, s32[8]{0:T(128)S(1)} %get-tuple-element.78.num_ref, bf16[4096,512]{1,0:T(8,128)(2,1)} %bitcast.19.x_ref, f32[224,256]{1,0:T(8,128)S(1)} %select_add_fusion.2.blur_ref, f32[8,8,128]{2,1,0:T(8,128)S(1)} %get-tuple-element.69.turned_ref, ...), custom_call_target="tpu_custom_call" | custom-call | flops 8000000000 | bytes 8388608 | tf_op jit(solution)/shard_map/row_warp/pallas_call | solution.py:169
  155.5 7.7 %all-to-all-start.1 = ((bf16[16,2,32,512]{3,2,1,0:T(8,128)(2,1)}), bf16[16,2,32,512]{3,2,1,0:T(8,128)(2,1)S(1)}, u32[]{:S(2)}, u32[]{:S(2)}) async-start(bf16[16,2,32,512]{3,2,1,0:T(8,128)(2,1)} %row_warp.2), calls=%async_computation.1 | async-start | bytes 2097152 | tf_op jit(solution)/shard_map/all_to_all | solution.py:375
  163.4 0.8 slice_reduce_fusion.19
  166.4 1.7 select_add_fusion.1.turned_ref
  168.1 3.8 %select_add_fusion.blur_ref = f32[4,288,256]{2,1,0:T(8,128)S(1)} fusion(f32[4]{0:T(128)} %get-tuple-element.27, f32[4]{0:T(128)} %get-tuple-element.28, f32[4]{0:T(128)} %get-tuple-element.29, f32[4]{0:T(128)} %get-tuple-element.30, f32[4]{0:T(128)} %get-tuple-element.31, f32[4]{0:T(128)} %get-tuple-element.32, f32[4]{0:T(128)} %get-tuple-element.33, ...), kind=kLoop, calls=%fused_computation.9 | loop fusion | flops 12091392 | bytes 2728272 | tf_op jit(solution)/shard_map/add | solution.py:90
  171.8 7.2 %all-to-all-done.1.z_ref = bf16[16,2,32,512]{3,2,1,0:T(8,128)(2,1)S(1)} async-done(((bf16[16,2,32,512]{3,2,1,0:T(8,128)(2,1)}), bf16[16,2,32,512]{3,2,1,0:T(8,128)(2,1)S(1)}, u32[]{:S(2)}, u32[]{:S(2)}) %all-to-all-start.1) | async-done | bytes 1048608 | tf_op jit(solution)/shard_map/all_to_all | solution.py:375
  179.1 1.2 copy-done
  181.6 17.9 %col_warp.2 = bf16[8,16,32,256]{3,2,1,0:T(8,128)(2,1)} custom-call(s32[8]{0:T(128)S(1)} %copy-done.3, s32[8,8]{1,0:T(8,128)S(1)} %stack.35.list_ref, s32[8,32]{1,0:T(8,128)S(1)} %get-tuple-element.77.low_ref, s32[8,32]{1,0:T(8,128)S(1)} %get-tuple-element.76.num_ref, s32[8,8]{1,0:T(8,128)S(1)} %copy.117.any_ref, f32[8]{0:T(128)S(1)} %copy-done.5, ...), custom_call_target="tpu_custom_call" | custom-call | flops 8000000000 | bytes 8388608 | tf_op jit(solution)/shard_map/col_warp/pallas_call | solution.py:274
  200.2 5.2 %row_warp.3 = bf16[16,2,32,512]{3,2,1,0:T(8,128)(2,1)S(1)} custom-call(s32[8]{0:T(128)S(1)} %copy-done.8, s32[8]{0:T(128)S(1)} %copy-done.7, bf16[4096,512]{1,0:T(8,128)(2,1)} %bitcast.19.x_ref, f32[224,256]{1,0:T(8,128)S(1)} %select_add_fusion.2.blur_ref, f32[8,8,128]{2,1,0:T(8,128)S(1)} %get-tuple-element.70.turned_ref, s32[8,8,128]{2,1,0:T(8,128)S(1)} %copy-done.2), custom_call_target="tpu_custom_call" | custom-call | flops 8000000000 | bytes 8388608 | tf_op jit(solution)/shard_map/row_warp/pallas_call | solution.py:169
  205.4 18.2 %all_to_all.25.z_ref = bf16[16,2,32,512]{3,2,1,0:T(8,128)(2,1)S(1)} all-to-all(bf16[16,2,32,512]{3,2,1,0:T(8,128)(2,1)S(1)} %row_warp.3), channel_id=1, replica_groups=mesh['visit'=8,'region'=16] {'region'}, dimensions={0} | all-to-all | bytes 2097152 | tf_op jit(solution)/shard_map/all_to_all | solution.py:375
  223.6 17.9 %col_warp.3 = bf16[8,16,32,256]{3,2,1,0:T(8,128)(2,1)} custom-call(s32[8]{0:T(128)S(1)} %copy-done.4, s32[8,8]{1,0:T(8,128)S(1)} %stack.35.list_ref, s32[8,32]{1,0:T(8,128)S(1)} %get-tuple-element.77.low_ref, s32[8,32]{1,0:T(8,128)S(1)} %get-tuple-element.76.num_ref, s32[8,8]{1,0:T(8,128)S(1)} %copy.117.any_ref, f32[8]{0:T(128)S(1)} %copy-done.6, ...), custom_call_target="tpu_custom_call" | custom-call | flops 8000000000 | bytes 8388608 | tf_op jit(solution)/shard_map/col_warp/pallas_call | solution.py:274
  242.6 10.2 %fusion.29 = f32[32,2,1024]{2,1,0:T(2,128)S(1)} fusion(s32[32,2,1024]{2,1,0:T(2,128)S(1)} %copy-done.10, f32[32,2,1024]{2,1,0:T(2,128)S(1)} %copy-done.11), kind=kLoop, calls=%fused_computation.51 | loop fusion | flops 5636096 | bytes 786432 | tf_op jit(solution)/shard_map/add | solution.py:68
  252.8 5.9 %all-to-all-start.2 = ((bf16[16,32,256]{2,1,0:T(8,128)(2,1)}), bf16[16,32,256]{2,1,0:T(8,128)(2,1)S(1)}, u32[]{:S(2)}, u32[]{:S(2)}) async-start(bf16[16,32,256]{2,1,0:T(8,128)(2,1)} %bitcast.100), calls=%async_computation.3 | async-start | bytes 524288 | tf_op jit(solution)/shard_map/all_to_all | solution.py:381
  258.6 3.3 %fusion.73 = f32[32,2,256]{2,1,0:T(2,128)S(1)} fusion(f32[32,2,4096]{2,1,0:T(2,128)} %param.18, s32[]{:T(128)S(6)} %select_n.491, s32[32,2,4096]{2,1,0:T(2,128)} %param.17, f32[32,2]{1,0:T(8,128)S(1)} %copy.119), kind=kLoop, calls=%fused_computation.163 | loop fusion | flops 1425408 | bytes 196868 | tf_op jit(solution)/shard_map/mul | solution.py:404
  262.7 10.0 %reduce-scatter.5.cloned.1.call-done = bf16[1,16,32,256]{3,2,1,0:T(8,128)(2,1)} async-done(((bf16[8,16,32,256]{3,2,1,0:T(8,128)(2,1)}), bf16[1,16,32,256]{3,2,1,0:T(8,128)(2,1)}) %reduce-scatter.5.cloned.1.call-update) | async-done | bytes 262160 | tf_op jit(solution)/shard_map/reduce_scatter | solution.py:380
  272.7 7.4 %all-to-all-start.4 = ((bf16[16,32,256]{2,1,0:T(8,128)(2,1)}), bf16[16,32,256]{2,1,0:T(8,128)(2,1)S(1)}, u32[]{:S(2)}, u32[]{:S(2)}) async-start(bf16[16,32,256]{2,1,0:T(8,128)(2,1)} %bitcast.101), calls=%async_computation.6 | async-start | bytes 524288 | tf_op jit(solution)/shard_map/all_to_all | solution.py:381
  280.1 1.0 fusion.30
  281.1 5.3 %all-to-all-done.4 = bf16[16,32,256]{2,1,0:T(8,128)(2,1)S(1)} async-done(((bf16[16,32,256]{2,1,0:T(8,128)(2,1)}), bf16[16,32,256]{2,1,0:T(8,128)(2,1)S(1)}, u32[]{:S(2)}, u32[]{:S(2)}) %all-to-all-start.4) | async-done | bytes 262176 | tf_op jit(solution)/shard_map/all_to_all | solution.py:381
  286.4 1.1 fusion.1
  (116 shorter events, 19.7 us)
Async XLA Ops:
  11.9 12.0 %copy-start.16 = (f32[4,3]{1,0:T(4,128)S(1)}, f32[4,3]{1,0:T(4,128)}, u32[]{:S(2)}) copy-start(f32[4,3]{1,0:T(4,128)} %param.13) | copy-start | bytes 148
  11.9 12.1 %copy-start.19 = (f32[3]{0:T(128)S(1)}, f32[3]{0:T(128)}, u32[]{:S(2)}) copy-start(f32[3]{0:T(128)} %constant.146) | copy-start | bytes 40
  11.9 15.9 %copy-start.12 = (s32[32,2]{0,1:T(2,128)S(1)}, s32[32,2]{0,1:T(2,128)}, u32[]{:S(2)}) copy-start(s32[32,2]{0,1:T(2,128)} %param.14) | copy-start | bytes 772
  11.9 137.4 %all-to-all-start = ((bf16[16,256,512]{2,1,0:T(8,128)(2,1)}), bf16[16,256,512]{2,1,0:T(8,128)(2,1)}, u32[]{:S(2)}, u32[]{:S(2)}) async-start(bf16[16,256,512]{2,1,0:T(8,128)(2,1)} %bitcast.96), calls=%async_computation | async-start | bytes 8388608 | tf_op jit(solution)/shard_map/all_to_all | solution.py:313
  155.5 23.6 %all-to-all-start.1 = ((bf16[16,2,32,512]{3,2,1,0:T(8,128)(2,1)}), bf16[16,2,32,512]{3,2,1,0:T(8,128)(2,1)S(1)}, u32[]{:S(2)}, u32[]{:S(2)}) async-start(bf16[16,2,32,512]{3,2,1,0:T(8,128)(2,1)} %row_warp.2), calls=%async_computation.1 | async-start | bytes 2097152 | tf_op jit(solution)/shard_map/all_to_all | solution.py:375
  163.2 89.6 %reduce-scatter.3.cloned.1.call-start = ((), (), s32[]{:S(2)}) async-start(), calls=%async_computation.7 | async-start | bytes 2359296 | tf_op jit(solution)/shard_map/reduce_scatter | solution.py:380
  164.9 0.5 copy-start.17
  166.4 1.7 copy-start.14
  166.4 1.7 copy-start.15
  179.1 1.2 copy-start
  180.3 0.6 copy-start.3
  180.9 0.7 copy-start.5
  199.4 0.8 copy-start.2
  199.5 0.8 copy-start.7
  199.5 0.8 copy-start.8
  199.5 73.2 %reduce-scatter.5.cloned.1.call-start = ((), (), s32[]{:S(2)}) async-start(), calls=%async_computation.8 | async-start | bytes 2359296 | tf_op jit(solution)/shard_map/reduce_scatter | solution.py:380
  205.4 18.2 %copy-start.1 = (f32[8,32,8,128]{3,2,1,0:T(8,128)S(1)}, f32[8,32,8,128]{3,2,1,0:T(8,128)}, u32[]{:S(2)}) copy-start(f32[8,32,8,128]{3,2,1,0:T(8,128)} %select_add_fusion.1.turned_ref) | copy-start | bytes 3145732
  205.4 18.2 %copy-start.4 = (s32[8]{0:T(128)S(1)}, s32[8]{0:T(128)}, u32[]{:S(2)}) copy-start(s32[8]{0:T(128)} %get-tuple-element.47.count_ref) | copy-start | bytes 100
  205.4 18.2 %copy-start.6 = (f32[8]{0:T(128)S(1)}, f32[8]{0:T(128)}, u32[]{:S(2)}) copy-start(f32[8]{0:T(128)} %reshape.616.weight_ref) | copy-start | bytes 100
  241.5 0.7 copy-start.13
  241.5 0.7 copy-start.18
  241.5 1.0 copy-start.10
  241.5 1.0 copy-start.11
  252.8 19.9 %all-to-all-start.2 = ((bf16[16,32,256]{2,1,0:T(8,128)(2,1)}), bf16[16,32,256]{2,1,0:T(8,128)(2,1)S(1)}, u32[]{:S(2)}, u32[]{:S(2)}) async-start(bf16[16,32,256]{2,1,0:T(8,128)(2,1)} %bitcast.100), calls=%async_computation.3 | async-start | bytes 524288 | tf_op jit(solution)/shard_map/all_to_all | solution.py:381
  272.7 13.7 %all-to-all-start.4 = ((bf16[16,32,256]{2,1,0:T(8,128)(2,1)}), bf16[16,32,256]{2,1,0:T(8,128)(2,1)S(1)}, u32[]{:S(2)}, u32[]{:S(2)}) async-start(bf16[16,32,256]{2,1,0:T(8,128)(2,1)} %bitcast.101), calls=%async_computation.6 | async-start | bytes 524288 | tf_op jit(solution)/shard_map/all_to_all | solution.py:381
  281.1 6.5 %copy-start.9 = (f32[1024,256,1]{1,0,2:T(8,128)}, f32[1024,256,1]{1,0,2:T(8,128)S(1)}, u32[]{:S(2)}) copy-start(f32[1024,256,1]{1,0,2:T(8,128)S(1)} %fusion.30) | copy-start | bytes 3145732
Sparse Core Ops, SparseCore 0:
  199.6 31.5 reduce-scatter.2
  241.7 30.9 reduce-scatter.4

commit v2 on v1

v2 whole, which is shorter than its diff:
```python
import functools
import math

import jax
import jax.numpy as jnp
from jax import lax
from jax.experimental import pallas as pl
from jax.experimental.pallas import tpu as pltpu
from jax.sharding import PartitionSpec as P

RADIUS = 10
TAPS = 6
SIGMAS = (1.0, 2.0, 4.0)
FLOOR_SHARE = 0.5
BF16 = jnp.bfloat16
F32 = jnp.float32

ROW_BLOCK = 128
ROW_STEP = 256
ROW_SPAN = 288
COL_BLOCK = 128
COL_STEP = 384
COL_GROUP = 4
BLUR_BLOCK = 256
BLUR_STEP = 512
BLUR_BAND = (112, 400)
LANES = 128
GROUPS = 1
LIMIT = 28 * 1024 * 1024


def psf_kernel(coefficient):
    offsets = jnp.arange(-RADIUS, RADIUS + 1).astype(coefficient.dtype)
    sigmas = jnp.array(SIGMAS, dtype=coefficient.dtype)
    gaussians = jnp.exp(
        -(offsets[None, :] * offsets[None, :]) / (2.0 * sigmas[:, None] * sigmas[:, None])
    )
    kernel = jnp.sum(coefficient[:, :, None] * gaussians[None, :, :], axis=1)
    return kernel / jnp.sum(kernel, axis=1, keepdims=True)


def lanczos_taps(f):
    g = 1.0 - f
    third = math.pi / 3.0
    tiny = 1e-6
    a = jnp.sin(third * f)
    b = jnp.sin(third * g)
    c = a + b
    fg = f * g
    a_over_f = jnp.where(f < tiny, third, a / jnp.maximum(f, tiny))
    b_over_g = jnp.where(g < tiny, third, b / jnp.maximum(g, tiny))
    values = [
        b * fg / ((f + 2.0) * (f + 2.0)),
        -c * fg / ((f + 1.0) * (f + 1.0)),
        a_over_f * g,
        b_over_g * f,
        -c * fg / ((2.0 - f) * (2.0 - f)),
        a * fg / ((3.0 - f) * (3.0 - f)),
    ]
    total = functools.reduce(jnp.add, values)
    return [lax.reduce_precision(value / total, 8, 7) for value in values]


def coverage(starts, taps, extent):
    running = jnp.zeros(starts.shape, F32)
    for tap_at, tap in enumerate(taps):
        position = starts + tap_at
        inside = (position >= 0) & (position < extent)
        running = running + jnp.where(inside, tap, 0.0)
    return running


def band_tables(starts, taps):
    place = jnp.arange(8, dtype=jnp.int32)[:, None]
    diff = place - starts[..., None, :]
    at = diff & 7
    turned = jnp.zeros(diff.shape, F32)
    for tap_at, tap in enumerate(taps):
        turned = turned + jnp.where(at == tap_at, tap[..., None, :], 0.0)
    return turned, diff - at


def toeplitz(kernel_ref, at, rows, cols, shift):
    diff = (
        lax.broadcasted_iota(jnp.int32, (rows, cols), 0)
        - lax.broadcasted_iota(jnp.int32, (rows, cols), 1)
    )
    full = jnp.zeros((rows, cols), F32)
    for tap_at in range(2 * RADIUS + 1):
        full = jnp.where(diff == tap_at - shift, kernel_ref[at, tap_at], full)
    return full


def dot(a, b):
    return jnp.dot(a, b, preferred_element_type=F32)


def two_parts(value):
    high = value.astype(BF16)
    return high, (value - high.astype(F32)).astype(BF16)


def halves_sum(value):
    half = value.shape[0] // 2
    return value[:half] + value[half:]


def band_of(turned, key, first, groups):
    moved = key + first
    return [jnp.where(moved == -8 * g, turned, 0.0) for g in range(groups)]


def row_matrix(blur_ref, turned, key, start, extent, masked):
    last = extent - ROW_STEP
    first = jnp.minimum(start, last)
    groups = ROW_SPAN // 8
    pieces = band_of(turned, key, first - 16, groups)
    for g in range(2):
        pieces[g] = jnp.where(first > 0, pieces[g], 0.0)
        pieces[groups - 1 - g] = jnp.where(first < last, pieces[groups - 1 - g], 0.0)
    band = jnp.concatenate(pieces, axis=0).astype(BF16)
    both = halves_sum(dot(blur_ref[...], band))
    if masked:
        row = lax.broadcasted_iota(jnp.int32, both.shape, 0) + first
        both = jnp.where(row >= start, both, 0.0)
    return jnp.concatenate(two_parts(both.T), axis=0)


def prepare_body(extent, own_ref, kernel_ref, low_ref, turned_ref, key_ref, rows_ref, blur_ref,
                 cols_ref, blur):
    step = pl.program_id(0)
    blocks = turned_ref.shape[1]
    high, rest = two_parts(
        toeplitz(kernel_ref, own_ref[step], ROW_STEP, ROW_SPAN, 16 + RADIUS)
    )
    blur[0:ROW_STEP] = high
    blur[ROW_STEP : 2 * ROW_STEP] = rest
    blur_ref[0] = blur[...]

    def block(at, carry):
        rows_ref[0, at] = row_matrix(
            blur, turned_ref[0, at], key_ref[0, at], low_ref[step, at], extent, False
        )
        return carry

    lax.fori_loop(0, blocks, block, 0)
    begin, end = BLUR_BAND
    for e in range(cols_ref.shape[0]):
        high, rest = two_parts(
            toeplitz(
                kernel_ref,
                step * cols_ref.shape[0] + e,
                end - begin,
                BLUR_BLOCK,
                begin - LANES + RADIUS,
            )
        )
        for n, part in enumerate((high, rest)):
            cols_ref[e, n, 0:begin] = jnp.zeros((begin, BLUR_BLOCK), BF16)
            cols_ref[e, n, begin:end] = part
            cols_ref[e, n, end:BLUR_STEP] = jnp.zeros((BLUR_STEP - end, BLUR_BLOCK), BF16)


def prepare(own, kernels, low, turned, key, extent):
    exposures = kernels.shape[0]
    blocks = turned.shape[1]
    smem = pl.BlockSpec(memory_space=pltpu.SMEM)
    table = pl.BlockSpec((1, blocks, 8, ROW_BLOCK), lambda g: (g, 0, 0, 0))
    return pl.pallas_call(
        functools.partial(prepare_body, extent),
        out_shape=(
            jax.ShapeDtypeStruct((GROUPS, blocks, 2 * ROW_BLOCK, ROW_STEP), BF16),
            jax.ShapeDtypeStruct((GROUPS, 2 * ROW_STEP, ROW_SPAN), BF16),
            jax.ShapeDtypeStruct((exposures, 2, BLUR_STEP, BLUR_BLOCK), BF16),
        ),
        grid=(GROUPS,),
        in_specs=[smem, smem, smem, table, table],
        out_specs=(
            pl.BlockSpec((1, blocks, 2 * ROW_BLOCK, ROW_STEP), lambda g: (g, 0, 0, 0)),
            pl.BlockSpec((1, 2 * ROW_STEP, ROW_SPAN), lambda g: (g, 0, 0)),
            pl.BlockSpec((exposures // GROUPS, 2, BLUR_STEP, BLUR_BLOCK), lambda g: (g, 0, 0, 0)),
        ),
        scratch_shapes=[pltpu.VMEM((2 * ROW_STEP, ROW_SPAN), BF16)],
        compiler_params=pltpu.CompilerParams(
            dimension_semantics=("arbitrary",), vmem_limit_bytes=LIMIT
        ),
        cost_estimate=pl.CostEstimate(
            flops=4_000_000_000, bytes_accessed=8 * 1024 * 1024, transcendentals=0
        ),
        name="prepare",
    )(own, kernels, low, turned, key)


def row_body(slots, low_ref, num_ref, x_ref, rows_ref, blur_ref, turned_ref, key_ref, out_ref):
    extent = x_ref.shape[0]
    owner_rows = out_ref.shape[2]
    blocks = turned_ref.shape[1] // slots

    def times(matrix, start):
        first = pl.multiple_of(jnp.minimum(start, extent - ROW_STEP), 16)
        return halves_sum(dot(matrix, x_ref[pl.ds(first, ROW_STEP), :]))

    def block(at, carry):
        indices = [slot * blocks + at for slot in range(slots)]
        sums = [times(rows_ref[0, index], low_ref[index]) for index in indices]
        for slot, index in enumerate(indices):

            def more(i, total, index=index):
                start = low_ref[index] + i * ROW_STEP
                matrix = row_matrix(
                    blur_ref.at[0], turned_ref[0, index], key_ref[0, index], start, extent, True
                )
                return total + times(matrix, start)

            total = lax.fori_loop(1, num_ref[index], more, sums[slot]).astype(BF16)
            for owner in range(ROW_BLOCK // owner_rows):
                out_ref[at * (ROW_BLOCK // owner_rows) + owner, slot] = total[
                    owner * owner_rows : (owner + 1) * owner_rows
                ]
        return carry

    lax.fori_loop(0, blocks, block, 0)


def row_warp(g, x, low, num, matrices, blur, turned, key, slots, owners):
    width = x.shape[1]
    blocks = turned.shape[1]
    owner_rows = blocks // slots * ROW_BLOCK // owners
    vmem = pl.BlockSpec(memory_space=pltpu.VMEM)
    smem = pl.BlockSpec(memory_space=pltpu.SMEM)

    def own(array):
        shape = (1,) + array.shape[1:]
        return pl.BlockSpec(shape, lambda i: (g,) + (0,) * (len(shape) - 1))

    return pl.pallas_call(
        functools.partial(row_body, slots),
        out_shape=jax.ShapeDtypeStruct((owners, slots, owner_rows, width), BF16),
        grid=(1,),
        in_specs=[smem, smem, vmem, own(matrices), own(blur), own(turned), own(key)],
        out_specs=vmem,
        compiler_params=pltpu.CompilerParams(
            dimension_semantics=("arbitrary",), vmem_limit_bytes=LIMIT
        ),
        cost_estimate=pl.CostEstimate(
            flops=2_000_000_000, bytes_accessed=8 * 1024 * 1024, transcendentals=0
        ),
        name="row_warp",
    )(low, num, x, matrices, blur, turned, key)


def col_body(g, cols, slots, has_prior, count_ref, list_ref, low_ref, most_ref, from_ref, to_ref,
             weight_ref, z_ref, blur_ref, turned_ref, key_ref, *refs):
    if has_prior:
        prior_ref, out_ref, padded, blurred, held = refs
    else:
        out_ref, padded, blurred, held = refs
    rows = z_ref.shape[2]
    width = z_ref.shape[3]
    sources = cols // width
    exposures = z_ref.shape[0] // sources
    base = g * exposures * slots
    patch = pl.program_id(0)

    @pl.when(patch == 0)
    def _():
        pad = jnp.zeros((slots * rows, LANES), BF16)
        padded[:, 0:LANES] = pad
        padded[:, LANES + cols : 2 * LANES + cols] = pad
        for e in range(exposures):
            for s in range(sources):
                padded[:, LANES + s * width : LANES + (s + 1) * width] = z_ref[
                    e * sources + s
                ].reshape(slots * rows, width)
            windows = jnp.concatenate(
                [
                    padded[:, b * BLUR_BLOCK : b * BLUR_BLOCK + BLUR_STEP]
                    for b in range(cols // BLUR_BLOCK)
                ],
                axis=0,
            )
            high, rest = two_parts(dot(windows, blur_ref[e, 0]) + dot(windows, blur_ref[e, 1]))
            for b in range(cols // BLUR_BLOCK):
                for j in range(slots):
                    at = (b * slots + j) * rows
                    span = slice(b * BLUR_BLOCK, (b + 1) * BLUR_BLOCK)
                    blurred[e * slots + j, 0:rows, span] = high[at : at + rows]
                    blurred[e * slots + j, rows : 2 * rows, span] = rest[at : at + rows]
            for j in range(slots):
                blurred[e * slots + j, :, cols : cols + COL_STEP] = jnp.zeros(
                    (2 * rows, COL_STEP), BF16
                )

    held[...] = prior_ref[0] if has_prior else jnp.zeros(held.shape, F32)

    def part(slot, b, n):
        first = pl.multiple_of(
            jnp.minimum(low_ref[base + slot, b] + n * COL_STEP, cols), LANES
        )
        band = band_of(turned_ref[slot, b], key_ref[slot, b], first, COL_STEP // 8)
        band = jnp.concatenate(band, axis=0).astype(BF16)
        return halves_sum(dot(blurred[slot, :, pl.ds(first, COL_STEP)], band))

    per_owner = held.shape[2] // COL_BLOCK

    def add_slot(i, carry):
        slot = list_ref[patch, i]
        weight = weight_ref[base + slot]

        def add_group(c, carry):
            def add_parts(n):
                for h in range(COL_GROUP):
                    owner = c * (COL_GROUP // per_owner) + h // per_owner
                    span = slice((h % per_owner) * COL_BLOCK, (h % per_owner + 1) * COL_BLOCK)
                    held[owner, :, span] += weight * part(slot, c * COL_GROUP + h, n)

            add_parts(0)

            def more(n, carry):
                add_parts(n)
                return carry

            lax.fori_loop(1, most_ref[base + slot, c], more, 0)
            return carry

        return lax.fori_loop(from_ref[base + slot], to_ref[base + slot], add_group, carry)

    lax.fori_loop(0, count_ref[patch], add_slot, 0)
    out_ref[0] = held[...].astype(out_ref.dtype)


def col_warp(g, z, count, listed, low, most, begin, end, weight, blur, turned, key, cols, patches,
             prior, out_type):
    owners, slots, rows = z.shape[:3]
    exposures = z.shape[0] * z.shape[3] // cols
    group_slots = exposures * slots
    blocks = turned.shape[1]
    own_cols = blocks * COL_BLOCK // owners
    vmem = pl.BlockSpec(memory_space=pltpu.VMEM)
    smem = pl.BlockSpec(memory_space=pltpu.SMEM)
    table = pl.BlockSpec((group_slots, blocks, 8, COL_BLOCK), lambda k: (g, 0, 0, 0))
    block = pl.BlockSpec((1, owners, rows, own_cols), lambda k: (k, 0, 0, 0))
    return pl.pallas_call(
        functools.partial(col_body, g, cols, slots, prior is not None),
        out_shape=jax.ShapeDtypeStruct((patches, owners, rows, own_cols), out_type),
        grid=(patches,),
        in_specs=[smem] * 7
        + [
            vmem,
            pl.BlockSpec((exposures, 2, BLUR_STEP, BLUR_BLOCK), lambda k: (g, 0, 0, 0)),
            table,
            table,
        ]
        + ([] if prior is None else [block]),
        out_specs=block,
        scratch_shapes=[
            pltpu.VMEM((slots * rows, cols + 2 * LANES), BF16),
            pltpu.VMEM((group_slots, 2 * rows, cols + COL_STEP), BF16),
            pltpu.VMEM((owners, rows, own_cols), F32),
        ],
        compiler_params=pltpu.CompilerParams(
            dimension_semantics=("arbitrary",), vmem_limit_bytes=LIMIT
        ),
        cost_estimate=pl.CostEstimate(
            flops=4_000_000_000, bytes_accessed=16 * 1024 * 1024, transcendentals=0
        ),
        name="col_warp",
    )(
        count, listed, low, most, begin, end, weight, z, blur, turned, key,
        *(() if prior is None else (prior,)),
    )


def split_body(parts, image_ref, out_ref, sems):
    exposures, _, width = image_ref.shape
    part = width // parts
    copies = []
    for e in range(exposures):
        for s in range(parts):
            at = e * parts + s
            copies.append(
                pltpu.make_async_copy(
                    image_ref.at[e, :, pl.ds(s * part, part)], out_ref.at[at], sems.at[at]
                )
            )
    for copy in copies:
        copy.start()
    for copy in copies:
        copy.wait()


def split_columns(image, parts):
    exposures, height, width = image.shape
    total = exposures * parts
    return pl.pallas_call(
        functools.partial(split_body, parts),
        out_shape=jax.ShapeDtypeStruct((total, height, width // parts), image.dtype),
        in_specs=[pl.BlockSpec(memory_space=pl.ANY)],
        out_specs=pl.BlockSpec(memory_space=pl.ANY),
        scratch_shapes=[pltpu.SemaphoreType.DMA((total,))],
        name="split_columns",
    )(image)


def butterfly_sum(x, axis):
    size = lax.axis_size(axis)
    step = 1
    while step < size:
        x = x + lax.ppermute(x, axis, [(i, i ^ step) for i in range(size)])
        step *= 2
    return x


def local(image, variance, psf_coef, correlations, row_start, row_frac, col_start, col_frac):
    exp_dev, height, width = image.shape
    exposures, slots = correlations.shape
    patch_rows = row_start.shape[2]
    patch_cols = col_start.shape[2]
    visits = lax.axis_size("visit")
    regions = lax.axis_size("region")
    extent = height * regions
    group_exp = exp_dev // GROUPS
    parts = regions // group_exp
    part_cols = width // parts
    own_cols = patch_cols // regions
    visit_at = lax.axis_index("visit")
    region_at = lax.axis_index("region")
    first_exp = visit_at * exp_dev

    def exchange(x, axis):
        return lax.all_to_all(x, axis, split_axis=0, concat_axis=0, tiled=True)

    columns = []
    for g in range(GROUPS):
        sent = split_columns(image[g * group_exp : (g + 1) * group_exp], parts)
        columns.append(exchange(sent, "region").reshape(extent, part_cols))

    local_sums = jnp.sum(variance.astype(F32), axis=(1, 2))
    tile = jnp.zeros((8, LANES), F32).at[0, :exp_dev].set(local_sums)
    tile = butterfly_sum(tile, "region")
    slot_weight = jnp.repeat(1.0 / (tile[0, :exp_dev] / (extent * width)), slots)

    kernels = psf_kernel(psf_coef)

    own_exp = jnp.arange(GROUPS, dtype=jnp.int32) * group_exp + region_at // parts
    starts = jnp.stack(
        [
            lax.dynamic_index_in_dim(row_start, first_exp + own_exp[g], 0, keepdims=False)
            for g in range(GROUPS)
        ]
    )
    fracs = jnp.stack(
        [
            lax.dynamic_index_in_dim(row_frac, first_exp + own_exp[g], 0, keepdims=False)
            for g in range(GROUPS)
        ]
    )
    blocks = slots * patch_rows // ROW_BLOCK
    starts = starts.reshape(GROUPS, blocks, ROW_BLOCK)
    fracs = fracs.reshape(GROUPS, blocks, ROW_BLOCK)
    row_turned, row_key = band_tables(starts, lanczos_taps(fracs))
    row_low = jnp.clip(starts[..., 0] - RADIUS, 0, extent - ROW_STEP) // 16 * 16
    row_end = jnp.minimum(starts[..., -1] + TAPS + RADIUS, extent)
    row_num = jnp.maximum(row_end - row_low + ROW_STEP - 1, 0) // ROW_STEP
    row_matrices, row_blur, col_blur = prepare(
        own_exp, kernels, row_low, row_turned, row_key, extent
    )

    slot_total = exp_dev * slots
    group_slots = group_exp * slots
    col_blocks = patch_cols // COL_BLOCK
    own_starts = lax.dynamic_slice_in_dim(col_start, first_exp, exp_dev, 0)
    own_fracs = lax.dynamic_slice_in_dim(col_frac, first_exp, exp_dev, 0)
    own_starts = own_starts.reshape(slot_total, col_blocks, COL_BLOCK)
    own_fracs = own_fracs.reshape(slot_total, col_blocks, COL_BLOCK)
    col_turned, col_key = band_tables(own_starts, lanczos_taps(own_fracs))
    col_low = jnp.clip(own_starts[:, :, 0], 0, width) // LANES * LANES
    col_end = jnp.minimum(own_starts[:, :, -1] + TAPS, width)
    col_num = jnp.maximum(col_end - col_low + COL_STEP - 1, 0) // COL_STEP
    col_most = jnp.max(col_num.reshape(slot_total, col_blocks // COL_GROUP, COL_GROUP), axis=2)
    group_at = jnp.arange(col_blocks // COL_GROUP, dtype=jnp.int32)
    col_from = jnp.min(jnp.where(col_most > 0, group_at, col_blocks // COL_GROUP), axis=1)
    col_to = jnp.max(jnp.where(col_most > 0, group_at + 1, 0), axis=1)
    owners = lax.dynamic_slice_in_dim(correlations, first_exp, exp_dev, 0)
    owners = owners.reshape(GROUPS, group_slots)
    named = owners[:, None, :] == jnp.arange(visits, dtype=jnp.int32)[:, None]
    named = named.astype(jnp.int32)
    count = jnp.sum(named, axis=2)
    slot_ids = jnp.arange(group_slots, dtype=jnp.int32)
    rank = jnp.sum(
        jnp.where(slot_ids[:, None] < slot_ids, named[..., :, None], 0), axis=2
    )
    listed = jnp.sum(
        jnp.where(
            (named[..., None, :] > 0) & (rank[..., None, :] == slot_ids[:, None]), slot_ids, 0
        ),
        axis=3,
    )

    rows = []
    for g in range(GROUPS):
        warped = row_warp(
            g, columns[g], row_low[g], row_num[g], row_matrices, row_blur, row_turned, row_key,
            slots, regions,
        )
        if g == GROUPS - 1:
            tile, warped = lax.optimization_barrier((tile, warped))
        rows.append(exchange(warped, "region"))
    tiles = jnp.zeros((visits, 8, LANES), F32)
    tiles = lax.dynamic_update_slice(tiles, tile[None], (visit_at, 0, 0))[:, 0]
    tiles = butterfly_sum(tiles, "visit")
    weight = 1.0 / (tiles[:, :exp_dev].reshape(exposures) / (extent * width))
    mean_weight = jnp.mean(weight)
    partial = None
    for g in range(GROUPS):
        partial = col_warp(
            g, rows[g], count[g], listed[g], col_low, col_most, col_from, col_to, slot_weight,
            col_blur, col_turned, col_key, width, visits, partial,
            BF16 if g == GROUPS - 1 else F32,
        )
    summed = lax.psum_scatter(partial, "visit", scatter_dimension=0, tiled=True)
    summed = exchange(summed[0], "region").reshape(1, patch_rows, own_cols).astype(F32)

    total_slots = exposures * slots
    row_cover = coverage(
        row_start.reshape(total_slots, patch_rows),
        lanczos_taps(row_frac.reshape(total_slots, patch_rows)),
        extent,
    )
    at = region_at * own_cols
    col_cover = coverage(
        lax.dynamic_slice_in_dim(col_start, at, own_cols, 2).reshape(total_slots, own_cols),
        lanczos_taps(
            lax.dynamic_slice_in_dim(col_frac, at, own_cols, 2).reshape(total_slots, own_cols)
        ),
        width,
    )
    scale = jnp.where(
        correlations.reshape(total_slots) == visit_at, jnp.repeat(weight, slots), 0.0
    )
    weight_map = lax.dot_general(
        row_cover,
        col_cover * scale[:, None],
        (((0,), (0,)), ((), ())),
        precision=lax.Precision.HIGHEST,
        preferred_element_type=F32,
    ).reshape(1, patch_rows, own_cols)
    coadd = summed / jnp.maximum(weight_map, FLOOR_SHARE * mean_weight)
    return coadd, weight_map


def solution(mesh):
    placed = (
        P("visit", "region", None),
        P("visit", "region", None),
        P("visit", None),
        P(),
        P(),
        P(),
        P(),
        P(),
    )
    return jax.shard_map(
        local,
        mesh=mesh,
        in_specs=placed,
        out_specs=(P("visit", None, "region"), P("visit", None, "region")),
        check_vma=False,
    )
```

time: 295 us -> 335 us (1.14)
  Pallas kernels: 47 us -> 158 us
  blocking collectives: 110 us -> 0 us
  waiting for transfers between devices: 22.6 us -> 75.1 us
  other arithmetic: 50.9 us -> 23.5 us
  starting transfers between devices: 29.6 us -> 48.7 us
  local copies, waits for them, and re-layouts: 17.7 us -> 11.3 us
    pallas_call x2 -> x3, Pallas kernels: 35.7 us -> 151 us  [the longest x1 128 us: split_columns(): pl.pallas_call(functools.partial(split_body, parts), out_shape=jax.ShapeD...]
    all_gather x1 -> x0, blocking collectives: 92.2 us -> none  [local(): gathered = lax.all_gather(tile, ('visit', 'region'), axis=0, tiled=False)]
    ppermute x0 -> x7, waiting for transfers between devices: none -> 35.1 us  [butterfly_sum(): x = x + lax.ppermute(x, axis, [(i, i ^ step) for i in range(size)])]
    ppermute x0 -> x7, starting transfers between devices: none -> 28.6 us  [butterfly_sum(): x = x + lax.ppermute(x, axis, [(i, i ^ step) for i in range(size)])]
    all_to_all x1 -> x0, blocking collectives: 18.2 us -> none  [local(): lax.all_to_all(row_warped, 'region', split_axis=0, concat_axis=0, tiled=T...]
    add x2 -> x7, other arithmetic: 17 us -> 0.02 us  [the longest x6 0.02 us: butterfly_sum(): x = x + lax.ppermute(x, axis, [(i, i ^ step) for i in range(size)])]
    all_to_all x4 -> x3, starting transfers between devices: 29.4 us -> 20.1 us  [exchange(): return lax.all_to_all(x, axis, split_axis=0, concat_axis=0, tiled=True)]
    reduce_scatter x2 -> x1, waiting for transfers between devices: 10 us -> 19.2 us  [local(): summed = lax.psum_scatter(partial, 'visit', scatter_dimension=0, tiled=True)]
  transfers between devices with their start and end apart: 6 -> 11, of which waited for: 3 -> 8; matrix products, arithmetic and copies ran while one was open for 20% -> 8% of each run, Pallas kernels for 8% -> 41%
where the time goes in v2:
time: 335 us; the launch traced here: 332 us
  Pallas kernels  158 us (47%)
  waiting for transfers between devices  75.1 us (22%)
  starting transfers between devices  48.7 us (15%)
  other arithmetic  23.5 us (7%)
  between operations  15 us (4%)
  local copies, waits for them, and re-layouts  11.3 us (3%)
    pallas_call x1, Pallas kernels, split_columns(): pl.pallas_call(functools.partial(split_body, parts), out_shape=jax.ShapeD...  128 us
    ppermute x7, waiting for transfers between devices, butterfly_sum(): x = x + lax.ppermute(x, axis, [(i, i ^ step) for i in range(size)])  35.1 us
    ppermute x7, starting transfers between devices, butterfly_sum(): x = x + lax.ppermute(x, axis, [(i, i ^ step) for i in range(size)])  28.6 us
    all_to_all x3, waiting for transfers between devices, exchange(): return lax.all_to_all(x, axis, split_axis=0, concat_axis=0, tiled=True)  20.8 us
    all_to_all x3, starting transfers between devices, exchange(): return lax.all_to_all(x, axis, split_axis=0, concat_axis=0, tiled=True)  20.1 us
    reduce_scatter x1, waiting for transfers between devices, local(): summed = lax.psum_scatter(partial, 'visit', scatter_dimension=0, tiled=True)  19.2 us
    pallas_call x1, Pallas kernels, col_warp(): pl.pallas_call(functools.partial(col_body, g, cols, slots, prior is not N...  15.5 us
    add x1, other arithmetic, coverage(): running = running + jnp.where(inside, tap, 0.0)  10.2 us
  transfers between devices with their start and end apart: 11, of which 8 were waited for; matrix products, arithmetic and copies ran while one was open for 8% of the time, Pallas kernels for 41%

profile of v2, /device:TPU:4, one launch (start us, length us, event | category | flops | bytes accessed | tf_op | source)
XLA Modules:
  0.0 332.2 jit_solution(14424966364699244218)
XLA Ops:
  7.2 2.9 convert_reduce_fusion
  10.1 2.0 collective-permute-start
  12.0 128.3 %split_columns.1 = bf16[16,256,512]{2,1,0:T(8,128)(2,1)} custom-call(bf16[4,256,2048]{2,1,0:T(8,128)(2,1)} %image_ref.1), custom_call_target="tpu_custom_call" | custom-call | tf_op jit(solution)/shard_map/split_columns/pallas_call | solution.py:395
  140.4 8.0 %all-to-all-start = ((bf16[16,256,512]{2,1,0:T(8,128)(2,1)}), bf16[16,256,512]{2,1,0:T(8,128)(2,1)}, u32[]{:S(2)}, u32[]{:S(2)}) async-start(bf16[16,256,512]{2,1,0:T(8,128)(2,1)} %split_columns.1), calls=%async_computation | async-start | bytes 8388608 | tf_op jit(solution)/shard_map/all_to_all | solution.py:431
  152.4 7.5 %prepare.1 = (bf16[1,16,256,256]{3,2,1,0:T(8,128)(2,1)S(1)}, bf16[1,512,288]{2,1,0:T(8,128)(2,1)S(1)}, bf16[4,2,512,256]{3,2,1,0:T(8,128)(2,1)S(1)}) custom-call(s32[1]{0:T(128)} %bitcast.6.own_ref, f32[4,21]{1,0:T(4,128)S(1)} %broadcast_divide_fusion.kernel_ref, s32[1,16]{1,0:T(1,128)S(1)} %fusion.55.low_ref, ...), custom_call_target="tpu_custom_call" | custom-call | flops 4000000000 | bytes 8388608 | tf_op jit(solution)/shard_map/prepare/pallas_call | solution.py:169
  159.9 1.4 copy-done.2
  162.5 3.0 collective-permute-start.1
  165.7 16.3 %collective-permute-done.1 = f32[8,128]{1,0:T(8,128)S(1)} collective-permute-done((f32[8,128]{1,0:T(8,128)S(1)}, f32[8,128]{1,0:T(8,128)S(1)}, u32[]{:S(2)}, u32[]{:S(2)}) %collective-permute-start.1) | collective-permute-done | bytes 4128 | tf_op jit(solution)/shard_map/ppermute | solution.py:409
  182.0 18.9 %collective-permute-start.2 = (f32[8,128]{1,0:T(8,128)S(1)}, f32[8,128]{1,0:T(8,128)S(1)}, u32[]{:S(2)}, u32[]{:S(2)}) collective-permute-start(f32[8,128]{1,0:T(8,128)S(1)} %add.810), channel_id=1, source_target_pairs={{0,4},{1,5},{2,6},{3,7},{4,0},{5,1},{6,2},{7,3},{8,12},{9,13},{10,... | collective-permute-start | bytes 12296 | tf_op jit(solution)/shard_map/ppermute | solution.py:409
  201.0 10.5 %collective-permute-done.2 = f32[8,128]{1,0:T(8,128)S(1)} collective-permute-done((f32[8,128]{1,0:T(8,128)S(1)}, f32[8,128]{1,0:T(8,128)S(1)}, u32[]{:S(2)}, u32[]{:S(2)}) %collective-permute-start.2) | collective-permute-done | bytes 4128 | tf_op jit(solution)/shard_map/ppermute | solution.py:409
  211.5 5.1 %collective-permute-done.3 = f32[8,128]{1,0:T(8,128)S(1)} collective-permute-done((f32[8,128]{1,0:T(8,128)S(1)}, f32[8,128]{1,0:T(8,128)S(1)}, u32[]{:S(2)}, u32[]{:S(2)}) %collective-permute-start.3) | collective-permute-done | bytes 4128 | tf_op jit(solution)/shard_map/ppermute | solution.py:409
  216.6 6.2 %row_warp.1 = bf16[16,2,64,512]{3,2,1,0:T(8,128)(2,1)} custom-call(s32[16]{0:T(128)S(1)} %get-tuple-element.37.low_ref, s32[16]{0:T(128)S(1)} %get-tuple-element.36.num_ref, bf16[4096,512]{1,0:T(8,128)(2,1)} %bitcast.5.x_ref, bf16[1,16,256,256]{3,2,1,0:T(8,128)(2,1)S(1)} %get-tuple-element.19.rows_ref, bf16[1,512,288]{2,1,0:T(8,128)(2,1)S(1)} %get-tuple-element.20.blur_ref, ...), custom_call_target="tpu_custom_call" | custom-call | flops 2000000000 | bytes 8388608 | tf_op jit(solution)/shard_map/row_warp/pallas_call | solution.py:236
  222.8 4.8 %all-to-all-start.1 = ((bf16[16,2,64,512]{3,2,1,0:T(8,128)(2,1)}), bf16[16,2,64,512]{3,2,1,0:T(8,128)(2,1)S(1)}, u32[]{:S(2)}, u32[]{:S(2)}) async-start(bf16[16,2,64,512]{3,2,1,0:T(8,128)(2,1)} %row_warp.1), calls=%async_computation.1 | async-start | bytes 4194304 | tf_op jit(solution)/shard_map/all_to_all | solution.py:431
  228.5 1.0 divide_reduce-precision_fusion.5
  229.6 1.0 divide_reduce-precision_fusion.4
  230.7 1.7 select_add_fusion.turned_ref
  232.6 18.2 %all-to-all-done.1.z_ref = bf16[16,2,64,512]{3,2,1,0:T(8,128)(2,1)S(1)} async-done(((bf16[16,2,64,512]{3,2,1,0:T(8,128)(2,1)}), bf16[16,2,64,512]{3,2,1,0:T(8,128)(2,1)S(1)}, u32[]{:S(2)}, u32[]{:S(2)}) %all-to-all-start.1) | async-done | bytes 2097184 | tf_op jit(solution)/shard_map/all_to_all | solution.py:431
  250.8 1.2 copy-done.1
  252.0 1.6 copy-done.3
  253.6 15.5 %col_warp.1 = bf16[8,16,64,256]{3,2,1,0:T(8,128)(2,1)S(1)} custom-call(s32[8]{0:T(128)S(1)} %convert_reduce_fusion.1.count_ref, s32[8,8]{1,0:T(8,128)S(1)} %select_reduce_fusion.list_ref, s32[8,32]{1,0:T(8,128)S(1)} %fusion.51.low_ref, s32[8,8]{1,0:T(8,128)S(1)} %copy.55.most_ref, s32[8]{0:T(128)S(1)} %get-tuple-element.29.from_ref, ...), custom_call_target="tpu_custom_call" | custom-call | flops 4000000000 | bytes 16777216 | tf_op jit(solution)/shard_map/col_warp/pallas_call | solution.py:343
  269.1 1.9 copy-done
  271.4 1.2 collective-permute-done.4
  272.5 1.6 collective-permute-start.5
  274.1 2.0 collective-permute-done.5
  276.2 2.9 collective-permute-start.6
  279.1 10.2 %fusion.7 = f32[32,2,1024]{2,1,0:T(2,128)S(1)} fusion(s32[32,2,1024]{2,1,0:T(2,128)S(1)} %copy-done.5, f32[32,2,1024]{2,1,0:T(2,128)S(1)} %copy-done.6), kind=kLoop, calls=%fused_computation.27 | loop fusion | flops 5636096 | bytes 786432 | tf_op jit(solution)/shard_map/add | solution.py:69
  290.1 19.2 %reduce-scatter.2.cloned.1.call-done = bf16[1,16,64,256]{3,2,1,0:T(8,128)(2,1)} async-done(((bf16[8,16,64,256]{3,2,1,0:T(8,128)(2,1)}), bf16[1,16,64,256]{3,2,1,0:T(8,128)(2,1)}) %reduce-scatter.2.cloned.1.call-update) | async-done | bytes 524304 | tf_op jit(solution)/shard_map/reduce_scatter | solution.py:521
  309.3 7.2 %all-to-all-start.2 = ((bf16[16,64,256]{2,1,0:T(8,128)(2,1)}), bf16[16,64,256]{2,1,0:T(8,128)(2,1)S(1)}, u32[]{:S(2)}, u32[]{:S(2)}) async-start(bf16[16,64,256]{2,1,0:T(8,128)(2,1)} %bitcast.53), calls=%async_computation.3 | async-start | bytes 1048576 | tf_op jit(solution)/shard_map/all_to_all | solution.py:431
  316.5 3.3 %fusion.30 = f32[32,2,256]{2,1,0:T(2,128)S(1)} fusion(f32[32,2,4096]{2,1,0:T(2,128)} %param.18, s32[]{:T(128)S(6)} %select_n.401, s32[32,2,4096]{2,1,0:T(2,128)} %param.17, f32[32,2]{1,0:T(8,128)S(1)} %copy.57), kind=kLoop, calls=%fused_computation.115 | loop fusion | flops 1425408 | bytes 196868 | tf_op jit(solution)/shard_map/mul | solution.py:543
  320.5 1.0 fusion.8
  321.6 2.7 all-to-all-done.2
  324.2 1.1 fusion
  (86 shorter events, 7.7 us)
Async XLA Ops:
  10.1 152.3 %collective-permute-start = (f32[8,128]{1,0:T(8,128)S(1)}, f32[8,128]{1,0:T(8,128)S(1)}, u32[]{:S(2)}, u32[]{:S(2)}) collective-permute-start(f32[8,128]{1,0:T(8,128)S(1)} %scatter.7), channel_id=1, source_target_pairs={{0,1},{1,0},{2,3},{3,2},{4,5},{5,4},{6,7},{7,6},{8,9},{9,8},{10,11... | collective-permute-start | bytes 12296 | tf_op jit(solution)/shard_map/ppermute | solution.py:409
  140.3 8.9 %copy-start.8 = (f32[4,3]{1,0:T(4,128)S(1)}, f32[4,3]{1,0:T(4,128)}, u32[]{:S(2)}) copy-start(f32[4,3]{1,0:T(4,128)} %param.13) | copy-start | bytes 148
  140.3 9.7 %copy-start.7 = (s32[32,2]{0,1:T(2,128)S(1)}, s32[32,2]{0,1:T(2,128)}, u32[]{:S(2)}) copy-start(s32[32,2]{0,1:T(2,128)} %param.14) | copy-start | bytes 772
  140.4 11.4 %copy-start.9 = (f32[3]{0:T(128)S(1)}, f32[3]{0:T(128)}, u32[]{:S(2)}) copy-start(f32[3]{0:T(128)} %constant.228) | copy-start | bytes 40
  140.4 76.2 %all-to-all-start = ((bf16[16,256,512]{2,1,0:T(8,128)(2,1)}), bf16[16,256,512]{2,1,0:T(8,128)(2,1)}, u32[]{:S(2)}, u32[]{:S(2)}) async-start(bf16[16,256,512]{2,1,0:T(8,128)(2,1)} %split_columns.1), calls=%async_computation | async-start | bytes 8388608 | tf_op jit(solution)/shard_map/all_to_all | solution.py:431
  159.9 1.4 copy-start.2
  162.5 19.5 %collective-permute-start.1 = (f32[8,128]{1,0:T(8,128)S(1)}, f32[8,128]{1,0:T(8,128)S(1)}, u32[]{:S(2)}, u32[]{:S(2)}) collective-permute-start(f32[8,128]{1,0:T(8,128)S(1)} %add.809), channel_id=1, source_target_pairs={{0,2},{1,3},{2,0},{3,1},{4,6},{5,7},{6,4},{7,5},{8,10},{9,11},{10,... | collective-permute-start | bytes 12296 | tf_op jit(solution)/shard_map/ppermute | solution.py:409
  182.0 29.4 %collective-permute-start.2 = (f32[8,128]{1,0:T(8,128)S(1)}, f32[8,128]{1,0:T(8,128)S(1)}, u32[]{:S(2)}, u32[]{:S(2)}) collective-permute-start(f32[8,128]{1,0:T(8,128)S(1)} %add.810), channel_id=1, source_target_pairs={{0,4},{1,5},{2,6},{3,7},{4,0},{5,1},{6,2},{7,3},{8,12},{9,13},{10,... | collective-permute-start | bytes 12296 | tf_op jit(solution)/shard_map/ppermute | solution.py:409
  211.4 5.1 %collective-permute-start.3 = (f32[8,128]{1,0:T(8,128)S(1)}, f32[8,128]{1,0:T(8,128)S(1)}, u32[]{:S(2)}, u32[]{:S(2)}) collective-permute-start(f32[8,128]{1,0:T(8,128)S(1)} %add.811), channel_id=1, source_target_pairs={{0,8},{1,9},{2,10},{3,11},{4,12},{5,13},{6,14},{7,15},{8,0},{9,1},... | collective-permute-start | bytes 12296 | tf_op jit(solution)/shard_map/ppermute | solution.py:409
  222.8 28.0 %all-to-all-start.1 = ((bf16[16,2,64,512]{3,2,1,0:T(8,128)(2,1)}), bf16[16,2,64,512]{3,2,1,0:T(8,128)(2,1)S(1)}, u32[]{:S(2)}, u32[]{:S(2)}) async-start(bf16[16,2,64,512]{3,2,1,0:T(8,128)(2,1)} %row_warp.1), calls=%async_computation.1 | async-start | bytes 4194304 | tf_op jit(solution)/shard_map/all_to_all | solution.py:431
  227.6 81.6 %reduce-scatter.2.cloned.1.call-start = ((), (), s32[]{:S(2)}) async-start(), calls=%async_computation.4 | async-start | bytes 4718592 | tf_op jit(solution)/shard_map/reduce_scatter | solution.py:521
  250.7 1.2 copy-start.1
  252.0 1.6 copy-start.3
  269.1 1.9 copy-start
  271.0 8.1 %copy-start.5 = (s32[32,2,1024]{2,1,0:T(2,128)S(1)}, s32[32,2,1024]{2,1,0:T(2,128)}, u32[]{:S(2)}) copy-start(s32[32,2,1024]{2,1,0:T(2,128)} %param.15) | copy-start | bytes 786436
  271.0 8.1 %copy-start.6 = (f32[32,2,1024]{2,1,0:T(2,128)S(1)}, f32[32,2,1024]{2,1,0:T(2,128)}, u32[]{:S(2)}) copy-start(f32[32,2,1024]{2,1,0:T(2,128)} %param.16) | copy-start | bytes 786436
  271.1 1.4 collective-permute-start.4
  272.5 3.6 %collective-permute-start.5 = (f32[8,128]{1,0:T(8,128)S(1)}, f32[8,128]{1,0:T(8,128)S(1)}, u32[]{:S(2)}, u32[]{:S(2)}) collective-permute-start(f32[8,128]{1,0:T(8,128)S(1)} %fusion.57), channel_id=1, source_target_pairs={{0,32},{16,48},{32,0},{48,16},{64,96},{80,112},{96,64},{112,80},{1... | collective-permute-start | bytes 12296 | tf_op jit(solution)/shard_map/ppermute | solution.py:409
  276.2 13.1 %collective-permute-start.6 = (f32[8,128]{1,0:T(8,128)S(1)}, f32[8,128]{1,0:T(8,128)S(1)}, u32[]{:S(2)}, u32[]{:S(2)}) collective-permute-start(f32[8,128]{1,0:T(8,128)S(1)} %add.893), channel_id=1, source_target_pairs={{0,64},{16,80},{32,96},{48,112},{64,0},{80,16},{96,32},{112,48},{1... | collective-permute-start | bytes 12296 | tf_op jit(solution)/shard_map/ppermute | solution.py:409
  309.3 15.0 %all-to-all-start.2 = ((bf16[16,64,256]{2,1,0:T(8,128)(2,1)}), bf16[16,64,256]{2,1,0:T(8,128)(2,1)S(1)}, u32[]{:S(2)}, u32[]{:S(2)}) async-start(bf16[16,64,256]{2,1,0:T(8,128)(2,1)} %bitcast.53), calls=%async_computation.3 | async-start | bytes 1048576 | tf_op jit(solution)/shard_map/all_to_all | solution.py:431
  321.6 3.8 %copy-start.4 = (f32[1024,256,1]{1,0,2:T(8,128)}, f32[1024,256,1]{1,0,2:T(8,128)S(1)}, u32[]{:S(2)}) copy-start(f32[1024,256,1]{1,0,2:T(8,128)S(1)} %fusion.8) | copy-start | bytes 3145732
Sparse Core Ops, SparseCore 0:
  271.2 38.0 reduce-scatter.1

commit v3 on v2

v3 whole, which is shorter than its diff:
```python
import functools
import math

import jax
import jax.numpy as jnp
from jax import lax
from jax.experimental import pallas as pl
from jax.experimental.pallas import tpu as pltpu
from jax.sharding import PartitionSpec as P

RADIUS = 10
TAPS = 6
SIGMAS = (1.0, 2.0, 4.0)
FLOOR_SHARE = 0.5
BF16 = jnp.bfloat16
F32 = jnp.float32

ROW_BLOCK = 128
ROW_STEP = 256
ROW_SPAN = 288
COL_BLOCK = 128
COL_STEP = 256
COL_GROUP = 8
BLUR_BLOCK = 256
BLUR_STEP = 512
BLUR_BAND = (112, 400)
LANES = 128
LIMIT = 28 * 1024 * 1024


def psf_kernel(coefficient):
    offsets = jnp.arange(-RADIUS, RADIUS + 1).astype(coefficient.dtype)
    sigmas = jnp.array(SIGMAS, dtype=coefficient.dtype)
    gaussians = jnp.exp(
        -(offsets[None, :] * offsets[None, :]) / (2.0 * sigmas[:, None] * sigmas[:, None])
    )
    kernel = jnp.sum(coefficient[:, :, None] * gaussians[None, :, :], axis=1)
    return kernel / jnp.sum(kernel, axis=1, keepdims=True)


def lanczos_taps(f):
    g = 1.0 - f
    third = math.pi / 3.0
    tiny = 1e-6
    a = jnp.sin(third * f)
    b = jnp.sin(third * g)
    c = a + b
    fg = f * g
    a_over_f = jnp.where(f < tiny, third, a / jnp.maximum(f, tiny))
    b_over_g = jnp.where(g < tiny, third, b / jnp.maximum(g, tiny))
    values = [
        b * fg / ((f + 2.0) * (f + 2.0)),
        -c * fg / ((f + 1.0) * (f + 1.0)),
        a_over_f * g,
        b_over_g * f,
        -c * fg / ((2.0 - f) * (2.0 - f)),
        a * fg / ((3.0 - f) * (3.0 - f)),
    ]
    total = functools.reduce(jnp.add, values)
    return [lax.reduce_precision(value / total, 8, 7) for value in values]


def coverage(starts, taps, extent):
    running = jnp.zeros(starts.shape, F32)
    for tap_at, tap in enumerate(taps):
        position = starts + tap_at
        inside = (position >= 0) & (position < extent)
        running = running + jnp.where(inside, tap, 0.0)
    return running


def band_tables(starts, taps):
    place = jnp.arange(8, dtype=jnp.int32)[:, None]
    diff = place - starts[..., None, :]
    at = diff & 7
    turned = jnp.zeros(diff.shape, F32)
    for tap_at, tap in enumerate(taps):
        turned = turned + jnp.where(at == tap_at, tap[..., None, :], 0.0)
    return turned, diff - at


def toeplitz(kernel_ref, at, rows, cols, shift):
    diff = (
        lax.broadcasted_iota(jnp.int32, (rows, cols), 0)
        - lax.broadcasted_iota(jnp.int32, (rows, cols), 1)
    )
    full = jnp.zeros((rows, cols), F32)
    for tap_at in range(2 * RADIUS + 1):
        full = jnp.where(diff == tap_at - shift, kernel_ref[at, tap_at], full)
    return full


def dot(a, b):
    return jnp.dot(a, b, preferred_element_type=F32)


def two_parts(value):
    high = value.astype(BF16)
    return high, (value - high.astype(F32)).astype(BF16)


def halves_sum(value):
    half = value.shape[0] // 2
    return value[:half] + value[half:]


def band_of(turned, key, first, groups):
    moved = key + first
    return [jnp.where(moved == -8 * g, turned, 0.0) for g in range(groups)]


def row_matrix(blur_ref, turned, key, start, extent, masked):
    last = extent - ROW_STEP
    first = jnp.minimum(start, last)
    groups = ROW_SPAN // 8
    pieces = band_of(turned, key, first - 16, groups)
    for g in range(2):
        pieces[g] = jnp.where(first > 0, pieces[g], 0.0)
        pieces[groups - 1 - g] = jnp.where(first < last, pieces[groups - 1 - g], 0.0)
    band = jnp.concatenate(pieces, axis=0).astype(BF16)
    both = halves_sum(dot(blur_ref[...], band))
    if masked:
        row = lax.broadcasted_iota(jnp.int32, both.shape, 0) + first
        both = jnp.where(row >= start, both, 0.0)
    return jnp.concatenate(two_parts(both.T), axis=0)


def prepare_body(extent, row_kernel_ref, kernel_ref, low_ref, turned_ref, key_ref, rows_ref,
                 blur_ref, cols_ref):
    high, rest = two_parts(toeplitz(row_kernel_ref, 0, ROW_STEP, ROW_SPAN, 16 + RADIUS))
    blur_ref[0:ROW_STEP] = high
    blur_ref[ROW_STEP : 2 * ROW_STEP] = rest

    def block(at, carry):
        rows_ref[at] = row_matrix(
            blur_ref, turned_ref[at], key_ref[at], low_ref[at], extent, False
        )
        return carry

    lax.fori_loop(0, turned_ref.shape[0], block, 0)
    begin, end = BLUR_BAND
    for e in range(cols_ref.shape[0]):
        high, rest = two_parts(
            toeplitz(kernel_ref, e, end - begin, BLUR_BLOCK, begin - LANES + RADIUS)
        )
        cols_ref[e, 0] = high
        cols_ref[e, 1] = rest


def prepare(row_kernel, kernels, low, turned, key, extent):
    exposures = kernels.shape[0]
    blocks = turned.shape[0]
    vmem = pl.BlockSpec(memory_space=pltpu.VMEM)
    smem = pl.BlockSpec(memory_space=pltpu.SMEM)
    return pl.pallas_call(
        functools.partial(prepare_body, extent),
        out_shape=(
            jax.ShapeDtypeStruct((blocks, 2 * ROW_BLOCK, ROW_STEP), BF16),
            jax.ShapeDtypeStruct((2 * ROW_STEP, ROW_SPAN), BF16),
            jax.ShapeDtypeStruct((exposures, 2, BLUR_BAND[1] - BLUR_BAND[0], BLUR_BLOCK), BF16),
        ),
        in_specs=[smem, smem, smem, vmem, vmem],
        out_specs=(vmem, vmem, vmem),
        compiler_params=pltpu.CompilerParams(vmem_limit_bytes=LIMIT),
        cost_estimate=pl.CostEstimate(
            flops=4_000_000_000, bytes_accessed=8 * 1024 * 1024, transcendentals=0
        ),
        name="prepare",
    )(row_kernel, kernels, low, turned, key)


def row_body(slots, low_ref, num_ref, x_ref, rows_ref, blur_ref, turned_ref, key_ref, out_ref):
    extent = x_ref.shape[0]
    owner_rows = out_ref.shape[2]
    blocks = turned_ref.shape[0] // slots

    def times(matrix, start):
        first = pl.multiple_of(jnp.minimum(start, extent - ROW_STEP), 16)
        return halves_sum(dot(matrix, x_ref[pl.ds(first, ROW_STEP), :]))

    def block(at, carry):
        indices = [slot * blocks + at for slot in range(slots)]
        sums = [times(rows_ref[index], low_ref[index]) for index in indices]
        for slot, index in enumerate(indices):

            def more(i, total, index=index):
                start = low_ref[index] + i * ROW_STEP
                matrix = row_matrix(
                    blur_ref, turned_ref[index], key_ref[index], start, extent, True
                )
                return total + times(matrix, start)

            total = lax.fori_loop(1, num_ref[index], more, sums[slot]).astype(BF16)
            for owner in range(ROW_BLOCK // owner_rows):
                out_ref[at * (ROW_BLOCK // owner_rows) + owner, slot] = total[
                    owner * owner_rows : (owner + 1) * owner_rows
                ]
        return carry

    lax.fori_loop(0, blocks, block, 0)


def row_warp(x, low, num, matrices, blur, turned, key, slots, owners):
    width = x.shape[1]
    owner_rows = turned.shape[0] // slots * ROW_BLOCK // owners
    vmem = pl.BlockSpec(memory_space=pltpu.VMEM)
    smem = pl.BlockSpec(memory_space=pltpu.SMEM)
    return pl.pallas_call(
        functools.partial(row_body, slots),
        out_shape=jax.ShapeDtypeStruct((owners, slots, owner_rows, width), BF16),
        in_specs=[smem, smem] + [vmem] * 5,
        out_specs=vmem,
        compiler_params=pltpu.CompilerParams(vmem_limit_bytes=LIMIT),
        cost_estimate=pl.CostEstimate(
            flops=2_000_000_000, bytes_accessed=8 * 1024 * 1024, transcendentals=0
        ),
        name="row_warp",
    )(low, num, x, matrices, blur, turned, key)


def col_body(cols, slots, count_ref, list_ref, low_ref, most_ref, from_ref, to_ref, weight_ref,
             z_ref, blur_ref, turned_ref, key_ref, out_ref, padded, blur, blurred, held):
    rows = z_ref.shape[2]
    width = z_ref.shape[3]
    sources = cols // width
    exposures = z_ref.shape[0] // sources
    patch = pl.program_id(0)
    begin, end = BLUR_BAND

    @pl.when(patch == 0)
    def _():
        pad = jnp.zeros((slots * rows, LANES), BF16)
        padded[:, 0:LANES] = pad
        padded[:, LANES + cols : 2 * LANES + cols] = pad
        for n in range(2):
            blur[n, 0:begin] = jnp.zeros((begin, BLUR_BLOCK), BF16)
            blur[n, end:BLUR_STEP] = jnp.zeros((BLUR_STEP - end, BLUR_BLOCK), BF16)
        for e in range(exposures):
            for n in range(2):
                blur[n, begin:end] = blur_ref[e, n]
            for s in range(sources):
                padded[:, LANES + s * width : LANES + (s + 1) * width] = z_ref[
                    e * sources + s
                ].reshape(slots * rows, width)
            windows = jnp.concatenate(
                [
                    padded[:, b * BLUR_BLOCK : b * BLUR_BLOCK + BLUR_STEP]
                    for b in range(cols // BLUR_BLOCK)
                ],
                axis=0,
            )
            high, rest = two_parts(dot(windows, blur[0]) + dot(windows, blur[1]))
            for b in range(cols // BLUR_BLOCK):
                for j in range(slots):
                    at = (b * slots + j) * rows
                    span = slice(b * BLUR_BLOCK, (b + 1) * BLUR_BLOCK)
                    blurred[e * slots + j, 0:rows, span] = high[at : at + rows]
                    blurred[e * slots + j, rows : 2 * rows, span] = rest[at : at + rows]
            for j in range(slots):
                blurred[e * slots + j, :, cols : cols + COL_STEP] = jnp.zeros(
                    (2 * rows, COL_STEP), BF16
                )

    held[...] = jnp.zeros(held.shape, F32)

    def part(slot, b, n):
        first = pl.multiple_of(jnp.minimum(low_ref[slot, b] + n * COL_STEP, cols), LANES)
        band = band_of(turned_ref[slot, b], key_ref[slot, b], first, COL_STEP // 8)
        band = jnp.concatenate(band, axis=0).astype(BF16)
        return halves_sum(dot(blurred[slot, :, pl.ds(first, COL_STEP)], band))

    per_owner = held.shape[2] // COL_BLOCK

    def add_slot(i, carry):
        slot = list_ref[patch, i]
        weight = weight_ref[slot]

        def add_group(c, carry):
            def add_parts(n):
                sums = [part(slot, c * COL_GROUP + h, n) for h in range(COL_GROUP)]
                for h, total in enumerate(sums):
                    owner = c * (COL_GROUP // per_owner) + h // per_owner
                    span = slice((h % per_owner) * COL_BLOCK, (h % per_owner + 1) * COL_BLOCK)
                    held[owner, :, span] += weight * total

            add_parts(0)

            def more(n, carry):
                add_parts(n)
                return carry

            lax.fori_loop(1, most_ref[slot, c], more, 0)
            return carry

        return lax.fori_loop(from_ref[slot], to_ref[slot], add_group, carry)

    lax.fori_loop(0, count_ref[patch], add_slot, 0)
    out_ref[0] = held[...].astype(out_ref.dtype)


def col_warp(z, count, listed, low, most, begin, end, weight, blur, turned, key, cols, patches,
             owners):
    slots, rows = z.shape[1:3]
    slot_total, blocks = turned.shape[:2]
    own_cols = blocks * COL_BLOCK // owners
    vmem = pl.BlockSpec(memory_space=pltpu.VMEM)
    smem = pl.BlockSpec(memory_space=pltpu.SMEM)
    return pl.pallas_call(
        functools.partial(col_body, cols, slots),
        out_shape=jax.ShapeDtypeStruct((patches, owners, rows, own_cols), BF16),
        grid=(patches,),
        in_specs=[smem] * 7 + [vmem] * 4,
        out_specs=pl.BlockSpec((1, owners, rows, own_cols), lambda k: (k, 0, 0, 0)),
        scratch_shapes=[
            pltpu.VMEM((slots * rows, cols + 2 * LANES), BF16),
            pltpu.VMEM((2, BLUR_STEP, BLUR_BLOCK), BF16),
            pltpu.VMEM((slot_total, 2 * rows, cols + COL_STEP), BF16),
            pltpu.VMEM((owners, rows, own_cols), F32),
        ],
        compiler_params=pltpu.CompilerParams(
            dimension_semantics=("arbitrary",), vmem_limit_bytes=LIMIT
        ),
        cost_estimate=pl.CostEstimate(
            flops=8_000_000_000, bytes_accessed=16 * 1024 * 1024, transcendentals=0
        ),
        name="col_warp",
    )(count, listed, low, most, begin, end, weight, z, blur, turned, key)


def butterfly_sum(x, axis):
    size = lax.axis_size(axis)
    step = 1
    while step < size:
        x = x + lax.ppermute(x, axis, [(i, i ^ step) for i in range(size)])
        step *= 2
    return x


def local(image, variance, psf_coef, correlations, row_start, row_frac, col_start, col_frac):
    exp_dev, height, width = image.shape
    exposures, slots = correlations.shape
    patch_rows = row_start.shape[2]
    patch_cols = col_start.shape[2]
    cores = lax.axis_size("core")
    visits = lax.axis_size("y") * cores
    regions = lax.axis_size("region")
    extent = height * regions
    parts = regions // exp_dev
    part_cols = width // parts
    own_cols = patch_cols // regions
    pair_at = lax.axis_index("y")
    core_at = lax.axis_index("core")
    visit_at = pair_at * cores + core_at
    region_at = lax.axis_index("region")

    def exchange(x, axis):
        return lax.all_to_all(x, axis, split_axis=0, concat_axis=0, tiled=True)

    sent = image.reshape(exp_dev, height, parts, part_cols).transpose(0, 2, 1, 3)
    sent, variance = lax.optimization_barrier(
        (sent.reshape(regions, height, part_cols), variance)
    )
    columns = exchange(sent, "region").reshape(extent, part_cols)

    kernels = psf_kernel(psf_coef)
    tile = jnp.zeros((8, LANES), F32).at[:exp_dev, : 2 * RADIUS + 1].set(kernels)
    other = lax.ppermute(tile, "core", [(i, i ^ 1) for i in range(cores)])
    other = other[:exp_dev, : 2 * RADIUS + 1]
    pair_kernels = jnp.concatenate(
        [jnp.where(core_at == 0, kernels, other), jnp.where(core_at == 0, other, kernels)]
    )
    local_sums = jnp.sum(variance.astype(F32), axis=(1, 2))
    tile = jnp.zeros((8, LANES), F32).at[0, :exp_dev].set(local_sums)
    tile = butterfly_sum(tile, "region")
    at_visit = lax.broadcasted_iota(jnp.int32, (8, LANES), 0) == visit_at
    tile = jnp.where(at_visit, tile[0:1], 0.0)
    tile = butterfly_sum(tile, "core")
    pair_exp = cores * exp_dev
    first_exp = pair_at * pair_exp
    pair_sums = lax.dynamic_slice_in_dim(tile, pair_at * cores, cores, 0)[:, :exp_dev]
    slot_weight = jnp.repeat(1.0 / (pair_sums.reshape(pair_exp) / (extent * width)), slots)

    own_exp = region_at // parts
    at_exp = visit_at * exp_dev + own_exp
    blocks = slots * patch_rows // ROW_BLOCK
    starts = lax.dynamic_index_in_dim(row_start, at_exp, 0, keepdims=False)
    fracs = lax.dynamic_index_in_dim(row_frac, at_exp, 0, keepdims=False)
    starts = starts.reshape(blocks, ROW_BLOCK)
    row_turned, row_key = band_tables(starts, lanczos_taps(fracs.reshape(blocks, ROW_BLOCK)))
    row_low = jnp.clip(starts[:, 0] - RADIUS, 0, extent - ROW_STEP) // 16 * 16
    row_end = jnp.minimum(starts[:, -1] + TAPS + RADIUS, extent)
    row_num = jnp.maximum(row_end - row_low + ROW_STEP - 1, 0) // ROW_STEP
    row_matrices, row_blur, col_blur = prepare(
        lax.dynamic_slice_in_dim(kernels, own_exp, 1, 0), pair_kernels, row_low, row_turned,
        row_key, extent,
    )

    slot_total = pair_exp * slots
    col_blocks = patch_cols // COL_BLOCK
    own_starts = lax.dynamic_slice_in_dim(col_start, first_exp, pair_exp, 0)
    own_fracs = lax.dynamic_slice_in_dim(col_frac, first_exp, pair_exp, 0)
    own_starts = own_starts.reshape(slot_total, col_blocks, COL_BLOCK)
    own_fracs = own_fracs.reshape(slot_total, col_blocks, COL_BLOCK)
    col_turned, col_key = band_tables(own_starts, lanczos_taps(own_fracs))
    col_low = jnp.clip(own_starts[:, :, 0], 0, width) // LANES * LANES
    col_end = jnp.minimum(own_starts[:, :, -1] + TAPS, width)
    col_num = jnp.maximum(col_end - col_low + COL_STEP - 1, 0) // COL_STEP
    col_most = jnp.max(col_num.reshape(slot_total, col_blocks // COL_GROUP, COL_GROUP), axis=2)
    group_at = jnp.arange(col_blocks // COL_GROUP, dtype=jnp.int32)
    col_from = jnp.min(jnp.where(col_most > 0, group_at, col_blocks // COL_GROUP), axis=1)
    col_to = jnp.max(jnp.where(col_most > 0, group_at + 1, 0), axis=1)
    owners = lax.dynamic_slice_in_dim(correlations, first_exp, pair_exp, 0).reshape(slot_total)
    named = owners == jnp.arange(visits, dtype=jnp.int32)[:, None]
    named = named.astype(jnp.int32)
    count = jnp.sum(named, axis=1)
    slot_ids = jnp.arange(slot_total, dtype=jnp.int32)
    rank = jnp.sum(jnp.where(slot_ids[:, None] < slot_ids, named[:, :, None], 0), axis=1)
    listed = jnp.sum(
        jnp.where((named[:, None, :] > 0) & (rank[:, None, :] == slot_ids[:, None]), slot_ids, 0),
        axis=2,
    )

    warped = row_warp(
        columns, row_low, row_num, row_matrices, row_blur, row_turned, row_key, slots,
        cores * regions,
    )
    tile, warped = lax.optimization_barrier((tile, warped))
    rows = exchange(warped, ("core", "region"))
    tile = butterfly_sum(tile, "y")
    weight = 1.0 / (tile[:visits, :exp_dev].reshape(exposures) / (extent * width))
    mean_weight = jnp.mean(weight)
    partial = col_warp(
        rows, count, listed, col_low, col_most, col_from, col_to, slot_weight, col_blur,
        col_turned, col_key, width, visits, regions,
    )
    pieces = exchange(
        partial.reshape((visits * regions,) + partial.shape[2:]), ("y", "core", "region")
    )
    summed = jnp.sum(
        pieces.reshape(visits // cores, patch_rows, own_cols).astype(F32), axis=0, keepdims=True
    )

    total_slots = exposures * slots
    row_cover = coverage(
        row_start.reshape(total_slots, patch_rows),
        lanczos_taps(row_frac.reshape(total_slots, patch_rows)),
        extent,
    )
    at = region_at * own_cols
    col_cover = coverage(
        lax.dynamic_slice_in_dim(col_start, at, own_cols, 2).reshape(total_slots, own_cols),
        lanczos_taps(
            lax.dynamic_slice_in_dim(col_frac, at, own_cols, 2).reshape(total_slots, own_cols)
        ),
        width,
    )
    scale = jnp.where(
        correlations.reshape(total_slots) == visit_at, jnp.repeat(weight, slots), 0.0
    )
    weight_map = lax.dot_general(
        row_cover,
        col_cover * scale[:, None],
        (((0,), (0,)), ((), ())),
        precision=lax.Precision.HIGHEST,
        preferred_element_type=F32,
    ).reshape(1, patch_rows, own_cols)
    coadd = summed / jnp.maximum(weight_map, FLOOR_SHARE * mean_weight)
    return coadd, weight_map


def solution(mesh):
    visits, regions = mesh.devices.shape
    split = jax.sharding.Mesh(
        mesh.devices.reshape(visits // 2, 2, regions), ("y", "core", "region")
    )
    visit = ("y", "core")
    placed = (
        P(visit, "region", None),
        P(visit, "region", None),
        P(visit, None),
        P(),
        P(),
        P(),
        P(),
        P(),
    )
    return jax.shard_map(
        local,
        mesh=split,
        in_specs=placed,
        out_specs=(P(visit, None, "region"), P(visit, None, "region")),
        check_vma=False,
    )
```

time: 335 us -> 198 us (0.59)
  Pallas kernels: 158 us -> 32.7 us
  between operations: 15 us -> 1.68 us
  waiting for transfers between devices: 75.1 us -> 68.5 us
  local copies, waits for them, and re-layouts: 11.3 us -> 15.6 us
  other arithmetic: 23.5 us -> 27.3 us
    pallas_call x2 -> x1, Pallas kernels: 144 us -> 18.1 us  [col_warp(): pl.pallas_call(functools.partial(col_body, cols, slots), out_shape=jax.Sh...]
    reduce_scatter x1 -> x0, waiting for transfers between devices: 19.2 us -> none  [local(): summed = lax.psum_scatter(partial, 'visit', scatter_dimension=0, tiled=True)]
    ppermute x7, waiting for transfers between devices: 35.1 us -> 41.8 us  [butterfly_sum(): x = x + lax.ppermute(x, axis, [(i, i ^ step) for i in range(size)])]
    all_to_all x3, waiting for transfers between devices: 20.8 us -> 26.7 us  [exchange(): return lax.all_to_all(x, axis, split_axis=0, concat_axis=0, tiled=True)]
    unnamed x23 -> x25, local copies, waits for them, and re-layouts: 6.48 us -> 7.91 us
  transfers between devices with their start and end apart: 11 -> 11, of which waited for: 8 -> 6; matrix products, arithmetic and copies ran while one was open for 8% -> 15% of each run, Pallas kernels for 41% -> 14%
where the time goes in v3:
time: 198 us; the launch traced here: 196 us
  waiting for transfers between devices  68.5 us (35%)
  starting transfers between devices  48.9 us (25%)
  Pallas kernels  32.7 us (17%)
  other arithmetic  27.3 us (14%)
  local copies, waits for them, and re-layouts  15.6 us (8%)
    ppermute x7, waiting for transfers between devices, butterfly_sum(): x = x + lax.ppermute(x, axis, [(i, i ^ step) for i in range(size)])  41.8 us
    ppermute x7, starting transfers between devices, butterfly_sum(): x = x + lax.ppermute(x, axis, [(i, i ^ step) for i in range(size)])  28.7 us
    all_to_all x3, waiting for transfers between devices, exchange(): return lax.all_to_all(x, axis, split_axis=0, concat_axis=0, tiled=True)  26.7 us
    all_to_all x3, starting transfers between devices, exchange(): return lax.all_to_all(x, axis, split_axis=0, concat_axis=0, tiled=True)  20.2 us
    pallas_call x1, Pallas kernels, col_warp(): pl.pallas_call(functools.partial(col_body, cols, slots), out_shape=jax.Sh...  18.1 us
    add x1, other arithmetic, coverage(): running = running + jnp.where(inside, tap, 0.0)  10.2 us
    pallas_call x1, Pallas kernels, prepare(): pl.pallas_call(functools.partial(prepare_body, extent), out_shape=(jax.Sh...  8.33 us
    unnamed x25, local copies, waits for them, and re-layouts  7.91 us
  transfers between devices with their start and end apart: 11, of which 6 were waited for; matrix products, arithmetic and copies ran while one was open for 15% of the time, Pallas kernels for 14%

profile of v3, /device:TPU:4, one launch (start us, length us, event | category | flops | bytes accessed | tf_op | source)
XLA Modules:
  0.0 195.6 jit_solution(12022964391878249761)
XLA Ops:
  0.6 2.6 %fusion.63 = (bf16[4,256,512]{2,1,0:T(8,128)(2,1)S(1)}, bf16[4,256,512]{2,1,0:T(8,128)(2,1)S(1)}, bf16[4,256,512]{2,1,0:T(8,128)(2,1)S(1)}, bf16[4,256,512]{2,1,0:T(8,128)(2,1)S(1)}) fusion(bf16[4,256,2048]{2,1,0:T(8,128)(2,1)} %param.13), kind=kLoop, calls=%fused_computation.221 | loop fusion | bytes 8388608 | tf_op jit(solution)/shard_map/slice.44
  3.2 2.3 %pad_maximum_fusion = bf16[4,1024,512]{2,1,0:T(8,128)(2,1)} fusion(bf16[4,256,512]{2,1,0:T(8,128)(2,1)S(1)} %get-tuple-element.56, bf16[4,256,512]{2,1,0:T(8,128)(2,1)S(1)} %get-tuple-element.57, bf16[4,256,512]{2,1,0:T(8,128)(2,1)S(1)} %get-tuple-element.55, bf16[4,256,512]{2,1,0:T(8,128)(2,1)S(1)} %get-tuple-element.54), kind=kLoop, calls=%fused_computation.1 | loop fusion | flops 16777216 | bytes 8388608 | tf_op jit(solution)/shard_map/concatenate.5
  5.5 1.4 copy-done.4
  7.6 2.0 %collective-permute-start = (f32[8,128]{1,0:T(8,128)S(1)}, f32[8,128]{1,0:T(8,128)S(1)}, u32[]{:S(2)}, u32[]{:S(2)}) collective-permute-start(f32[8,128]{1,0:T(8,128)S(1)} %scatter.12), channel_id=1, source_target_pairs={{0,1},{1,0},{2,3},{3,2},{4,5},{5,4},{6,7},{7,6},{8,9},{9,8},{10,11... | collective-permute-start | bytes 12296 | tf_op jit(solution)/shard_map/ppermute | solution.py:334
  9.6 7.8 %all-to-all-start = ((bf16[16,256,512]{2,1,0:T(8,128)(2,1)}), bf16[16,256,512]{2,1,0:T(8,128)(2,1)}, u32[]{:S(2)}, u32[]{:S(2)}) async-start(bf16[16,256,512]{2,1,0:T(8,128)(2,1)} %bitcast.57), calls=%async_computation | async-start | bytes 8388608 | tf_op jit(solution)/shard_map/all_to_all | solution.py:357
  22.5 1.0 constant_dynamic-slice_fusion
  23.7 3.0 %collective-permute-start.1 = (f32[8,128]{1,0:T(8,128)S(1)}, f32[8,128]{1,0:T(8,128)S(1)}, u32[]{:S(2)}, u32[]{:S(2)}) collective-permute-start(f32[8,128]{1,0:T(8,128)S(1)} %add.688), channel_id=1, source_target_pairs={{0,2},{1,3},{2,0},{3,1},{4,6},{5,7},{6,4},{7,5},{8,10},{9,11},{10,... | collective-permute-start | bytes 12296 | tf_op jit(solution)/shard_map/ppermute | solution.py:334
  26.8 24.4 %collective-permute-done.1 = f32[8,128]{1,0:T(8,128)S(1)} collective-permute-done((f32[8,128]{1,0:T(8,128)S(1)}, f32[8,128]{1,0:T(8,128)S(1)}, u32[]{:S(2)}, u32[]{:S(2)}) %collective-permute-start.1) | collective-permute-done | bytes 4128 | tf_op jit(solution)/shard_map/ppermute | solution.py:334
  51.2 18.9 %collective-permute-start.2 = (f32[8,128]{1,0:T(8,128)S(1)}, f32[8,128]{1,0:T(8,128)S(1)}, u32[]{:S(2)}, u32[]{:S(2)}) collective-permute-start(f32[8,128]{1,0:T(8,128)S(1)} %add.689), channel_id=1, source_target_pairs={{0,4},{1,5},{2,6},{3,7},{4,0},{5,1},{6,2},{7,3},{8,12},{9,13},{10,... | collective-permute-start | bytes 12296 | tf_op jit(solution)/shard_map/ppermute | solution.py:334
  70.1 10.5 %collective-permute-done.2 = f32[8,128]{1,0:T(8,128)S(1)} collective-permute-done((f32[8,128]{1,0:T(8,128)S(1)}, f32[8,128]{1,0:T(8,128)S(1)}, u32[]{:S(2)}, u32[]{:S(2)}) %collective-permute-start.2) | collective-permute-done | bytes 4128 | tf_op jit(solution)/shard_map/ppermute | solution.py:334
  80.6 5.1 %collective-permute-done.3 = f32[8,128]{1,0:T(8,128)S(1)} collective-permute-done((f32[8,128]{1,0:T(8,128)S(1)}, f32[8,128]{1,0:T(8,128)S(1)}, u32[]{:S(2)}, u32[]{:S(2)}) %collective-permute-start.3) | collective-permute-done | bytes 4128 | tf_op jit(solution)/shard_map/ppermute | solution.py:334
  85.8 8.3 %prepare.1 = (bf16[16,256,256]{2,1,0:T(8,128)(2,1)S(1)}, bf16[512,288]{1,0:T(8,128)(2,1)S(1)}, bf16[8,2,288,256]{3,2,1,0:T(8,128)(2,1)S(1)}) custom-call(f32[1,21]{1,0:T(1,128)S(1)} %constant_dynamic-slice_fusion.2.row_kernel_ref, f32[8,21]{1,0:T(8,128)S(1)} %pad_maximum_fusion.1.kernel_ref, s32[16]{0:T(128)S(1)} %get-tuple-element.53.low_ref, ...), custom_call_target="tpu_custom_call" | custom-call | flops 4000000000 | bytes 8388608 | tf_op jit(solution)/shard_map/prepare/pallas_call | solution.py:155
  94.1 1.5 copy-done.2
  95.7 6.2 %row_warp.1 = bf16[32,2,32,512]{3,2,1,0:T(8,128)(2,1)} custom-call(s32[16]{0:T(128)S(1)} %get-tuple-element.53.low_ref, s32[16]{0:T(128)S(1)} %get-tuple-element.52.num_ref, bf16[4096,512]{1,0:T(8,128)(2,1)} %bitcast.6.x_ref, bf16[16,256,256]{2,1,0:T(8,128)(2,1)S(1)} %get-tuple-element.35.rows_ref, bf16[512,288]{1,0:T(8,128)(2,1)S(1)} %get-tuple-element.36.blur_ref, ...), custom_call_target="tpu_custom_call" | custom-call | flops 2000000000 | bytes 8388608 | tf_op jit(solution)/shard_map/row_warp/pallas_call | solution.py:208
  101.9 5.1 %all-to-all-start.1 = ((bf16[32,2,32,512]{3,2,1,0:T(8,128)(2,1)}), bf16[32,2,32,512]{3,2,1,0:T(8,128)(2,1)}, u32[]{:S(2)}, u32[]{:S(2)}) async-start(bf16[32,2,32,512]{3,2,1,0:T(8,128)(2,1)} %row_warp.1), calls=%async_computation.1 | async-start | bytes 4194304 | tf_op jit(solution)/shard_map/all_to_all | solution.py:357
  107.7 2.1 %divide_reduce-precision_fusion.5 = (f32[16,32,128]{2,1,0:T(8,128)S(1)}, f32[16,32,128]{2,1,0:T(8,128)S(1)}) fusion(f32[16,32,128]{2,1,0:T(8,128)S(1)} %reshape.624), kind=kLoop, calls=%fused_computation.62 | loop fusion | flops 2555904 | bytes 786432 | tf_op jit(solution)/shard_map/reduce_precision | solution.py:60
  109.9 2.1 %divide_reduce-precision_fusion.4 = (f32[16,32,128]{2,1,0:T(8,128)S(1)}, f32[16,32,128]{2,1,0:T(8,128)S(1)}, f32[16,32,128]{2,1,0:T(8,128)S(1)}, f32[16,32,128]{2,1,0:T(8,128)S(1)}, f32[16,32,128]{2,1,0:T(8,128)S(1)}) fusion(f32[16,32,128]{2,1,0:T(8,128)S(1)} %get-tuple-element.49, f32[16,32,128]{2,1,0:T(8,128)S(1)} %reshape.624), kind=kLoop, calls=%fused_computation.61 | loop fusion | flops 2424832 | bytes 1835008 | tf_op jit(solution)/shard_map/reduce_precision | solution.py:60
  112.0 2.5 %select_add_fusion.turned_ref = f32[16,32,8,128]{3,2,1,0:T(8,128)} fusion(f32[16,32,128]{2,1,0:T(8,128)S(1)} %get-tuple-element.62, f32[16,32,128]{2,1,0:T(8,128)S(1)} %get-tuple-element.59, f32[16,32,128]{2,1,0:T(8,128)S(1)} %get-tuple-element.60, f32[16,32,128]{2,1,0:T(8,128)S(1)} %get-tuple-element.61, f32[16,32,128]{2,1,0:T(8,128)S(1)} %get-tuple-element.58, ...), kind=kLoop, calls=%fused_computation.10 | loop fusion | flops 9961472 | bytes 3932160 | tf_op jit(solution)/shard_map/add | solution.py:78
  114.5 1.6 collective-permute-start.6
  116.3 1.8 collective-permute-done.6
  118.1 3.2 %collective-permute-start.7 = (f32[8,128]{1,0:T(8,128)S(1)}, f32[8,128]{1,0:T(8,128)S(1)}, u32[]{:S(2)}, u32[]{:S(2)}) collective-permute-start(f32[8,128]{1,0:T(8,128)S(1)} %add.772), channel_id=1, source_target_pairs={{0,64},{32,96},{64,0},{96,32},{1,65},{33,97},{65,1},{97,33},{2,66}... | collective-permute-start | bytes 12296 | tf_op jit(solution)/shard_map/ppermute | solution.py:334
  121.3 13.9 %all-to-all-done.1.z_ref = bf16[32,2,32,512]{3,2,1,0:T(8,128)(2,1)} async-done(((bf16[32,2,32,512]{3,2,1,0:T(8,128)(2,1)}), bf16[32,2,32,512]{3,2,1,0:T(8,128)(2,1)}, u32[]{:S(2)}, u32[]{:S(2)}) %all-to-all-start.1) | async-done | bytes 2097184 | tf_op jit(solution)/shard_map/all_to_all | solution.py:357
  135.2 1.6 copy-done.1
  136.8 1.7 copy-done.3
  138.5 18.1 %col_warp.1 = bf16[8,16,32,256]{3,2,1,0:T(8,128)(2,1)S(1)} custom-call(s32[8]{0:T(128)S(1)} %fusion.58.count_ref, s32[8,16]{1,0:T(8,128)S(1)} %select_reduce_fusion.list_ref, s32[16,32]{1,0:T(8,128)S(1)} %fusion.47.low_ref, s32[16,4]{1,0:T(8,128)S(1)} %copy.48.most_ref, s32[16]{0:T(128)S(1)} %get-tuple-element.45.from_ref, s32[16]{0:T(128)S(1)} %get-tuple-element.44.to_ref, ...), custom_call_target="tpu_custom_call" | custom-call | flops 8000000000 | bytes 16777216 | tf_op jit(solution)/shard_map/col_warp/pallas_call | solution.py:308
  156.6 1.3 copy-done
  158.0 7.2 %all-to-all-start.2 = ((bf16[128,32,256]{2,1,0:T(8,128)(2,1)}), bf16[128,32,256]{2,1,0:T(8,128)(2,1)S(1)}, u32[]{:S(2)}, u32[]{:S(2)}) async-start(bf16[128,32,256]{2,1,0:T(8,128)(2,1)} %bitcast.56), calls=%async_computation.2 | async-start | bytes 4194304 | tf_op jit(solution)/shard_map/all_to_all | solution.py:357
  165.2 10.2 %fusion.12 = f32[32,2,1024]{2,1,0:T(2,128)S(1)} fusion(s32[32,2,1024]{2,1,0:T(2,128)S(1)} %copy-done.6, f32[32,2,1024]{2,1,0:T(2,128)S(1)} %copy-done.7), kind=kLoop, calls=%fused_computation.38 | loop fusion | flops 5636096 | bytes 786432 | tf_op jit(solution)/shard_map/add | solution.py:68
  176.9 3.4 %fusion.31 = f32[32,2,256]{2,1,0:T(2,128)S(1)} fusion(f32[32,2,4096]{2,1,0:T(2,128)} %param.20, s32[]{:T(128)S(6)} %select_n.331, s32[32,2,4096]{2,1,0:T(2,128)} %param.19, f32[32,2]{1,0:T(8,128)S(1)} %copy.49), kind=kLoop, calls=%fused_computation.120 | loop fusion | flops 1425408 | bytes 196868 | tf_op jit(solution)/shard_map/mul | solution.py:462
  180.3 1.0 fusion.13
  181.3 12.8 %all-to-all-done.2 = bf16[128,32,256]{2,1,0:T(8,128)(2,1)S(1)} async-done(((bf16[128,32,256]{2,1,0:T(8,128)(2,1)}), bf16[128,32,256]{2,1,0:T(8,128)(2,1)S(1)}, u32[]{:S(2)}, u32[]{:S(2)}) %all-to-all-start.2) | async-done | bytes 2097184 | tf_op jit(solution)/shard_map/all_to_all | solution.py:357
  194.4 1.2 fusion.1
  (91 shorter events, 8.1 us)
Async XLA Ops:
  3.2 3.7 %copy-start.4 = (bf16[4,256,2048]{2,1,0:T(8,128)(2,1)S(1)}, bf16[4,256,2048]{2,1,0:T(8,128)(2,1)}, u32[]{:S(2)}) copy-start(bf16[4,256,2048]{2,1,0:T(8,128)(2,1)} %param.14) | copy-start | bytes 12582916
  7.6 9.9 %copy-start.9 = (f32[4,3]{1,0:T(4,128)S(1)}, f32[4,3]{1,0:T(4,128)}, u32[]{:S(2)}) copy-start(f32[4,3]{1,0:T(4,128)} %param.15) | copy-start | bytes 148
  7.6 10.0 %copy-start.10 = (f32[3]{0:T(128)S(1)}, f32[3]{0:T(128)}, u32[]{:S(2)}) copy-start(f32[3]{0:T(128)} %constant.259) | copy-start | bytes 40
  7.6 10.4 %copy-start.8 = (s32[32,2]{0,1:T(2,128)S(1)}, s32[32,2]{0,1:T(2,128)}, u32[]{:S(2)}) copy-start(s32[32,2]{0,1:T(2,128)} %param.16) | copy-start | bytes 772
  7.6 15.8 %collective-permute-start = (f32[8,128]{1,0:T(8,128)S(1)}, f32[8,128]{1,0:T(8,128)S(1)}, u32[]{:S(2)}, u32[]{:S(2)}) collective-permute-start(f32[8,128]{1,0:T(8,128)S(1)} %scatter.12), channel_id=1, source_target_pairs={{0,1},{1,0},{2,3},{3,2},{4,5},{5,4},{6,7},{7,6},{8,9},{9,8},{10,11... | collective-permute-start | bytes 12296 | tf_op jit(solution)/shard_map/ppermute | solution.py:334
  9.6 86.0 %all-to-all-start = ((bf16[16,256,512]{2,1,0:T(8,128)(2,1)}), bf16[16,256,512]{2,1,0:T(8,128)(2,1)}, u32[]{:S(2)}, u32[]{:S(2)}) async-start(bf16[16,256,512]{2,1,0:T(8,128)(2,1)} %bitcast.57), calls=%async_computation | async-start | bytes 8388608 | tf_op jit(solution)/shard_map/all_to_all | solution.py:357
  17.9 52.1 %collective-permute-start.5 = (f32[8,128]{1,0:T(8,128)S(1)}, f32[8,128]{1,0:T(8,128)S(1)}, u32[]{:S(2)}, u32[]{:S(2)}) collective-permute-start(f32[8,128]{1,0:T(8,128)S(1)} %scatter.14), channel_id=1, source_target_pairs={{0,16},{16,0},{1,17},{17,1},{2,18},{18,2},{3,19},{19,3},{4,20},{20... | collective-permute-start | bytes 12296 | tf_op jit(solution)/shard_map/ppermute | solution.py:367
  23.7 27.5 %collective-permute-start.1 = (f32[8,128]{1,0:T(8,128)S(1)}, f32[8,128]{1,0:T(8,128)S(1)}, u32[]{:S(2)}, u32[]{:S(2)}) collective-permute-start(f32[8,128]{1,0:T(8,128)S(1)} %add.688), channel_id=1, source_target_pairs={{0,2},{1,3},{2,0},{3,1},{4,6},{5,7},{6,4},{7,5},{8,10},{9,11},{10,... | collective-permute-start | bytes 12296 | tf_op jit(solution)/shard_map/ppermute | solution.py:334
  51.2 29.4 %collective-permute-start.2 = (f32[8,128]{1,0:T(8,128)S(1)}, f32[8,128]{1,0:T(8,128)S(1)}, u32[]{:S(2)}, u32[]{:S(2)}) collective-permute-start(f32[8,128]{1,0:T(8,128)S(1)} %add.689), channel_id=1, source_target_pairs={{0,4},{1,5},{2,6},{3,7},{4,0},{5,1},{6,2},{7,3},{8,12},{9,13},{10,... | collective-permute-start | bytes 12296 | tf_op jit(solution)/shard_map/ppermute | solution.py:334
  80.6 5.1 %collective-permute-start.3 = (f32[8,128]{1,0:T(8,128)S(1)}, f32[8,128]{1,0:T(8,128)S(1)}, u32[]{:S(2)}, u32[]{:S(2)}) collective-permute-start(f32[8,128]{1,0:T(8,128)S(1)} %add.690), channel_id=1, source_target_pairs={{0,8},{1,9},{2,10},{3,11},{4,12},{5,13},{6,14},{7,15},{8,0},{9,1},... | collective-permute-start | bytes 12296 | tf_op jit(solution)/shard_map/ppermute | solution.py:334
  85.8 9.8 %collective-permute-start.4 = (f32[8,128]{1,0:T(8,128)S(1)}, f32[8,128]{1,0:T(8,128)S(1)}, u32[]{:S(2)}, u32[]{:S(2)}) collective-permute-start(f32[8,128]{1,0:T(8,128)S(1)} %broadcast_select_fusion), channel_id=1, source_target_pairs={{0,16},{16,0},{1,17},{17,1},{2,18},{18,2},{3,19},{19,3},{4,20},{20... | collective-permute-start | bytes 12296 | tf_op jit(solution)/shard_map/ppermute | solution.py:334
  94.1 1.5 copy-start.2
  101.9 33.3 %all-to-all-start.1 = ((bf16[32,2,32,512]{3,2,1,0:T(8,128)(2,1)}), bf16[32,2,32,512]{3,2,1,0:T(8,128)(2,1)}, u32[]{:S(2)}, u32[]{:S(2)}) async-start(bf16[32,2,32,512]{3,2,1,0:T(8,128)(2,1)} %row_warp.1), calls=%async_computation.1 | async-start | bytes 4194304 | tf_op jit(solution)/shard_map/all_to_all | solution.py:357
  114.5 3.6 %collective-permute-start.6 = (f32[8,128]{1,0:T(8,128)S(1)}, f32[8,128]{1,0:T(8,128)S(1)}, u32[]{:S(2)}, u32[]{:S(2)}) collective-permute-start(f32[8,128]{1,0:T(8,128)S(1)} %fusion.59), channel_id=1, source_target_pairs={{0,32},{32,0},{64,96},{96,64},{1,33},{33,1},{65,97},{97,65},{2,34}... | collective-permute-start | bytes 12296 | tf_op jit(solution)/shard_map/ppermute | solution.py:334
  118.1 57.3 %collective-permute-start.7 = (f32[8,128]{1,0:T(8,128)S(1)}, f32[8,128]{1,0:T(8,128)S(1)}, u32[]{:S(2)}, u32[]{:S(2)}) collective-permute-start(f32[8,128]{1,0:T(8,128)S(1)} %add.772), channel_id=1, source_target_pairs={{0,64},{32,96},{64,0},{96,32},{1,65},{33,97},{65,1},{97,33},{2,66}... | collective-permute-start | bytes 12296 | tf_op jit(solution)/shard_map/ppermute | solution.py:334
  135.2 1.6 copy-start.1
  136.8 1.7 copy-start.3
  156.6 1.3 copy-start
  158.0 7.2 %copy-start.6 = (s32[32,2,1024]{2,1,0:T(2,128)S(1)}, s32[32,2,1024]{2,1,0:T(2,128)}, u32[]{:S(2)}) copy-start(s32[32,2,1024]{2,1,0:T(2,128)} %param.17) | copy-start | bytes 786436
  158.0 7.3 %copy-start.7 = (f32[32,2,1024]{2,1,0:T(2,128)S(1)}, f32[32,2,1024]{2,1,0:T(2,128)}, u32[]{:S(2)}) copy-start(f32[32,2,1024]{2,1,0:T(2,128)} %param.18) | copy-start | bytes 786436
  158.0 36.1 %all-to-all-start.2 = ((bf16[128,32,256]{2,1,0:T(8,128)(2,1)}), bf16[128,32,256]{2,1,0:T(8,128)(2,1)S(1)}, u32[]{:S(2)}, u32[]{:S(2)}) async-start(bf16[128,32,256]{2,1,0:T(8,128)(2,1)} %bitcast.56), calls=%async_computation.2 | async-start | bytes 4194304 | tf_op jit(solution)/shard_map/all_to_all | solution.py:357
  181.3 14.3 %copy-start.5 = (f32[1024,256,1]{1,0,2:T(8,128)}, f32[1024,256,1]{1,0,2:T(8,128)S(1)}, u32[]{:S(2)}) copy-start(f32[1024,256,1]{1,0,2:T(8,128)S(1)} %fusion.13) | copy-start | bytes 3145732

commit v4 on v3

--- a/solution.py
+++ b/solution.py
@@ -26,6 +26,7 @@
 BLUR_BAND = (112, 400)
 LANES = 128
 LIMIT = 28 * 1024 * 1024
+COL_LIMIT = 56 * 1024 * 1024
 
 
 def psf_kernel(coefficient):
@@ -218,48 +219,78 @@
     )(low, num, x, matrices, blur, turned, key)
 
 
-def col_body(cols, slots, count_ref, list_ref, low_ref, most_ref, from_ref, to_ref, weight_ref,
-             z_ref, blur_ref, turned_ref, key_ref, out_ref, padded, blur, blurred, held):
-    rows = z_ref.shape[2]
-    width = z_ref.shape[3]
+def col_body(cols, count_ref, list_ref, low_ref, most_ref, from_ref, to_ref, weight_ref, z_hbm,
+             blur_hbm, turned_hbm, key_hbm, out_ref, padded, blur, turned_ref, key_ref, blurred,
+             held, z_sems, blur_sems, table_sems):
+    slots, rows, width = z_hbm.shape[1:]
     sources = cols // width
-    exposures = z_ref.shape[0] // sources
+    exposures = z_hbm.shape[0] // sources
     patch = pl.program_id(0)
     begin, end = BLUR_BAND
 
     @pl.when(patch == 0)
     def _():
+        waits = []
+        for e in range(exposures):
+            copies = []
+            for s in range(sources):
+                for j in range(slots):
+                    copies.append(
+                        pltpu.make_async_copy(
+                            z_hbm.at[e * sources + s, j],
+                            padded.at[
+                                e, pl.ds(j * rows, rows), pl.ds(LANES + s * width, width)
+                            ],
+                            z_sems.at[e, s, j],
+                        )
+                    )
+            for n in range(2):
+                copies.append(
+                    pltpu.make_async_copy(
+                        blur_hbm.at[e, n],
+                        blur.at[e, n, pl.ds(begin, end - begin)],
+                        blur_sems.at[e, n],
+                    )
+                )
+            for copy in copies:
+                copy.start()
+            waits.append(copies)
+        tables = [
+            pltpu.make_async_copy(turned_hbm, turned_ref, table_sems.at[0]),
+            pltpu.make_async_copy(key_hbm, key_ref, table_sems.at[1]),
+        ]
+        for copy in tables:
+            copy.start()
         pad = jnp.zeros((slots * rows, LANES), BF16)
-        padded[:, 0:LANES] = pad
-        padded[:, LANES + cols : 2 * LANES + cols] = pad
-        for n in range(2):
-            blur[n, 0:begin] = jnp.zeros((begin, BLUR_BLOCK), BF16)
-            blur[n, end:BLUR_STEP] = jnp.zeros((BLUR_STEP - end, BLUR_BLOCK), BF16)
         for e in range(exposures):
+            padded[e, :, 0:LANES] = pad
+            padded[e, :, LANES + cols : 2 * LANES + cols] = pad
             for n in range(2):
-                blur[n, begin:end] = blur_ref[e, n]
-            for s in range(sources):
-                padded[:, LANES + s * width : LANES + (s + 1) * width] = z_ref[
-                    e * sources + s
-                ].reshape(slots * rows, width)
+                blur[e, n, 0:begin] = jnp.zeros((begin, BLUR_BLOCK), BF16)
+                blur[e, n, end:BLUR_STEP] = jnp.zeros((BLUR_STEP - end, BLUR_BLOCK), BF16)
+            for j in range(slots):
+                blurred[e * slots + j, :, cols : cols + COL_STEP] = jnp.zeros(
+                    (2 * rows, COL_STEP), BF16
+                )
+        for e in range(exposures):
+            for copy in waits[e]:
+                copy.wait()
             windows = jnp.concatenate(
                 [
-                    padded[:, b * BLUR_BLOCK : b * BLUR_BLOCK + BLUR_STEP]
+                    padded[e, :, b * BLUR_BLOCK : b * BLUR_BLOCK + BLUR_STEP]
                     for b in range(cols // BLUR_BLOCK)
                 ],
                 axis=0,
             )
-            high, rest = two_parts(dot(windows, blur[0]) + dot(windows, blur[1]))
+            high, rest = two_parts(dot(windows, blur[e, 0]) + dot(windows, blur[e, 1]))
             for b in range(cols // BLUR_BLOCK):
                 for j in range(slots):
                     at = (b * slots + j) * rows
                     span = slice(b * BLUR_BLOCK, (b + 1) * BLUR_BLOCK)
                     blurred[e * slots + j, 0:rows, span] = high[at : at + rows]
                     blurred[e * slots + j, rows : 2 * rows, span] = rest[at : at + rows]
-            for j in range(slots):
-                blurred[e * slots + j, :, cols : cols + COL_STEP] = jnp.zeros(
-                    (2 * rows, COL_STEP), BF16
-                )
+        for copy in tables:
+            copy.wait()
 
     held[...] = jnp.zeros(held.shape, F32)
 
@@ -300,31 +331,68 @@
 
 def col_warp(z, count, listed, low, most, begin, end, weight, blur, turned, key, cols, patches,
              owners):
-    slots, rows = z.shape[1:3]
+    slots, rows, width = z.shape[1:]
     slot_total, blocks = turned.shape[:2]
+    exposures = blur.shape[0]
     own_cols = blocks * COL_BLOCK // owners
-    vmem = pl.BlockSpec(memory_space=pltpu.VMEM)
     smem = pl.BlockSpec(memory_space=pltpu.SMEM)
     return pl.pallas_call(
-        functools.partial(col_body, cols, slots),
+        functools.partial(col_body, cols),
         out_shape=jax.ShapeDtypeStruct((patches, owners, rows, own_cols), BF16),
         grid=(patches,),
-        in_specs=[smem] * 7 + [vmem] * 4,
+        in_specs=[smem] * 7 + [pl.BlockSpec(memory_space=pl.ANY)] * 4,
         out_specs=pl.BlockSpec((1, owners, rows, own_cols), lambda k: (k, 0, 0, 0)),
         scratch_shapes=[
-            pltpu.VMEM((slots * rows, cols + 2 * LANES), BF16),
-            pltpu.VMEM((2, BLUR_STEP, BLUR_BLOCK), BF16),
+            pltpu.VMEM((exposures, slots * rows, cols + 2 * LANES), BF16),
+            pltpu.VMEM((exposures, 2, BLUR_STEP, BLUR_BLOCK), BF16),
+            pltpu.VMEM(turned.shape, F32),
+            pltpu.VMEM(key.shape, jnp.int32),
             pltpu.VMEM((slot_total, 2 * rows, cols + COL_STEP), BF16),
             pltpu.VMEM((owners, rows, own_cols), F32),
+            pltpu.SemaphoreType.DMA((exposures, cols // width, slots)),
+            pltpu.SemaphoreType.DMA((exposures, 2)),
+            pltpu.SemaphoreType.DMA((2,)),
         ],
         compiler_params=pltpu.CompilerParams(
-            dimension_semantics=("arbitrary",), vmem_limit_bytes=LIMIT
+            dimension_semantics=("arbitrary",), vmem_limit_bytes=COL_LIMIT
         ),
         cost_estimate=pl.CostEstimate(
             flops=8_000_000_000, bytes_accessed=16 * 1024 * 1024, transcendentals=0
         ),
         name="col_warp",
     )(count, listed, low, most, begin, end, weight, z, blur, turned, key)
+
+
+def split_body(image_ref, out_ref):
+    out_ref[...] = image_ref[...]
+
+
+def split_columns(image, parts):
+    exposures, height, width = image.shape
+    block = (1, height, width // parts)
+    return pl.pallas_call(
+        split_body,
+        out_shape=jax.ShapeDtypeStruct((exposures * parts,) + block[1:], image.dtype),
+        grid=(exposures * parts,),
+        in_specs=[pl.BlockSpec(block, lambda i: (i // parts, 0, i % parts))],
+        out_specs=pl.BlockSpec(block, lambda i: (i, 0, 0)),
+        compiler_params=pltpu.CompilerParams(
+            dimension_semantics=("arbitrary",), vmem_limit_bytes=COL_LIMIT
+        ),
+        name="split_columns",
+    )(image)
+
+
+def ring_sum(x, axis, count, stride):
+    size = lax.axis_size(axis)
+    total = x
+    for step in range(1, count):
+        pairs = []
+        for i in range(size):
+            at = i // stride % count
+            pairs.append((i, i + ((at + step) % count - at) * stride))
+        total = total + lax.ppermute(x, axis, pairs)
+    return total
 
 
 def butterfly_sum(x, axis):
@@ -356,10 +424,7 @@
     def exchange(x, axis):
         return lax.all_to_all(x, axis, split_axis=0, concat_axis=0, tiled=True)
 
-    sent = image.reshape(exp_dev, height, parts, part_cols).transpose(0, 2, 1, 3)
-    sent, variance = lax.optimization_barrier(
-        (sent.reshape(regions, height, part_cols), variance)
-    )
+    sent, variance = lax.optimization_barrier((split_columns(image, parts), variance))
     columns = exchange(sent, "region").reshape(extent, part_cols)
 
     kernels = psf_kernel(psf_coef)
@@ -371,14 +436,10 @@
     )
     local_sums = jnp.sum(variance.astype(F32), axis=(1, 2))
     tile = jnp.zeros((8, LANES), F32).at[0, :exp_dev].set(local_sums)
-    tile = butterfly_sum(tile, "region")
-    at_visit = lax.broadcasted_iota(jnp.int32, (8, LANES), 0) == visit_at
-    tile = jnp.where(at_visit, tile[0:1], 0.0)
-    tile = butterfly_sum(tile, "core")
+    inner = 4
+    tile = ring_sum(tile, "region", inner, 1)
     pair_exp = cores * exp_dev
     first_exp = pair_at * pair_exp
-    pair_sums = lax.dynamic_slice_in_dim(tile, pair_at * cores, cores, 0)[:, :exp_dev]
-    slot_weight = jnp.repeat(1.0 / (pair_sums.reshape(pair_exp) / (extent * width)), slots)
 
     own_exp = region_at // parts
     at_exp = visit_at * exp_dev + own_exp
@@ -394,6 +455,10 @@
         lax.dynamic_slice_in_dim(kernels, own_exp, 1, 0), pair_kernels, row_low, row_turned,
         row_key, extent,
     )
+    tile, row_matrices, row_blur, col_blur = lax.optimization_barrier(
+        (tile, row_matrices, row_blur, col_blur)
+    )
+    tile = ring_sum(tile, "region", regions // inner, inner)
 
     slot_total = pair_exp * slots
     col_blocks = patch_cols // COL_BLOCK
@@ -426,6 +491,11 @@
     )
     tile, warped = lax.optimization_barrier((tile, warped))
     rows = exchange(warped, ("core", "region"))
+    at_visit = lax.broadcasted_iota(jnp.int32, (8, LANES), 0) == visit_at
+    tile = jnp.where(at_visit, tile[0:1], 0.0)
+    tile = butterfly_sum(tile, "core")
+    pair_sums = lax.dynamic_slice_in_dim(tile, pair_at * cores, cores, 0)[:, :exp_dev]
+    slot_weight = jnp.repeat(1.0 / (pair_sums.reshape(pair_exp) / (extent * width)), slots)
     tile = butterfly_sum(tile, "y")
     weight = 1.0 / (tile[:visits, :exp_dev].reshape(exposures) / (extent * width))
     mean_weight = jnp.mean(weight)

time: 198 us -> 194 us (0.980)
  Pallas kernels: 32.7 us -> 48.2 us
  starting transfers between devices: 48.9 us -> 35.1 us
  local copies, waits for them, and re-layouts: 15.6 us -> 9.48 us
  waiting for transfers between devices: 68.5 us -> 64.7 us
  other arithmetic: 27.3 us -> 30.4 us
    ppermute x7 -> x3, waiting for transfers between devices: 41.8 us -> 1.19 us  [butterfly_sum(): x = x + lax.ppermute(x, axis, [(i, i ^ step) for i in range(size)])]
    ppermute x0 -> x6, waiting for transfers between devices: none -> 35.1 us  [ring_sum(): total = total + lax.ppermute(x, axis, pairs)]
    ppermute x7 -> x3, starting transfers between devices: 28.7 us -> 4.96 us  [butterfly_sum(): x = x + lax.ppermute(x, axis, [(i, i ^ step) for i in range(size)])]
    pallas_call x1 -> x2, Pallas kernels: 18.1 us -> 33.7 us  [the longest x1 23.1 us: col_warp(): pl.pallas_call(functools.partial(col_body, cols), out_shape=jax.ShapeDtyp...]
    ppermute x0 -> x6, starting transfers between devices: none -> 9.33 us  [ring_sum(): total = total + lax.ppermute(x, axis, pairs)]
    unnamed x25, local copies, waits for them, and re-layouts: 7.91 us -> 3.22 us
    another operation x1 -> x0, local copies, waits for them, and re-layouts: 2.56 us -> none
    another operation x1 -> x0, other arithmetic: 2.3 us -> none
  transfers between devices with their start and end apart: 11 -> 13, of which waited for: 6 -> 6; matrix products, arithmetic and copies ran while one was open for 15% -> 19% of each run, Pallas kernels for 14% -> 17%
where the time goes in v4:
time: 194 us; the launch traced here: 191 us
  waiting for transfers between devices  64.7 us (33%)
  Pallas kernels  48.2 us (25%)
  starting transfers between devices  35.1 us (18%)
  other arithmetic  30.4 us (16%)
  local copies, waits for them, and re-layouts  9.48 us (5%)
    ppermute x6, waiting for transfers between devices, ring_sum(): total = total + lax.ppermute(x, axis, pairs)  35.1 us
    all_to_all x3, waiting for transfers between devices, exchange(): return lax.all_to_all(x, axis, split_axis=0, concat_axis=0, tiled=True)  28.3 us
    pallas_call x1, Pallas kernels, col_warp(): pl.pallas_call(functools.partial(col_body, cols), out_shape=jax.ShapeDtyp...  23.1 us
    all_to_all x3, starting transfers between devices, exchange(): return lax.all_to_all(x, axis, split_axis=0, concat_axis=0, tiled=True)  20.8 us
    pallas_call x1, Pallas kernels, split_columns(): pl.pallas_call(split_body, out_shape=jax.ShapeDtypeStruct((exposures * pa...  10.6 us
    add x1, other arithmetic, coverage(): running = running + jnp.where(inside, tap, 0.0)  10.2 us
    ppermute x6, starting transfers between devices, ring_sum(): total = total + lax.ppermute(x, axis, pairs)  9.33 us
    pallas_call x1, Pallas kernels, prepare(): pl.pallas_call(functools.partial(prepare_body, extent), out_shape=(jax.Sh...  8.32 us
  transfers between devices with their start and end apart: 13, of which 6 were waited for; matrix products, arithmetic and copies ran while one was open for 19% of the time, Pallas kernels for 17%

profile of v4, /device:TPU:4, one launch (start us, length us, event | category | flops | bytes accessed | tf_op | source)
XLA Modules:
  0.0 190.5 jit_solution(10038524341575042001)
XLA Ops:
  0.6 10.6 %split_columns.1 = bf16[16,256,512]{2,1,0:T(8,128)(2,1)} custom-call(bf16[4,256,2048]{2,1,0:T(8,128)(2,1)} %image_ref.1), custom_call_target="tpu_custom_call" | custom-call | tf_op jit(solution)/shard_map/split_columns/pallas_call | solution.py:373
  11.9 2.0 %collective-permute-start = (f32[8,128]{1,0:T(8,128)S(1)}, f32[8,128]{1,0:T(8,128)S(1)}, u32[]{:S(2)}, u32[]{:S(2)}) collective-permute-start(f32[8,128]{1,0:T(8,128)S(1)} %scatter.12), channel_id=1, source_target_pairs={{0,1},{1,2},{2,3},{3,0},{4,5},{5,6},{6,7},{7,4},{8,9},{9,10},{10,1... | collective-permute-start | bytes 12296 | tf_op jit(solution)/shard_map/ppermute | solution.py:394
  13.9 3.6 %collective-permute-start.1 = (f32[8,128]{1,0:T(8,128)S(1)}, f32[8,128]{1,0:T(8,128)S(1)}, u32[]{:S(2)}, u32[]{:S(2)}) collective-permute-start(f32[8,128]{1,0:T(8,128)S(1)} %scatter.12), channel_id=1, source_target_pairs={{0,2},{1,3},{2,0},{3,1},{4,6},{5,7},{6,4},{7,5},{8,10},{9,11},{10,... | collective-permute-start | bytes 12296 | tf_op jit(solution)/shard_map/ppermute | solution.py:394
  17.5 1.0 collective-permute-start.2
  19.0 5.3 %all-to-all-start = ((bf16[16,256,512]{2,1,0:T(8,128)(2,1)}), bf16[16,256,512]{2,1,0:T(8,128)(2,1)}, u32[]{:S(2)}, u32[]{:S(2)}) async-start(bf16[16,256,512]{2,1,0:T(8,128)(2,1)} %split_columns.1), calls=%async_computation | async-start | bytes 8388608 | tf_op jit(solution)/shard_map/all_to_all | solution.py:425
  25.9 1.0 constant_dynamic-slice_fusion
  26.9 1.0 constant_dynamic-slice_fusion.5
  31.1 1.6 and_subtract_fusion.key_hbm
  32.7 2.1 %divide_reduce-precision_fusion.5 = (f32[16,32,128]{2,1,0:T(8,128)S(1)}, f32[16,32,128]{2,1,0:T(8,128)S(1)}) fusion(f32[16,32,128]{2,1,0:T(8,128)S(1)} %reshape.619), kind=kLoop, calls=%fused_computation.61 | loop fusion | flops 2555904 | bytes 786432 | tf_op jit(solution)/shard_map/reduce_precision | solution.py:61
  34.9 2.9 %divide_reduce-precision_fusion.4 = (f32[16,32,128]{2,1,0:T(8,128)S(1)}, f32[16,32,128]{2,1,0:T(8,128)}, f32[16,32,128]{2,1,0:T(8,128)}, f32[16,32,128]{2,1,0:T(8,128)}, f32[16,32,128]{2,1,0:T(8,128)}) fusion(f32[16,32,128]{2,1,0:T(8,128)S(1)} %get-tuple-element.57, f32[16,32,128]{2,1,0:T(8,128)S(1)} %reshape.619), kind=kLoop, calls=%fused_computation.60 | loop fusion | flops 2424832 | bytes 1835008 | tf_op jit(solution)/shard_map/reduce_precision | solution.py:61
  38.1 8.3 %prepare.1 = (bf16[16,256,256]{2,1,0:T(8,128)(2,1)S(1)}, bf16[512,288]{1,0:T(8,128)(2,1)S(1)}, bf16[8,2,288,256]{3,2,1,0:T(8,128)(2,1)S(1)}) custom-call(f32[1,21]{1,0:T(1,128)S(1)} %constant_dynamic-slice_fusion.4.row_kernel_ref, f32[8,21]{1,0:T(8,128)S(1)} %pad_maximum_fusion.kernel_ref, s32[16]{0:T(128)S(1)} %get-tuple-element.59.low_ref, ...), custom_call_target="tpu_custom_call" | custom-call | flops 4000000000 | bytes 8388608 | tf_op jit(solution)/shard_map/prepare/pallas_call | solution.py:156
  46.4 1.5 copy-done
  47.9 1.2 collective-permute-start.4
  49.1 0.9 collective-permute-start.5
  50.7 27.9 %collective-permute-done.4 = f32[8,128]{1,0:T(8,128)S(1)} collective-permute-done((f32[8,128]{1,0:T(8,128)S(1)}, f32[8,128]{1,0:T(8,128)S(1)}, u32[]{:S(2)}, u32[]{:S(2)}) %collective-permute-start.4) | collective-permute-done | bytes 4128 | tf_op jit(solution)/shard_map/ppermute | solution.py:394
  78.6 0.9 collective-permute-done.5
  79.4 6.4 %collective-permute-done.6 = f32[8,128]{1,0:T(8,128)S(1)} collective-permute-done((f32[8,128]{1,0:T(8,128)S(1)}, f32[8,128]{1,0:T(8,128)S(1)}, u32[]{:S(2)}, u32[]{:S(2)}) %collective-permute-start.6) | collective-permute-done | bytes 4128 | tf_op jit(solution)/shard_map/ppermute | solution.py:394
  85.8 6.2 %row_warp.1 = bf16[32,2,32,512]{3,2,1,0:T(8,128)(2,1)} custom-call(s32[16]{0:T(128)S(1)} %get-tuple-element.59.low_ref, s32[16]{0:T(128)S(1)} %get-tuple-element.58.num_ref, bf16[4096,512]{1,0:T(8,128)(2,1)} %bitcast.4.x_ref, bf16[16,256,256]{2,1,0:T(8,128)(2,1)S(1)} %get-tuple-element.43.rows_ref, bf16[512,288]{1,0:T(8,128)(2,1)S(1)} %get-tuple-element.44.blur_ref, ...), custom_call_target="tpu_custom_call" | custom-call | flops 2000000000 | bytes 8388608 | tf_op jit(solution)/shard_map/row_warp/pallas_call | solution.py:209
  92.1 7.6 %all-to-all-start.1 = ((bf16[32,2,32,512]{3,2,1,0:T(8,128)(2,1)}), bf16[32,2,32,512]{3,2,1,0:T(8,128)(2,1)S(1)}, u32[]{:S(2)}, u32[]{:S(2)}) async-start(bf16[32,2,32,512]{3,2,1,0:T(8,128)(2,1)} %row_warp.1), calls=%async_computation.1 | async-start | bytes 4194304 | tf_op jit(solution)/shard_map/all_to_all | solution.py:425
  100.3 3.5 %select_add_fusion.turned_hbm = f32[16,32,8,128]{3,2,1,0:T(8,128)} fusion(f32[16,32,128]{2,1,0:T(8,128)} %get-tuple-element.66, f32[16,32,128]{2,1,0:T(8,128)S(1)} %copy-done.4, f32[16,32,128]{2,1,0:T(8,128)S(1)} %copy-done.5, f32[16,32,128]{2,1,0:T(8,128)} %get-tuple-element.65, f32[16,32,128]{2,1,0:T(8,128)S(1)} %get-tuple-element.62, ...), kind=kLoop, calls=%fused_computation.9 | loop fusion | flops 9961472 | bytes 3932160 | tf_op jit(solution)/shard_map/add | solution.py:79
  105.4 1.6 collective-permute-start.8
  107.9 1.2 collective-permute-done.8
  109.1 3.2 %collective-permute-start.9 = (f32[8,128]{1,0:T(8,128)S(1)}, f32[8,128]{1,0:T(8,128)S(1)}, u32[]{:S(2)}, u32[]{:S(2)}) collective-permute-start(f32[8,128]{1,0:T(8,128)S(1)} %fusion.64), channel_id=1, source_target_pairs={{0,64},{32,96},{64,0},{96,32},{1,65},{33,97},{65,1},{97,33},{2,66}... | collective-permute-start | bytes 12296 | tf_op jit(solution)/shard_map/ppermute | solution.py:402
  112.3 15.5 %all-to-all-done.1.z_hbm = bf16[32,2,32,512]{3,2,1,0:T(8,128)(2,1)S(1)} async-done(((bf16[32,2,32,512]{3,2,1,0:T(8,128)(2,1)}), bf16[32,2,32,512]{3,2,1,0:T(8,128)(2,1)S(1)}, u32[]{:S(2)}, u32[]{:S(2)}) %all-to-all-start.1) | async-done | bytes 2097184 | tf_op jit(solution)/shard_map/all_to_all | solution.py:425
  127.9 1.3 copy-done.3
  129.2 23.1 %col_warp.1 = bf16[8,16,32,256]{3,2,1,0:T(8,128)(2,1)} custom-call(s32[8]{0:T(128)} %fusion.58.count_ref, s32[8,16]{1,0:T(8,128)} %select_reduce_fusion.list_ref, s32[16,32]{1,0:T(8,128)} %fusion.47.low_ref, s32[16,4]{1,0:T(8,128)} %copy.48.most_ref, s32[16]{0:T(128)} %get-tuple-element.53.from_ref, s32[16]{0:T(128)} %get-tuple-element.52.to_ref, ...), custom_call_target="tpu_custom_call" | custom-call | flops 8000000000 | bytes 16777216 | tf_op jit(solution)/shard_map/col_warp/pallas_call | solution.py:339
  152.3 7.8 %all-to-all-start.2 = ((bf16[128,32,256]{2,1,0:T(8,128)(2,1)}), bf16[128,32,256]{2,1,0:T(8,128)(2,1)S(1)}, u32[]{:S(2)}, u32[]{:S(2)}) async-start(bf16[128,32,256]{2,1,0:T(8,128)(2,1)} %bitcast.57), calls=%async_computation.2 | async-start | bytes 4194304 | tf_op jit(solution)/shard_map/all_to_all | solution.py:425
  160.2 10.2 %fusion.12 = f32[32,2,1024]{2,1,0:T(2,128)S(1)} fusion(s32[32,2,1024]{2,1,0:T(2,128)S(1)} %copy-done.6, f32[32,2,1024]{2,1,0:T(2,128)S(1)} %copy-done.7), kind=kLoop, calls=%fused_computation.37 | loop fusion | flops 5636096 | bytes 786432 | tf_op jit(solution)/shard_map/add | solution.py:69
  171.8 3.4 %fusion.31 = f32[32,2,256]{2,1,0:T(2,128)S(1)} fusion(f32[32,2,4096]{2,1,0:T(2,128)} %param.20, s32[]{:T(128)S(6)} %select_n.331, s32[32,2,4096]{2,1,0:T(2,128)} %param.19, f32[32,2]{1,0:T(8,128)S(1)} %copy.49), kind=kLoop, calls=%fused_computation.119 | loop fusion | flops 1425408 | bytes 196868 | tf_op jit(solution)/shard_map/mul | solution.py:532
  175.2 1.0 fusion.13
  176.2 12.8 %all-to-all-done.2 = bf16[128,32,256]{2,1,0:T(8,128)(2,1)S(1)} async-done(((bf16[128,32,256]{2,1,0:T(8,128)(2,1)}), bf16[128,32,256]{2,1,0:T(8,128)(2,1)S(1)}, u32[]{:S(2)}, u32[]{:S(2)}) %all-to-all-start.2) | async-done | bytes 2097184 | tf_op jit(solution)/shard_map/all_to_all | solution.py:425
  189.4 1.2 fusion.1
  (93 shorter events, 11.3 us)
Async XLA Ops:
  0.6 10.6 %copy-start.1 = (bf16[4,256,2048]{2,1,0:T(8,128)(2,1)S(1)}, bf16[4,256,2048]{2,1,0:T(8,128)(2,1)}, u32[]{:S(2)}) copy-start(bf16[4,256,2048]{2,1,0:T(8,128)(2,1)} %param.14) | copy-start | bytes 12582916
  11.2 7.3 %copy-start.9 = (f32[4,3]{1,0:T(4,128)S(1)}, f32[4,3]{1,0:T(4,128)}, u32[]{:S(2)}) copy-start(f32[4,3]{1,0:T(4,128)} %param.15) | copy-start | bytes 148
  11.2 7.4 %copy-start.10 = (f32[3]{0:T(128)S(1)}, f32[3]{0:T(128)}, u32[]{:S(2)}) copy-start(f32[3]{0:T(128)} %constant.259) | copy-start | bytes 40
  11.9 25.8 %collective-permute-start = (f32[8,128]{1,0:T(8,128)S(1)}, f32[8,128]{1,0:T(8,128)S(1)}, u32[]{:S(2)}, u32[]{:S(2)}) collective-permute-start(f32[8,128]{1,0:T(8,128)S(1)} %scatter.12), channel_id=1, source_target_pairs={{0,1},{1,2},{2,3},{3,0},{4,5},{5,6},{6,7},{7,4},{8,9},{9,10},{10,1... | collective-permute-start | bytes 12296 | tf_op jit(solution)/shard_map/ppermute | solution.py:394
  13.9 24.2 %collective-permute-start.1 = (f32[8,128]{1,0:T(8,128)S(1)}, f32[8,128]{1,0:T(8,128)S(1)}, u32[]{:S(2)}, u32[]{:S(2)}) collective-permute-start(f32[8,128]{1,0:T(8,128)S(1)} %scatter.12), channel_id=1, source_target_pairs={{0,2},{1,3},{2,0},{3,1},{4,6},{5,7},{6,4},{7,5},{8,10},{9,11},{10,... | collective-permute-start | bytes 12296 | tf_op jit(solution)/shard_map/ppermute | solution.py:394
  17.5 20.6 %collective-permute-start.2 = (f32[8,128]{1,0:T(8,128)S(1)}, f32[8,128]{1,0:T(8,128)S(1)}, u32[]{:S(2)}, u32[]{:S(2)}) collective-permute-start(f32[8,128]{1,0:T(8,128)S(1)} %scatter.12), channel_id=1, source_target_pairs={{0,3},{1,0},{2,1},{3,2},{4,7},{5,4},{6,5},{7,6},{8,11},{9,8},{10,9... | collective-permute-start | bytes 12296 | tf_op jit(solution)/shard_map/ppermute | solution.py:394
  18.9 18.8 %collective-permute-start.3 = (f32[8,128]{1,0:T(8,128)S(1)}, f32[8,128]{1,0:T(8,128)S(1)}, u32[]{:S(2)}, u32[]{:S(2)}) collective-permute-start(f32[8,128]{1,0:T(8,128)S(1)} %scatter.14), channel_id=1, source_target_pairs={{0,16},{16,0},{1,17},{17,1},{2,18},{18,2},{3,19},{19,3},{4,20},{20... | collective-permute-start | bytes 12296 | tf_op jit(solution)/shard_map/ppermute | solution.py:432
  19.0 66.9 %all-to-all-start = ((bf16[16,256,512]{2,1,0:T(8,128)(2,1)}), bf16[16,256,512]{2,1,0:T(8,128)(2,1)}, u32[]{:S(2)}, u32[]{:S(2)}) async-start(bf16[16,256,512]{2,1,0:T(8,128)(2,1)} %split_columns.1), calls=%async_computation | async-start | bytes 8388608 | tf_op jit(solution)/shard_map/all_to_all | solution.py:425
  24.3 4.5 %copy-start.8 = (s32[32,2]{0,1:T(2,128)S(1)}, s32[32,2]{0,1:T(2,128)}, u32[]{:S(2)}) copy-start(s32[32,2]{0,1:T(2,128)} %param.16) | copy-start | bytes 772
  46.4 1.5 copy-start
  47.9 30.7 %collective-permute-start.4 = (f32[8,128]{1,0:T(8,128)S(1)}, f32[8,128]{1,0:T(8,128)S(1)}, u32[]{:S(2)}, u32[]{:S(2)}) collective-permute-start(f32[8,128]{1,0:T(8,128)S(1)} %add_add_fusion.1), channel_id=1, source_target_pairs={{0,4},{1,5},{2,6},{3,7},{4,8},{5,9},{6,10},{7,11},{8,12},{9,13},{1... | collective-permute-start | bytes 12296 | tf_op jit(solution)/shard_map/ppermute | solution.py:394
  49.1 30.4 %collective-permute-start.5 = (f32[8,128]{1,0:T(8,128)S(1)}, f32[8,128]{1,0:T(8,128)S(1)}, u32[]{:S(2)}, u32[]{:S(2)}) collective-permute-start(f32[8,128]{1,0:T(8,128)S(1)} %add_add_fusion.1), channel_id=1, source_target_pairs={{0,8},{1,9},{2,10},{3,11},{4,12},{5,13},{6,14},{7,15},{8,0},{9,1},... | collective-permute-start | bytes 12296 | tf_op jit(solution)/shard_map/ppermute | solution.py:394
  49.9 35.9 %collective-permute-start.6 = (f32[8,128]{1,0:T(8,128)S(1)}, f32[8,128]{1,0:T(8,128)S(1)}, u32[]{:S(2)}, u32[]{:S(2)}) collective-permute-start(f32[8,128]{1,0:T(8,128)S(1)} %add_add_fusion.1), channel_id=1, source_target_pairs={{0,12},{1,13},{2,14},{3,15},{4,0},{5,1},{6,2},{7,3},{8,4},{9,5},{1... | collective-permute-start | bytes 12296 | tf_op jit(solution)/shard_map/ppermute | solution.py:394
  92.1 8.3 %copy-start.4 = (f32[16,32,128]{2,1,0:T(8,128)S(1)}, f32[16,32,128]{2,1,0:T(8,128)}, u32[]{:S(2)}) copy-start(f32[16,32,128]{2,1,0:T(8,128)} %get-tuple-element.63) | copy-start | bytes 786436
  92.1 8.3 %copy-start.5 = (f32[16,32,128]{2,1,0:T(8,128)S(1)}, f32[16,32,128]{2,1,0:T(8,128)}, u32[]{:S(2)}) copy-start(f32[16,32,128]{2,1,0:T(8,128)} %get-tuple-element.64) | copy-start | bytes 786436
  92.1 35.8 %all-to-all-start.1 = ((bf16[32,2,32,512]{3,2,1,0:T(8,128)(2,1)}), bf16[32,2,32,512]{3,2,1,0:T(8,128)(2,1)S(1)}, u32[]{:S(2)}, u32[]{:S(2)}) async-start(bf16[32,2,32,512]{3,2,1,0:T(8,128)(2,1)} %row_warp.1), calls=%async_computation.1 | async-start | bytes 4194304 | tf_op jit(solution)/shard_map/all_to_all | solution.py:425
  103.9 1.5 collective-permute-start.7
  105.4 3.6 %collective-permute-start.8 = (f32[8,128]{1,0:T(8,128)S(1)}, f32[8,128]{1,0:T(8,128)S(1)}, u32[]{:S(2)}, u32[]{:S(2)}) collective-permute-start(f32[8,128]{1,0:T(8,128)S(1)} %fusion.59), channel_id=1, source_target_pairs={{0,32},{32,0},{64,96},{96,64},{1,33},{33,1},{65,97},{97,65},{2,34}... | collective-permute-start | bytes 12296 | tf_op jit(solution)/shard_map/ppermute | solution.py:402
  109.1 61.2 %collective-permute-start.9 = (f32[8,128]{1,0:T(8,128)S(1)}, f32[8,128]{1,0:T(8,128)S(1)}, u32[]{:S(2)}, u32[]{:S(2)}) collective-permute-start(f32[8,128]{1,0:T(8,128)S(1)} %fusion.64), channel_id=1, source_target_pairs={{0,64},{32,96},{64,0},{96,32},{1,65},{33,97},{65,1},{97,33},{2,66}... | collective-permute-start | bytes 12296 | tf_op jit(solution)/shard_map/ppermute | solution.py:402
  127.9 1.3 copy-start.3
  152.3 7.9 %copy-start.6 = (s32[32,2,1024]{2,1,0:T(2,128)S(1)}, s32[32,2,1024]{2,1,0:T(2,128)}, u32[]{:S(2)}) copy-start(s32[32,2,1024]{2,1,0:T(2,128)} %param.17) | copy-start | bytes 786436
  152.3 7.9 %copy-start.7 = (f32[32,2,1024]{2,1,0:T(2,128)S(1)}, f32[32,2,1024]{2,1,0:T(2,128)}, u32[]{:S(2)}) copy-start(f32[32,2,1024]{2,1,0:T(2,128)} %param.18) | copy-start | bytes 786436
  152.3 36.7 %all-to-all-start.2 = ((bf16[128,32,256]{2,1,0:T(8,128)(2,1)}), bf16[128,32,256]{2,1,0:T(8,128)(2,1)S(1)}, u32[]{:S(2)}, u32[]{:S(2)}) async-start(bf16[128,32,256]{2,1,0:T(8,128)(2,1)} %bitcast.57), calls=%async_computation.2 | async-start | bytes 4194304 | tf_op jit(solution)/shard_map/all_to_all | solution.py:425
  176.2 14.3 %copy-start.2 = (f32[1024,256,1]{1,0,2:T(8,128)}, f32[1024,256,1]{1,0,2:T(8,128)S(1)}, u32[]{:S(2)}) copy-start(f32[1024,256,1]{1,0,2:T(8,128)S(1)} %fusion.13) | copy-start | bytes 3145732

commit v5 on v4

--- a/solution.py
+++ b/solution.py
@@ -20,12 +20,12 @@
 ROW_SPAN = 288
 COL_BLOCK = 128
 COL_STEP = 256
-COL_GROUP = 8
+COL_GROUP = 9
 BLUR_BLOCK = 256
 BLUR_STEP = 512
 BLUR_BAND = (112, 400)
 LANES = 128
-LIMIT = 28 * 1024 * 1024
+LIMIT = 14 * 1024 * 1024
 COL_LIMIT = 56 * 1024 * 1024
 
 
@@ -126,9 +126,8 @@
     return jnp.concatenate(two_parts(both.T), axis=0)
 
 
-def prepare_body(extent, row_kernel_ref, kernel_ref, low_ref, turned_ref, key_ref, rows_ref,
-                 blur_ref, cols_ref):
-    high, rest = two_parts(toeplitz(row_kernel_ref, 0, ROW_STEP, ROW_SPAN, 16 + RADIUS))
+def row_matrices_body(extent, kernel_ref, low_ref, turned_ref, key_ref, rows_ref, blur_ref):
+    high, rest = two_parts(toeplitz(kernel_ref, 0, ROW_STEP, ROW_SPAN, 16 + RADIUS))
     blur_ref[0:ROW_STEP] = high
     blur_ref[ROW_STEP : 2 * ROW_STEP] = rest
 
@@ -139,6 +138,26 @@
         return carry
 
     lax.fori_loop(0, turned_ref.shape[0], block, 0)
+
+
+def make_row_matrices(kernel, low, turned, key, extent):
+    blocks = turned.shape[0]
+    vmem = pl.BlockSpec(memory_space=pltpu.VMEM)
+    smem = pl.BlockSpec(memory_space=pltpu.SMEM)
+    return pl.pallas_call(
+        functools.partial(row_matrices_body, extent),
+        out_shape=(
+            jax.ShapeDtypeStruct((blocks, 2 * ROW_BLOCK, ROW_STEP), BF16),
+            jax.ShapeDtypeStruct((2 * ROW_STEP, ROW_SPAN), BF16),
+        ),
+        in_specs=[smem, smem, vmem, vmem],
+        out_specs=(vmem, vmem),
+        compiler_params=pltpu.CompilerParams(vmem_limit_bytes=LIMIT),
+        name="row_matrices",
+    )(kernel, low, turned, key)
+
+
+def col_matrices_body(kernel_ref, cols_ref):
     begin, end = BLUR_BAND
     for e in range(cols_ref.shape[0]):
         high, rest = two_parts(
@@ -148,26 +167,17 @@
         cols_ref[e, 1] = rest
 
 
-def prepare(row_kernel, kernels, low, turned, key, extent):
-    exposures = kernels.shape[0]
-    blocks = turned.shape[0]
-    vmem = pl.BlockSpec(memory_space=pltpu.VMEM)
-    smem = pl.BlockSpec(memory_space=pltpu.SMEM)
+def make_col_matrices(kernels):
     return pl.pallas_call(
-        functools.partial(prepare_body, extent),
-        out_shape=(
-            jax.ShapeDtypeStruct((blocks, 2 * ROW_BLOCK, ROW_STEP), BF16),
-            jax.ShapeDtypeStruct((2 * ROW_STEP, ROW_SPAN), BF16),
-            jax.ShapeDtypeStruct((exposures, 2, BLUR_BAND[1] - BLUR_BAND[0], BLUR_BLOCK), BF16),
+        col_matrices_body,
+        out_shape=jax.ShapeDtypeStruct(
+            (kernels.shape[0], 2, BLUR_BAND[1] - BLUR_BAND[0], BLUR_BLOCK), BF16
         ),
-        in_specs=[smem, smem, smem, vmem, vmem],
-        out_specs=(vmem, vmem, vmem),
-        compiler_params=pltpu.CompilerParams(vmem_limit_bytes=LIMIT),
-        cost_estimate=pl.CostEstimate(
-            flops=4_000_000_000, bytes_accessed=8 * 1024 * 1024, transcendentals=0
-        ),
-        name="prepare",
-    )(row_kernel, kernels, low, turned, key)
+        in_specs=[pl.BlockSpec(memory_space=pltpu.SMEM)],
+        out_specs=pl.BlockSpec(memory_space=pltpu.VMEM),
+        compiler_params=pltpu.CompilerParams(vmem_limit_bytes=COL_LIMIT),
+        name="col_matrices",
+    )(kernels)
 
 
 def row_body(slots, low_ref, num_ref, x_ref, rows_ref, blur_ref, turned_ref, key_ref, out_ref):
@@ -219,7 +229,7 @@
     )(low, num, x, matrices, blur, turned, key)
 
 
-def col_body(cols, count_ref, list_ref, low_ref, most_ref, from_ref, to_ref, weight_ref, z_hbm,
+def col_body(cols, count_ref, list_ref, low_ref, num_ref, from_ref, to_ref, weight_ref, z_hbm,
              blur_hbm, turned_hbm, key_hbm, out_ref, padded, blur, turned_ref, key_ref, blurred,
              held, z_sems, blur_sems, table_sems):
     slots, rows, width = z_hbm.shape[1:]
@@ -232,26 +242,19 @@
     def _():
         waits = []
         for e in range(exposures):
-            copies = []
-            for s in range(sources):
-                for j in range(slots):
-                    copies.append(
-                        pltpu.make_async_copy(
-                            z_hbm.at[e * sources + s, j],
-                            padded.at[
-                                e, pl.ds(j * rows, rows), pl.ds(LANES + s * width, width)
-                            ],
-                            z_sems.at[e, s, j],
-                        )
-                    )
-            for n in range(2):
-                copies.append(
-                    pltpu.make_async_copy(
-                        blur_hbm.at[e, n],
-                        blur.at[e, n, pl.ds(begin, end - begin)],
-                        blur_sems.at[e, n],
-                    )
+            copies = [
+                pltpu.make_async_copy(
+                    z_hbm.at[e * sources + s],
+                    padded.at[e, :, :, pl.ds(LANES + s * width, width)],
+                    z_sems.at[e, s],
                 )
+                for s in range(sources)
+            ]
+            copies.append(
+                pltpu.make_async_copy(
+                    blur_hbm.at[e], blur.at[e, :, pl.ds(begin, end - begin)], blur_sems.at[e]
+                )
+            )
             for copy in copies:
                 copy.start()
             waits.append(copies)
@@ -261,10 +264,10 @@
         ]
         for copy in tables:
             copy.start()
-        pad = jnp.zeros((slots * rows, LANES), BF16)
+        pad = jnp.zeros((slots, rows, LANES), BF16)
         for e in range(exposures):
-            padded[e, :, 0:LANES] = pad
-            padded[e, :, LANES + cols : 2 * LANES + cols] = pad
+            padded[e, :, :, 0:LANES] = pad
+            padded[e, :, :, LANES + cols : 2 * LANES + cols] = pad
             for n in range(2):
                 blur[e, n, 0:begin] = jnp.zeros((begin, BLUR_BLOCK), BF16)
                 blur[e, n, end:BLUR_STEP] = jnp.zeros((BLUR_STEP - end, BLUR_BLOCK), BF16)
@@ -277,7 +280,9 @@
                 copy.wait()
             windows = jnp.concatenate(
                 [
-                    padded[e, :, b * BLUR_BLOCK : b * BLUR_BLOCK + BLUR_STEP]
+                    padded[e, :, :, b * BLUR_BLOCK : b * BLUR_BLOCK + BLUR_STEP].reshape(
+                        slots * rows, BLUR_STEP
+                    )
                     for b in range(cols // BLUR_BLOCK)
                 ],
                 axis=0,
@@ -294,42 +299,51 @@
 
     held[...] = jnp.zeros(held.shape, F32)
 
+    blocks = turned_ref.shape[1]
+
     def part(slot, b, n):
         first = pl.multiple_of(jnp.minimum(low_ref[slot, b] + n * COL_STEP, cols), LANES)
         band = band_of(turned_ref[slot, b], key_ref[slot, b], first, COL_STEP // 8)
         band = jnp.concatenate(band, axis=0).astype(BF16)
         return halves_sum(dot(blurred[slot, :, pl.ds(first, COL_STEP)], band))
 
-    per_owner = held.shape[2] // COL_BLOCK
-
     def add_slot(i, carry):
         slot = list_ref[patch, i]
-        weight = weight_ref[slot]
+        begin, end = from_ref[slot], to_ref[slot]
 
         def add_group(c, carry):
+            at = begin + c * COL_GROUP
+            spots = [jnp.minimum(at + h, blocks - 1) for h in range(COL_GROUP)]
+            weights = [jnp.where(at + h < end, weight_ref[slot], 0.0) for h in range(COL_GROUP)]
+
             def add_parts(n):
-                sums = [part(slot, c * COL_GROUP + h, n) for h in range(COL_GROUP)]
-                for h, total in enumerate(sums):
-                    owner = c * (COL_GROUP // per_owner) + h // per_owner
-                    span = slice((h % per_owner) * COL_BLOCK, (h % per_owner + 1) * COL_BLOCK)
-                    held[owner, :, span] += weight * total
+                sums = [part(slot, b, n) for b in spots]
+                for b, weight, total in zip(spots, weights, sums):
+                    span = pl.ds(pl.multiple_of(b * COL_BLOCK, COL_BLOCK), COL_BLOCK)
+                    held[:, span] += weight * total
 
             add_parts(0)
+            most = num_ref[slot, spots[0]]
+            for b in spots[1:]:
+                most = jnp.maximum(most, num_ref[slot, b])
 
             def more(n, carry):
                 add_parts(n)
                 return carry
 
-            lax.fori_loop(1, most_ref[slot, c], more, 0)
+            lax.fori_loop(1, most, more, 0)
             return carry
 
-        return lax.fori_loop(from_ref[slot], to_ref[slot], add_group, carry)
+        steps = (end - begin + COL_GROUP - 1) // COL_GROUP
+        return lax.fori_loop(0, steps, add_group, carry)
 
     lax.fori_loop(0, count_ref[patch], add_slot, 0)
-    out_ref[0] = held[...].astype(out_ref.dtype)
-
-
-def col_warp(z, count, listed, low, most, begin, end, weight, blur, turned, key, cols, patches,
+    own_cols = out_ref.shape[3]
+    for owner in range(out_ref.shape[1]):
+        out_ref[0, owner] = held[:, owner * own_cols : (owner + 1) * own_cols].astype(BF16)
+
+
+def col_warp(z, count, listed, low, num, begin, end, weight, blur, turned, key, cols, patches,
              owners):
     slots, rows, width = z.shape[1:]
     slot_total, blocks = turned.shape[:2]
@@ -343,14 +357,14 @@
         in_specs=[smem] * 7 + [pl.BlockSpec(memory_space=pl.ANY)] * 4,
         out_specs=pl.BlockSpec((1, owners, rows, own_cols), lambda k: (k, 0, 0, 0)),
         scratch_shapes=[
-            pltpu.VMEM((exposures, slots * rows, cols + 2 * LANES), BF16),
+            pltpu.VMEM((exposures, slots, rows, cols + 2 * LANES), BF16),
             pltpu.VMEM((exposures, 2, BLUR_STEP, BLUR_BLOCK), BF16),
             pltpu.VMEM(turned.shape, F32),
             pltpu.VMEM(key.shape, jnp.int32),
             pltpu.VMEM((slot_total, 2 * rows, cols + COL_STEP), BF16),
-            pltpu.VMEM((owners, rows, own_cols), F32),
-            pltpu.SemaphoreType.DMA((exposures, cols // width, slots)),
-            pltpu.SemaphoreType.DMA((exposures, 2)),
+            pltpu.VMEM((rows, owners * own_cols), F32),
+            pltpu.SemaphoreType.DMA((exposures, cols // width)),
+            pltpu.SemaphoreType.DMA((exposures,)),
             pltpu.SemaphoreType.DMA((2,)),
         ],
         compiler_params=pltpu.CompilerParams(
@@ -360,25 +374,35 @@
             flops=8_000_000_000, bytes_accessed=16 * 1024 * 1024, transcendentals=0
         ),
         name="col_warp",
-    )(count, listed, low, most, begin, end, weight, z, blur, turned, key)
-
-
-def split_body(image_ref, out_ref):
-    out_ref[...] = image_ref[...]
+    )(count, listed, low, num, begin, end, weight, z, blur, turned, key)
+
+
+def split_body(parts, image_ref, out_ref, sems):
+    width = out_ref.shape[2]
+    copies = [
+        pltpu.make_async_copy(
+            image_ref.at[at // parts, :, pl.ds(at % parts * width, width)],
+            out_ref.at[at],
+            sems.at[at],
+        )
+        for at in range(out_ref.shape[0])
+    ]
+    for copy in copies:
+        copy.start()
+    for copy in copies:
+        copy.wait()
 
 
 def split_columns(image, parts):
     exposures, height, width = image.shape
-    block = (1, height, width // parts)
+    total = exposures * parts
     return pl.pallas_call(
-        split_body,
-        out_shape=jax.ShapeDtypeStruct((exposures * parts,) + block[1:], image.dtype),
-        grid=(exposures * parts,),
-        in_specs=[pl.BlockSpec(block, lambda i: (i // parts, 0, i % parts))],
-        out_specs=pl.BlockSpec(block, lambda i: (i, 0, 0)),
-        compiler_params=pltpu.CompilerParams(
-            dimension_semantics=("arbitrary",), vmem_limit_bytes=COL_LIMIT
-        ),
+        functools.partial(split_body, parts),
+        out_shape=jax.ShapeDtypeStruct((total, height, width // parts), image.dtype),
+        in_specs=[pl.BlockSpec(memory_space=pl.ANY)],
+        out_specs=pl.BlockSpec(memory_space=pltpu.VMEM),
+        scratch_shapes=[pltpu.SemaphoreType.DMA((total,))],
+        compiler_params=pltpu.CompilerParams(vmem_limit_bytes=LIMIT),
         name="split_columns",
     )(image)
 
@@ -424,22 +448,9 @@
     def exchange(x, axis):
         return lax.all_to_all(x, axis, split_axis=0, concat_axis=0, tiled=True)
 
-    sent, variance = lax.optimization_barrier((split_columns(image, parts), variance))
-    columns = exchange(sent, "region").reshape(extent, part_cols)
+    columns = exchange(split_columns(image, parts), "region").reshape(extent, part_cols)
 
     kernels = psf_kernel(psf_coef)
-    tile = jnp.zeros((8, LANES), F32).at[:exp_dev, : 2 * RADIUS + 1].set(kernels)
-    other = lax.ppermute(tile, "core", [(i, i ^ 1) for i in range(cores)])
-    other = other[:exp_dev, : 2 * RADIUS + 1]
-    pair_kernels = jnp.concatenate(
-        [jnp.where(core_at == 0, kernels, other), jnp.where(core_at == 0, other, kernels)]
-    )
-    local_sums = jnp.sum(variance.astype(F32), axis=(1, 2))
-    tile = jnp.zeros((8, LANES), F32).at[0, :exp_dev].set(local_sums)
-    inner = 4
-    tile = ring_sum(tile, "region", inner, 1)
-    pair_exp = cores * exp_dev
-    first_exp = pair_at * pair_exp
 
     own_exp = region_at // parts
     at_exp = visit_at * exp_dev + own_exp
@@ -451,14 +462,31 @@
     row_low = jnp.clip(starts[:, 0] - RADIUS, 0, extent - ROW_STEP) // 16 * 16
     row_end = jnp.minimum(starts[:, -1] + TAPS + RADIUS, extent)
     row_num = jnp.maximum(row_end - row_low + ROW_STEP - 1, 0) // ROW_STEP
-    row_matrices, row_blur, col_blur = prepare(
-        lax.dynamic_slice_in_dim(kernels, own_exp, 1, 0), pair_kernels, row_low, row_turned,
-        row_key, extent,
-    )
-    tile, row_matrices, row_blur, col_blur = lax.optimization_barrier(
-        (tile, row_matrices, row_blur, col_blur)
-    )
+    row_matrices, row_blur = make_row_matrices(
+        lax.dynamic_slice_in_dim(kernels, own_exp, 1, 0), row_low, row_turned, row_key, extent
+    )
+
+    variance, psf_tile, row_matrices = lax.optimization_barrier(
+        (
+            variance,
+            jnp.zeros((8, LANES), F32).at[:exp_dev, : 2 * RADIUS + 1].set(kernels),
+            row_matrices,
+        )
+    )
+    other = lax.ppermute(psf_tile, "core", [(i, i ^ 1) for i in range(cores)])
+    other = other[:exp_dev, : 2 * RADIUS + 1]
+    col_blur = make_col_matrices(
+        jnp.concatenate(
+            [jnp.where(core_at == 0, kernels, other), jnp.where(core_at == 0, other, kernels)]
+        )
+    )
+    local_sums = jnp.sum(variance.astype(F32), axis=(1, 2))
+    tile = jnp.zeros((8, LANES), F32).at[0, :exp_dev].set(local_sums)
+    inner = 4
+    tile = ring_sum(tile, "region", inner, 1)
     tile = ring_sum(tile, "region", regions // inner, inner)
+    pair_exp = cores * exp_dev
+    first_exp = pair_at * pair_exp
 
     slot_total = pair_exp * slots
     col_blocks = patch_cols // COL_BLOCK
@@ -470,10 +498,10 @@
     col_low = jnp.clip(own_starts[:, :, 0], 0, width) // LANES * LANES
     col_end = jnp.minimum(own_starts[:, :, -1] + TAPS, width)
     col_num = jnp.maximum(col_end - col_low + COL_STEP - 1, 0) // COL_STEP
-    col_most = jnp.max(col_num.reshape(slot_total, col_blocks // COL_GROUP, COL_GROUP), axis=2)
-    group_at = jnp.arange(col_blocks // COL_GROUP, dtype=jnp.int32)
-    col_from = jnp.min(jnp.where(col_most > 0, group_at, col_blocks // COL_GROUP), axis=1)
-    col_to = jnp.max(jnp.where(col_most > 0, group_at + 1, 0), axis=1)
+    block_at = jnp.arange(col_blocks, dtype=jnp.int32)
+    col_from = jnp.min(jnp.where(col_num > 0, block_at, col_blocks), axis=1)
+    col_to = jnp.max(jnp.where(col_num > 0, block_at + 1, 0), axis=1)
+    col_from = jnp.minimum(col_from, col_to)
     owners = lax.dynamic_slice_in_dim(correlations, first_exp, pair_exp, 0).reshape(slot_total)
     named = owners == jnp.arange(visits, dtype=jnp.int32)[:, None]
     named = named.astype(jnp.int32)
@@ -500,7 +528,7 @@
     weight = 1.0 / (tile[:visits, :exp_dev].reshape(exposures) / (extent * width))
     mean_weight = jnp.mean(weight)
     partial = col_warp(
-        rows, count, listed, col_low, col_most, col_from, col_to, slot_weight, col_blur,
+        rows, count, listed, col_low, col_num, col_from, col_to, slot_weight, col_blur,
         col_turned, col_key, width, visits, regions,
     )
     pieces = exchange(

time: 194 us -> 187 us (0.964)
  Pallas kernels: 48.2 us -> 36.4 us
  other arithmetic: 30.4 us -> 32.9 us
    pallas_call x2 -> x3, Pallas kernels: 18.9 us -> 10.9 us  [the longest x1 6.56 us: make_row_matrices(): pl.pallas_call(functools.partial(row_matrices_body, extent), out_shape=(j...]
    pallas_call x1, Pallas kernels: 23.1 us -> 19.2 us  [col_warp(): pl.pallas_call(functools.partial(col_body, cols), out_shape=jax.ShapeDtyp...]
    ppermute x6, waiting for transfers between devices: 35.1 us -> 39.1 us  [ring_sum(): total = total + lax.ppermute(x, axis, pairs)]
    reduce_sum x1, other arithmetic: 0.7 us -> 3.04 us  [local(): local_sums = jnp.sum(variance.astype(F32), axis=(1, 2))]
    all_to_all x3, waiting for transfers between devices: 28.3 us -> 26.3 us  [exchange(): return lax.all_to_all(x, axis, split_axis=0, concat_axis=0, tiled=True)]
    unnamed x25 -> x19, local copies, waits for them, and re-layouts: 3.22 us -> 4.51 us
  transfers between devices with their start and end apart: 13 -> 13, of which waited for: 6 -> 4; matrix products, arithmetic and copies ran while one was open for 19% -> 17% of each run, Pallas kernels for 17% -> 16%
where the time goes in v5:
time: 187 us; the launch traced here: 185 us
  waiting for transfers between devices  66.6 us (36%)
  starting transfers between devices  36.5 us (20%)
  Pallas kernels  36.4 us (19%)
  other arithmetic  32.9 us (18%)
  local copies, waits for them, and re-layouts  9.94 us (5%)
    ppermute x6, waiting for transfers between devices, ring_sum(): total = total + lax.ppermute(x, axis, pairs)  39.1 us
    all_to_all x3, waiting for transfers between devices, exchange(): return lax.all_to_all(x, axis, split_axis=0, concat_axis=0, tiled=True)  26.3 us
    all_to_all x3, starting transfers between devices, exchange(): return lax.all_to_all(x, axis, split_axis=0, concat_axis=0, tiled=True)  22.3 us
    pallas_call x1, Pallas kernels, col_warp(): pl.pallas_call(functools.partial(col_body, cols), out_shape=jax.ShapeDtyp...  19.2 us
    add x1, other arithmetic, coverage(): running = running + jnp.where(inside, tap, 0.0)  10.2 us
    ppermute x6, starting transfers between devices, ring_sum(): total = total + lax.ppermute(x, axis, pairs)  9.25 us
    pallas_call x1, Pallas kernels, make_row_matrices(): pl.pallas_call(functools.partial(row_matrices_body, extent), out_shape=(j...  6.56 us
    pallas_call x1, Pallas kernels, row_warp(): pl.pallas_call(functools.partial(row_body, slots), out_shape=jax.ShapeDty...  6.28 us
  transfers between devices with their start and end apart: 13, of which 4 were waited for; matrix products, arithmetic and copies ran while one was open for 17% of the time, Pallas kernels for 16%

profile of v5, /device:TPU:4, one launch (start us, length us, event | category | flops | bytes accessed | tf_op | source)
XLA Modules:
  0.0 185.1 jit_solution(6875050265723423487)
XLA Ops:
  1.6 0.8 copy.32
  2.4 0.7 multiply_exponential_fusion
  4.4 6.6 %row_matrices.1 = (bf16[16,256,256]{2,1,0:T(8,128)(2,1)S(1)}, bf16[512,288]{1,0:T(8,128)(2,1)S(1)}) custom-call(f32[1,21]{1,0:T(1,128)S(1)} %constant_dynamic-slice_fusion.4.kernel_ref, s32[16]{0:T(128)S(1)} %get-tuple-element.51.low_ref, f32[16,8,128]{2,1,0:T(8,128)S(1)} %select_add_fusion.1.turned_ref, s32[16,8,128]{2,1,0:T(8,128)S(1)} %and_subtract_fusion.1.key_ref), custom_call_target="tpu_custom_call" | custom-call | tf_op jit(solution)/shard_map/row_matrices/pallas_call | solution.py:147
  11.0 3.0 %convert_reduce_fusion = f32[4]{0:T(128)S(1)} fusion(bf16[4,256,2048]{2,1,0:T(8,128)(2,1)} %param.14), kind=kLoop, calls=%fused_computation | loop fusion | flops 4194300 | bytes 4194320 | tf_op jit(solution)/shard_map/reduce_sum | solution.py:483
  14.0 4.1 %collective-permute-start.2 = (f32[8,128]{1,0:T(8,128)S(1)}, f32[8,128]{1,0:T(8,128)S(1)}, u32[]{:S(2)}, u32[]{:S(2)}) collective-permute-start(f32[8,128]{1,0:T(8,128)S(1)} %scatter.13), channel_id=1, source_target_pairs={{0,3},{1,0},{2,1},{3,2},{4,7},{5,4},{6,5},{7,6},{8,11},{9,8},{10,9... | collective-permute-start | bytes 12296 | tf_op jit(solution)/shard_map/ppermute | solution.py:418
  18.1 1.9 %collective-permute-start.1 = (f32[8,128]{1,0:T(8,128)S(1)}, f32[8,128]{1,0:T(8,128)S(1)}, u32[]{:S(2)}, u32[]{:S(2)}) collective-permute-start(f32[8,128]{1,0:T(8,128)S(1)} %scatter.13), channel_id=1, source_target_pairs={{0,2},{1,3},{2,0},{3,1},{4,6},{5,7},{6,4},{7,5},{8,10},{9,11},{10,... | collective-permute-start | bytes 12296 | tf_op jit(solution)/shard_map/ppermute | solution.py:418
  20.5 2.0 %copy-done = bf16[16,256,512]{2,1,0:T(8,128)(2,1)} copy-done((bf16[16,256,512]{2,1,0:T(8,128)(2,1)}, bf16[16,256,512]{2,1,0:T(8,128)(2,1)S(1)}, u32[]{:S(2)}) %copy-start) | copy-done | bytes 4194328
  22.5 6.6 %all-to-all-start = ((bf16[16,256,512]{2,1,0:T(8,128)(2,1)}), bf16[16,256,512]{2,1,0:T(8,128)(2,1)}, u32[]{:S(2)}, u32[]{:S(2)}) async-start(bf16[16,256,512]{2,1,0:T(8,128)(2,1)} %copy-done), calls=%async_computation | async-start | bytes 8388608 | tf_op jit(solution)/shard_map/all_to_all | solution.py:449
  29.3 1.0 constant_dynamic-slice_fusion.5
  31.0 1.0 constant_dynamic-slice_fusion
  33.6 2.1 %divide_reduce-precision_fusion.5 = (f32[16,32,128]{2,1,0:T(8,128)S(1)}, f32[16,32,128]{2,1,0:T(8,128)S(1)}) fusion(f32[16,32,128]{2,1,0:T(8,128)S(1)} %reshape.613), kind=kLoop, calls=%fused_computation.61 | loop fusion | flops 2555904 | bytes 786432 | tf_op jit(solution)/shard_map/reduce_precision | solution.py:61
  35.8 2.1 %divide_reduce-precision_fusion.4 = (f32[16,32,128]{2,1,0:T(8,128)S(1)}, f32[16,32,128]{2,1,0:T(8,128)S(1)}, f32[16,32,128]{2,1,0:T(8,128)S(1)}, f32[16,32,128]{2,1,0:T(8,128)S(1)}, f32[16,32,128]{2,1,0:T(8,128)S(1)}) fusion(f32[16,32,128]{2,1,0:T(8,128)S(1)} %get-tuple-element.49, f32[16,32,128]{2,1,0:T(8,128)S(1)} %reshape.613), kind=kLoop, calls=%fused_computation.60 | loop fusion | flops 2424832 | bytes 1835008 | tf_op jit(solution)/shard_map/reduce_precision | solution.py:61
  37.9 2.6 %select_add_fusion.turned_hbm = f32[16,32,8,128]{3,2,1,0:T(8,128)} fusion(f32[16,32,128]{2,1,0:T(8,128)S(1)} %get-tuple-element.60, f32[16,32,128]{2,1,0:T(8,128)S(1)} %get-tuple-element.57, f32[16,32,128]{2,1,0:T(8,128)S(1)} %get-tuple-element.58, f32[16,32,128]{2,1,0:T(8,128)S(1)} %get-tuple-element.59, f32[16,32,128]{2,1,0:T(8,128)S(1)} %get-tuple-element.56, ...), kind=kLoop, calls=%fused_computation.9 | loop fusion | flops 9961472 | bytes 3932160 | tf_op jit(solution)/shard_map/add | solution.py:79
  41.4 2.7 %collective-permute-start.4 = (f32[8,128]{1,0:T(8,128)S(1)}, f32[8,128]{1,0:T(8,128)S(1)}, u32[]{:S(2)}, u32[]{:S(2)}) collective-permute-start(f32[8,128]{1,0:T(8,128)S(1)} %add_add_fusion.1), channel_id=1, source_target_pairs={{0,8},{1,9},{2,10},{3,11},{4,12},{5,13},{6,14},{7,15},{8,0},{9,1},... | collective-permute-start | bytes 12296 | tf_op jit(solution)/shard_map/ppermute | solution.py:418
  44.1 0.8 select_reduce_fusion.list_ref
  44.9 39.0 %collective-permute-done.5 = f32[8,128]{1,0:T(8,128)S(1)} collective-permute-done((f32[8,128]{1,0:T(8,128)S(1)}, f32[8,128]{1,0:T(8,128)S(1)}, u32[]{:S(2)}, u32[]{:S(2)}) %collective-permute-start.5) | collective-permute-done | bytes 4128 | tf_op jit(solution)/shard_map/ppermute | solution.py:418
  84.0 6.3 %row_warp.1 = bf16[32,2,32,512]{3,2,1,0:T(8,128)(2,1)} custom-call(s32[16]{0:T(128)S(1)} %get-tuple-element.51.low_ref, s32[16]{0:T(128)S(1)} %get-tuple-element.50.num_ref, bf16[4096,512]{1,0:T(8,128)(2,1)} %bitcast.3.x_ref, bf16[16,256,256]{2,1,0:T(8,128)(2,1)S(1)} %get-tuple-element.35.rows_ref, bf16[512,288]{1,0:T(8,128)(2,1)S(1)} %get-tuple-element.36.blur_ref, ...), custom_call_target="tpu_custom_call" | custom-call | flops 2000000000 | bytes 8388608 | tf_op jit(solution)/shard_map/row_warp/pallas_call | solution.py:219
  90.2 7.2 %all-to-all-start.1 = ((bf16[32,2,32,512]{3,2,1,0:T(8,128)(2,1)}), bf16[32,2,32,512]{3,2,1,0:T(8,128)(2,1)S(1)}, u32[]{:S(2)}, u32[]{:S(2)}) async-start(bf16[32,2,32,512]{3,2,1,0:T(8,128)(2,1)} %row_warp.1), calls=%async_computation.1 | async-start | bytes 4194304 | tf_op jit(solution)/shard_map/all_to_all | solution.py:449
  98.1 1.6 and_subtract_fusion.key_hbm
  101.3 3.8 %col_matrices.1.blur_hbm = bf16[8,2,288,256]{3,2,1,0:T(8,128)(2,1)} custom-call(f32[8,21]{1,0:T(8,128)} %pad_maximum_fusion.kernel_ref), custom_call_target="tpu_custom_call" | custom-call | tf_op jit(solution)/shard_map/col_matrices/pallas_call | solution.py:171
  105.2 1.5 collective-permute-start.8
  107.6 1.3 collective-permute-done.8
  108.9 3.1 %collective-permute-start.9 = (f32[8,128]{1,0:T(8,128)S(1)}, f32[8,128]{1,0:T(8,128)S(1)}, u32[]{:S(2)}, u32[]{:S(2)}) collective-permute-start(f32[8,128]{1,0:T(8,128)S(1)} %fusion.58), channel_id=1, source_target_pairs={{0,64},{32,96},{64,0},{96,32},{1,65},{33,97},{65,1},{97,33},{2,66}... | collective-permute-start | bytes 12296 | tf_op jit(solution)/shard_map/ppermute | solution.py:426
  112.1 13.5 %all-to-all-done.1.z_hbm = bf16[32,2,32,512]{3,2,1,0:T(8,128)(2,1)S(1)} async-done(((bf16[32,2,32,512]{3,2,1,0:T(8,128)(2,1)}), bf16[32,2,32,512]{3,2,1,0:T(8,128)(2,1)S(1)}, u32[]{:S(2)}, u32[]{:S(2)}) %all-to-all-start.1) | async-done | bytes 2097184 | tf_op jit(solution)/shard_map/all_to_all | solution.py:449
  125.6 1.4 copy-done.3
  126.9 19.2 %col_warp.1 = bf16[8,16,32,256]{3,2,1,0:T(8,128)(2,1)} custom-call(s32[8]{0:T(128)} %fusion.52.count_ref, s32[8,16]{1,0:T(8,128)} %select_reduce_fusion.list_ref, s32[16,32]{1,0:T(8,128)} %get-tuple-element.72.low_ref, s32[16,32]{1,0:T(8,128)} %get-tuple-element.55.num_ref, s32[16]{0:T(128)} %min.41.from_ref, s32[16]{0:T(128)} %copy-done.7, ...), custom_call_target="tpu_custom_call" | custom-call | flops 8000000000 | bytes 16777216 | tf_op jit(solution)/shard_map/col_warp/pallas_call | solution.py:353
  146.2 8.5 %all-to-all-start.2 = ((bf16[128,32,256]{2,1,0:T(8,128)(2,1)}), bf16[128,32,256]{2,1,0:T(8,128)(2,1)S(1)}, u32[]{:S(2)}, u32[]{:S(2)}) async-start(bf16[128,32,256]{2,1,0:T(8,128)(2,1)} %bitcast.49), calls=%async_computation.2 | async-start | bytes 4194304 | tf_op jit(solution)/shard_map/all_to_all | solution.py:449
  154.7 10.2 %fusion.12 = f32[32,2,1024]{2,1,0:T(2,128)S(1)} fusion(s32[32,2,1024]{2,1,0:T(2,128)S(1)} %copy-done.4, f32[32,2,1024]{2,1,0:T(2,128)S(1)} %copy-done.5), kind=kLoop, calls=%fused_computation.37 | loop fusion | flops 5636096 | bytes 786432 | tf_op jit(solution)/shard_map/add | solution.py:69
  166.4 3.4 %fusion.31 = f32[32,2,256]{2,1,0:T(2,128)S(1)} fusion(f32[32,2,4096]{2,1,0:T(2,128)} %param.20, s32[]{:T(128)S(6)} %select_n.318, s32[32,2,4096]{2,1,0:T(2,128)} %param.19, f32[32,2]{1,0:T(8,128)S(1)} %copy.33), kind=kLoop, calls=%fused_computation.119 | loop fusion | flops 1425408 | bytes 196868 | tf_op jit(solution)/shard_map/mul | solution.py:560
  169.7 1.0 fusion.13
  170.8 12.8 %all-to-all-done.2 = bf16[128,32,256]{2,1,0:T(8,128)(2,1)S(1)} async-done(((bf16[128,32,256]{2,1,0:T(8,128)(2,1)}), bf16[128,32,256]{2,1,0:T(8,128)(2,1)S(1)}, u32[]{:S(2)}, u32[]{:S(2)}) %all-to-all-start.2) | async-done | bytes 2097184 | tf_op jit(solution)/shard_map/all_to_all | solution.py:449
  183.9 1.2 fusion.1
  (83 shorter events, 10.6 us)
Async XLA Ops:
  10.9 9.0 %copy-start.1 = (bf16[4,256,2048]{2,1,0:T(8,128)(2,1)S(1)}, bf16[4,256,2048]{2,1,0:T(8,128)(2,1)}, u32[]{:S(2)}) copy-start(bf16[4,256,2048]{2,1,0:T(8,128)(2,1)} %image_ref.1) | copy-start | bytes 12582916
  14.0 26.7 %collective-permute-start.2 = (f32[8,128]{1,0:T(8,128)S(1)}, f32[8,128]{1,0:T(8,128)S(1)}, u32[]{:S(2)}, u32[]{:S(2)}) collective-permute-start(f32[8,128]{1,0:T(8,128)S(1)} %scatter.13), channel_id=1, source_target_pairs={{0,3},{1,0},{2,1},{3,2},{4,7},{5,4},{6,5},{7,6},{8,11},{9,8},{10,9... | collective-permute-start | bytes 12296 | tf_op jit(solution)/shard_map/ppermute | solution.py:418
  18.1 22.5 %collective-permute-start = (f32[8,128]{1,0:T(8,128)S(1)}, f32[8,128]{1,0:T(8,128)S(1)}, u32[]{:S(2)}, u32[]{:S(2)}) collective-permute-start(f32[8,128]{1,0:T(8,128)S(1)} %scatter.13), channel_id=1, source_target_pairs={{0,1},{1,2},{2,3},{3,0},{4,5},{5,6},{6,7},{7,4},{8,9},{9,10},{10,1... | collective-permute-start | bytes 12296 | tf_op jit(solution)/shard_map/ppermute | solution.py:418
  18.1 22.7 %collective-permute-start.1 = (f32[8,128]{1,0:T(8,128)S(1)}, f32[8,128]{1,0:T(8,128)S(1)}, u32[]{:S(2)}, u32[]{:S(2)}) collective-permute-start(f32[8,128]{1,0:T(8,128)S(1)} %scatter.13), channel_id=1, source_target_pairs={{0,2},{1,3},{2,0},{3,1},{4,6},{5,7},{6,4},{7,5},{8,10},{9,11},{10,... | collective-permute-start | bytes 12296 | tf_op jit(solution)/shard_map/ppermute | solution.py:418
  20.4 2.0 %copy-start = (bf16[16,256,512]{2,1,0:T(8,128)(2,1)}, bf16[16,256,512]{2,1,0:T(8,128)(2,1)S(1)}, u32[]{:S(2)}) copy-start(bf16[16,256,512]{2,1,0:T(8,128)(2,1)S(1)} %split_columns.1) | copy-start | bytes 12582916
  22.5 6.6 %copy-start.6 = (s32[32,2]{0,1:T(2,128)S(1)}, s32[32,2]{0,1:T(2,128)}, u32[]{:S(2)}) copy-start(s32[32,2]{0,1:T(2,128)} %param.16) | copy-start | bytes 772
  22.5 61.5 %all-to-all-start = ((bf16[16,256,512]{2,1,0:T(8,128)(2,1)}), bf16[16,256,512]{2,1,0:T(8,128)(2,1)}, u32[]{:S(2)}, u32[]{:S(2)}) async-start(bf16[16,256,512]{2,1,0:T(8,128)(2,1)} %copy-done), calls=%async_computation | async-start | bytes 8388608 | tf_op jit(solution)/shard_map/all_to_all | solution.py:449
  29.1 71.2 %collective-permute-start.7 = (f32[8,128]{1,0:T(8,128)S(1)}, f32[8,128]{1,0:T(8,128)S(1)}, u32[]{:S(2)}, u32[]{:S(2)}) collective-permute-start(f32[8,128]{1,0:T(8,128)S(1)} %scatter.12), channel_id=1, source_target_pairs={{0,16},{16,0},{1,17},{17,1},{2,18},{18,2},{3,19},{19,3},{4,20},{20... | collective-permute-start | bytes 12296 | tf_op jit(solution)/shard_map/ppermute | solution.py:476
  33.6 66.1 %copy-start.7 = (s32[16]{0:T(128)}, s32[16]{0:T(128)S(1)}, u32[]{:S(2)}) copy-start(s32[16]{0:T(128)S(1)} %get-tuple-element.44.to_ref) | copy-start | bytes 196
  40.8 43.2 %collective-permute-start.5 = (f32[8,128]{1,0:T(8,128)S(1)}, f32[8,128]{1,0:T(8,128)S(1)}, u32[]{:S(2)}, u32[]{:S(2)}) collective-permute-start(f32[8,128]{1,0:T(8,128)S(1)} %add_add_fusion.1), channel_id=1, source_target_pairs={{0,12},{1,13},{2,14},{3,15},{4,0},{5,1},{6,2},{7,3},{8,4},{9,5},{1... | collective-permute-start | bytes 12296 | tf_op jit(solution)/shard_map/ppermute | solution.py:418
  41.4 42.5 %collective-permute-start.4 = (f32[8,128]{1,0:T(8,128)S(1)}, f32[8,128]{1,0:T(8,128)S(1)}, u32[]{:S(2)}, u32[]{:S(2)}) collective-permute-start(f32[8,128]{1,0:T(8,128)S(1)} %add_add_fusion.1), channel_id=1, source_target_pairs={{0,8},{1,9},{2,10},{3,11},{4,12},{5,13},{6,14},{7,15},{8,0},{9,1},... | collective-permute-start | bytes 12296 | tf_op jit(solution)/shard_map/ppermute | solution.py:418
  44.1 39.9 %collective-permute-start.3 = (f32[8,128]{1,0:T(8,128)S(1)}, f32[8,128]{1,0:T(8,128)S(1)}, u32[]{:S(2)}, u32[]{:S(2)}) collective-permute-start(f32[8,128]{1,0:T(8,128)S(1)} %add_add_fusion.1), channel_id=1, source_target_pairs={{0,4},{1,5},{2,6},{3,7},{4,8},{5,9},{6,10},{7,11},{8,12},{9,13},{1... | collective-permute-start | bytes 12296 | tf_op jit(solution)/shard_map/ppermute | solution.py:418
  90.2 35.3 %all-to-all-start.1 = ((bf16[32,2,32,512]{3,2,1,0:T(8,128)(2,1)}), bf16[32,2,32,512]{3,2,1,0:T(8,128)(2,1)S(1)}, u32[]{:S(2)}, u32[]{:S(2)}) async-start(bf16[32,2,32,512]{3,2,1,0:T(8,128)(2,1)} %row_warp.1), calls=%async_computation.1 | async-start | bytes 4194304 | tf_op jit(solution)/shard_map/all_to_all | solution.py:449
  100.4 4.8 %collective-permute-start.6 = (f32[8,128]{1,0:T(8,128)S(1)}, f32[8,128]{1,0:T(8,128)S(1)}, u32[]{:S(2)}, u32[]{:S(2)}) collective-permute-start(f32[8,128]{1,0:T(8,128)S(1)} %broadcast_select_fusion), channel_id=1, source_target_pairs={{0,16},{16,0},{1,17},{17,1},{2,18},{18,2},{3,19},{19,3},{4,20},{20... | collective-permute-start | bytes 12296 | tf_op jit(solution)/shard_map/ppermute | solution.py:426
  105.2 3.6 %collective-permute-start.8 = (f32[8,128]{1,0:T(8,128)S(1)}, f32[8,128]{1,0:T(8,128)S(1)}, u32[]{:S(2)}, u32[]{:S(2)}) collective-permute-start(f32[8,128]{1,0:T(8,128)S(1)} %fusion.53), channel_id=1, source_target_pairs={{0,32},{32,0},{64,96},{96,64},{1,33},{33,1},{65,97},{97,65},{2,34}... | collective-permute-start | bytes 12296 | tf_op jit(solution)/shard_map/ppermute | solution.py:426
  108.9 56.0 %collective-permute-start.9 = (f32[8,128]{1,0:T(8,128)S(1)}, f32[8,128]{1,0:T(8,128)S(1)}, u32[]{:S(2)}, u32[]{:S(2)}) collective-permute-start(f32[8,128]{1,0:T(8,128)S(1)} %fusion.58), channel_id=1, source_target_pairs={{0,64},{32,96},{64,0},{96,32},{1,65},{33,97},{65,1},{97,33},{2,66}... | collective-permute-start | bytes 12296 | tf_op jit(solution)/shard_map/ppermute | solution.py:426
  125.6 1.4 copy-start.3
  146.2 8.6 %copy-start.4 = (s32[32,2,1024]{2,1,0:T(2,128)S(1)}, s32[32,2,1024]{2,1,0:T(2,128)}, u32[]{:S(2)}) copy-start(s32[32,2,1024]{2,1,0:T(2,128)} %param.17) | copy-start | bytes 786436
  146.2 8.6 %copy-start.5 = (f32[32,2,1024]{2,1,0:T(2,128)S(1)}, f32[32,2,1024]{2,1,0:T(2,128)}, u32[]{:S(2)}) copy-start(f32[32,2,1024]{2,1,0:T(2,128)} %param.18) | copy-start | bytes 786436
  146.2 37.4 %all-to-all-start.2 = ((bf16[128,32,256]{2,1,0:T(8,128)(2,1)}), bf16[128,32,256]{2,1,0:T(8,128)(2,1)S(1)}, u32[]{:S(2)}, u32[]{:S(2)}) async-start(bf16[128,32,256]{2,1,0:T(8,128)(2,1)} %bitcast.49), calls=%async_computation.2 | async-start | bytes 4194304 | tf_op jit(solution)/shard_map/all_to_all | solution.py:449
  170.8 14.3 %copy-start.2 = (f32[1024,256,1]{1,0,2:T(8,128)}, f32[1024,256,1]{1,0,2:T(8,128)S(1)}, u32[]{:S(2)}) copy-start(f32[1024,256,1]{1,0,2:T(8,128)S(1)} %fusion.13) | copy-start | bytes 3145732

commit v6 on v5

--- a/solution.py
+++ b/solution.py
@@ -20,11 +20,12 @@
 ROW_SPAN = 288
 COL_BLOCK = 128
 COL_STEP = 256
-COL_GROUP = 9
+COL_GROUP = 18
 BLUR_BLOCK = 256
 BLUR_STEP = 512
 BLUR_BAND = (112, 400)
 LANES = 128
+TAIL = 16
 LIMIT = 14 * 1024 * 1024
 COL_LIMIT = 56 * 1024 * 1024
 
@@ -180,10 +181,15 @@
     )(kernels)
 
 
-def row_body(slots, low_ref, num_ref, x_ref, rows_ref, blur_ref, turned_ref, key_ref, out_ref):
-    extent = x_ref.shape[0]
-    owner_rows = out_ref.shape[2]
+def row_body(slots, low_ref, num_ref, x_ref, rows_ref, blur_ref, turned_ref, key_ref, tail_ref,
+             out_ref):
+    extent, width = x_ref.shape
+    owners = out_ref.shape[0]
     blocks = turned_ref.shape[0] // slots
+    owner_rows = blocks * ROW_BLOCK // owners
+    data_rows = out_ref.shape[1] - TAIL
+    for owner in range(owners):
+        out_ref[owner, data_rows : data_rows + TAIL, :] = tail_ref[...]
 
     def times(matrix, start):
         first = pl.multiple_of(jnp.minimum(start, extent - ROW_STEP), 16)
@@ -203,38 +209,47 @@
 
             total = lax.fori_loop(1, num_ref[index], more, sums[slot]).astype(BF16)
             for owner in range(ROW_BLOCK // owner_rows):
-                out_ref[at * (ROW_BLOCK // owner_rows) + owner, slot] = total[
-                    owner * owner_rows : (owner + 1) * owner_rows
-                ]
+                for t in range(width // LANES):
+                    place = (t * slots + slot) * owner_rows
+                    out_ref[
+                        at * (ROW_BLOCK // owner_rows) + owner, place : place + owner_rows, :
+                    ] = total[
+                        owner * owner_rows : (owner + 1) * owner_rows,
+                        t * LANES : (t + 1) * LANES,
+                    ]
         return carry
 
     lax.fori_loop(0, blocks, block, 0)
 
 
-def row_warp(x, low, num, matrices, blur, turned, key, slots, owners):
+def row_warp(x, low, num, matrices, blur, turned, key, tail, slots, owners):
     width = x.shape[1]
     owner_rows = turned.shape[0] // slots * ROW_BLOCK // owners
     vmem = pl.BlockSpec(memory_space=pltpu.VMEM)
     smem = pl.BlockSpec(memory_space=pltpu.SMEM)
     return pl.pallas_call(
         functools.partial(row_body, slots),
-        out_shape=jax.ShapeDtypeStruct((owners, slots, owner_rows, width), BF16),
-        in_specs=[smem, smem] + [vmem] * 5,
+        out_shape=jax.ShapeDtypeStruct(
+            (owners, width // LANES * slots * owner_rows + TAIL, LANES), BF16
+        ),
+        in_specs=[smem, smem] + [vmem] * 6,
         out_specs=vmem,
         compiler_params=pltpu.CompilerParams(vmem_limit_bytes=LIMIT),
         cost_estimate=pl.CostEstimate(
             flops=2_000_000_000, bytes_accessed=8 * 1024 * 1024, transcendentals=0
         ),
         name="row_warp",
-    )(low, num, x, matrices, blur, turned, key)
-
-
-def col_body(cols, count_ref, list_ref, low_ref, num_ref, from_ref, to_ref, weight_ref, z_hbm,
-             blur_hbm, turned_hbm, key_hbm, out_ref, padded, blur, turned_ref, key_ref, blurred,
-             held, z_sems, blur_sems, table_sems):
-    slots, rows, width = z_hbm.shape[1:]
-    sources = cols // width
-    exposures = z_hbm.shape[0] // sources
+    )(low, num, x, matrices, blur, turned, key, tail)
+
+
+def col_body(cols, slots, pixels, count_ref, list_ref, low_ref, num_ref, from_ref, to_ref, z_hbm,
+             blur_hbm, turned_hbm, key_hbm, out_ref, padded, blur, turned_ref, key_ref, tails,
+             blurred, held, weight_ref, z_sems, blur_sems, table_sems):
+    data_rows = z_hbm.shape[1] - TAIL
+    exposures = blur_hbm.shape[0]
+    sources = z_hbm.shape[0] // exposures
+    tile_rows = data_rows // (cols // sources // LANES)
+    rows = tile_rows // slots
     patch = pl.program_id(0)
     begin, end = BLUR_BAND
 
@@ -244,8 +259,8 @@
         for e in range(exposures):
             copies = [
                 pltpu.make_async_copy(
-                    z_hbm.at[e * sources + s],
-                    padded.at[e, :, :, pl.ds(LANES + s * width, width)],
+                    z_hbm.at[e * sources + s, pl.ds(0, data_rows)],
+                    padded.at[e, pl.ds(tile_rows + s * data_rows, data_rows)],
                     z_sems.at[e, s],
                 )
                 for s in range(sources)
@@ -261,13 +276,17 @@
         tables = [
             pltpu.make_async_copy(turned_hbm, turned_ref, table_sems.at[0]),
             pltpu.make_async_copy(key_hbm, key_ref, table_sems.at[1]),
+            pltpu.make_async_copy(
+                z_hbm.at[:, pl.ds(data_rows, TAIL)], tails, table_sems.at[2]
+            ),
         ]
         for copy in tables:
             copy.start()
-        pad = jnp.zeros((slots, rows, LANES), BF16)
+        pad = jnp.zeros((tile_rows, LANES), BF16)
+        last = padded.shape[1] - tile_rows
         for e in range(exposures):
-            padded[e, :, :, 0:LANES] = pad
-            padded[e, :, :, LANES + cols : 2 * LANES + cols] = pad
+            padded[e, 0:tile_rows] = pad
+            padded[e, last : last + tile_rows] = pad
             for n in range(2):
                 blur[e, n, 0:begin] = jnp.zeros((begin, BLUR_BLOCK), BF16)
                 blur[e, n, end:BLUR_STEP] = jnp.zeros((BLUR_STEP - end, BLUR_BLOCK), BF16)
@@ -280,8 +299,14 @@
                 copy.wait()
             windows = jnp.concatenate(
                 [
-                    padded[e, :, :, b * BLUR_BLOCK : b * BLUR_BLOCK + BLUR_STEP].reshape(
-                        slots * rows, BLUR_STEP
+                    jnp.concatenate(
+                        [
+                            padded[e, t * tile_rows : (t + 1) * tile_rows]
+                            for t in range(
+                                b * BLUR_BLOCK // LANES, (b * BLUR_BLOCK + BLUR_STEP) // LANES
+                            )
+                        ],
+                        axis=1,
                     )
                     for b in range(cols // BLUR_BLOCK)
                 ],
@@ -296,6 +321,21 @@
                     blurred[e * slots + j, rows : 2 * rows, span] = rest[at : at + rows]
         for copy in tables:
             copy.wait()
+        sums = jnp.sum(tails[...].astype(F32), axis=1)
+        cores = 2
+        visit_exp = exposures // cores
+        lane = lax.broadcasted_iota(jnp.int32, (1, LANES), 1)
+        for core in range(cores):
+            per_core = sums.shape[0] // cores
+            total = jnp.sum(
+                sums[core * per_core : (core + 1) * per_core], axis=0, keepdims=True
+            )
+            for e in range(visit_exp):
+                variance = jnp.sum(
+                    jnp.where((lane < 3 * visit_exp) & (lane % visit_exp == e), total, 0.0)
+                )
+                for j in range(slots):
+                    weight_ref[(core * visit_exp + e) * slots + j] = 1.0 / (variance / pixels)
 
     held[...] = jnp.zeros(held.shape, F32)
 
@@ -343,29 +383,33 @@
         out_ref[0, owner] = held[:, owner * own_cols : (owner + 1) * own_cols].astype(BF16)
 
 
-def col_warp(z, count, listed, low, num, begin, end, weight, blur, turned, key, cols, patches,
-             owners):
-    slots, rows, width = z.shape[1:]
+def col_warp(z, count, listed, low, num, begin, end, blur, turned, key, cols, slots, patches,
+             owners, pixels):
     slot_total, blocks = turned.shape[:2]
     exposures = blur.shape[0]
+    sources = z.shape[0] // exposures
+    tile_rows = (z.shape[1] - TAIL) // (cols // sources // LANES)
+    rows = tile_rows // slots
     own_cols = blocks * COL_BLOCK // owners
     smem = pl.BlockSpec(memory_space=pltpu.SMEM)
     return pl.pallas_call(
-        functools.partial(col_body, cols),
+        functools.partial(col_body, cols, slots, pixels),
         out_shape=jax.ShapeDtypeStruct((patches, owners, rows, own_cols), BF16),
         grid=(patches,),
-        in_specs=[smem] * 7 + [pl.BlockSpec(memory_space=pl.ANY)] * 4,
+        in_specs=[smem] * 6 + [pl.BlockSpec(memory_space=pl.ANY)] * 4,
         out_specs=pl.BlockSpec((1, owners, rows, own_cols), lambda k: (k, 0, 0, 0)),
         scratch_shapes=[
-            pltpu.VMEM((exposures, slots, rows, cols + 2 * LANES), BF16),
+            pltpu.VMEM((exposures, (cols // LANES + 2) * tile_rows, LANES), BF16),
             pltpu.VMEM((exposures, 2, BLUR_STEP, BLUR_BLOCK), BF16),
             pltpu.VMEM(turned.shape, F32),
             pltpu.VMEM(key.shape, jnp.int32),
+            pltpu.VMEM((z.shape[0], TAIL, LANES), BF16),
             pltpu.VMEM((slot_total, 2 * rows, cols + COL_STEP), BF16),
             pltpu.VMEM((rows, owners * own_cols), F32),
-            pltpu.SemaphoreType.DMA((exposures, cols // width)),
+            pltpu.SMEM((slot_total,), F32),
+            pltpu.SemaphoreType.DMA((exposures, sources)),
             pltpu.SemaphoreType.DMA((exposures,)),
-            pltpu.SemaphoreType.DMA((2,)),
+            pltpu.SemaphoreType.DMA((3,)),
         ],
         compiler_params=pltpu.CompilerParams(
             dimension_semantics=("arbitrary",), vmem_limit_bytes=COL_LIMIT
@@ -374,49 +418,49 @@
             flops=8_000_000_000, bytes_accessed=16 * 1024 * 1024, transcendentals=0
         ),
         name="col_warp",
-    )(count, listed, low, num, begin, end, weight, z, blur, turned, key)
-
-
-def split_body(parts, image_ref, out_ref, sems):
-    width = out_ref.shape[2]
-    copies = [
+    )(count, listed, low, num, begin, end, z, blur, turned, key)
+
+
+def split_body(parts, image_ref, out_ref, held, in_sems, out_sems):
+    total, _, width = out_ref.shape
+    reads = [
         pltpu.make_async_copy(
             image_ref.at[at // parts, :, pl.ds(at % parts * width, width)],
-            out_ref.at[at],
-            sems.at[at],
+            held.at[at],
+            in_sems.at[at],
         )
-        for at in range(out_ref.shape[0])
+        for at in range(total)
     ]
-    for copy in copies:
-        copy.start()
-    for copy in copies:
-        copy.wait()
+    writes = [
+        pltpu.make_async_copy(held.at[at], out_ref.at[at], out_sems.at[at])
+        for at in range(total)
+    ]
+    for read in reads:
+        read.start()
+    for read, write in zip(reads, writes):
+        read.wait()
+        write.start()
+    for write in writes:
+        write.wait()
 
 
 def split_columns(image, parts):
     exposures, height, width = image.shape
     total = exposures * parts
+    shape = (total, height, width // parts)
     return pl.pallas_call(
         functools.partial(split_body, parts),
-        out_shape=jax.ShapeDtypeStruct((total, height, width // parts), image.dtype),
+        out_shape=jax.ShapeDtypeStruct(shape, image.dtype),
         in_specs=[pl.BlockSpec(memory_space=pl.ANY)],
-        out_specs=pl.BlockSpec(memory_space=pltpu.VMEM),
-        scratch_shapes=[pltpu.SemaphoreType.DMA((total,))],
-        compiler_params=pltpu.CompilerParams(vmem_limit_bytes=LIMIT),
+        out_specs=pl.BlockSpec(memory_space=pl.ANY),
+        scratch_shapes=[
+            pltpu.VMEM(shape, image.dtype),
+            pltpu.SemaphoreType.DMA((total,)),
+            pltpu.SemaphoreType.DMA((total,)),
+        ],
+        compiler_params=pltpu.CompilerParams(vmem_limit_bytes=COL_LIMIT),
         name="split_columns",
     )(image)
-
-
-def ring_sum(x, axis, count, stride):
-    size = lax.axis_size(axis)
-    total = x
-    for step in range(1, count):
-        pairs = []
-        for i in range(size):
-            at = i // stride % count
-            pairs.append((i, i + ((at + step) % count - at) * stride))
-        total = total + lax.ppermute(x, axis, pairs)
-    return total
 
 
 def butterfly_sum(x, axis):
@@ -448,7 +492,11 @@
     def exchange(x, axis):
         return lax.all_to_all(x, axis, split_axis=0, concat_axis=0, tiled=True)
 
-    columns = exchange(split_columns(image, parts), "region").reshape(extent, part_cols)
+    sent = split_columns(image, parts)
+    (sent, variance, psf_coef, row_start, row_frac, col_start, col_frac) = lax.optimization_barrier(
+        (sent, variance, psf_coef, row_start, row_frac, col_start, col_frac)
+    )
+    columns = exchange(sent, "region").reshape(extent, part_cols)
 
     kernels = psf_kernel(psf_coef)
 
@@ -466,25 +514,13 @@
         lax.dynamic_slice_in_dim(kernels, own_exp, 1, 0), row_low, row_turned, row_key, extent
     )
 
-    variance, psf_tile, row_matrices = lax.optimization_barrier(
-        (
-            variance,
-            jnp.zeros((8, LANES), F32).at[:exp_dev, : 2 * RADIUS + 1].set(kernels),
-            row_matrices,
-        )
-    )
-    other = lax.ppermute(psf_tile, "core", [(i, i ^ 1) for i in range(cores)])
-    other = other[:exp_dev, : 2 * RADIUS + 1]
-    col_blur = make_col_matrices(
-        jnp.concatenate(
-            [jnp.where(core_at == 0, kernels, other), jnp.where(core_at == 0, other, kernels)]
-        )
-    )
-    local_sums = jnp.sum(variance.astype(F32), axis=(1, 2))
-    tile = jnp.zeros((8, LANES), F32).at[0, :exp_dev].set(local_sums)
-    inner = 4
-    tile = ring_sum(tile, "region", inner, 1)
-    tile = ring_sum(tile, "region", regions // inner, inner)
+    rest = jnp.sum(variance.astype(F32), axis=(1, 2))
+    sum_parts = []
+    for _ in range(3):
+        sum_parts.append(lax.reduce_precision(rest, 8, 7))
+        rest = rest - sum_parts[-1]
+    tail = jnp.zeros((TAIL, LANES), F32).at[0, : 3 * exp_dev].set(jnp.concatenate(sum_parts))
+    tail = tail.astype(BF16)
     pair_exp = cores * exp_dev
     first_exp = pair_at * pair_exp
 
@@ -514,23 +550,30 @@
     )
 
     warped = row_warp(
-        columns, row_low, row_num, row_matrices, row_blur, row_turned, row_key, slots,
+        columns, row_low, row_num, row_matrices, row_blur, row_turned, row_key, tail, slots,
         cores * regions,
     )
-    tile, warped = lax.optimization_barrier((tile, warped))
+    psf_tile = jnp.zeros((8, LANES), F32).at[:exp_dev, : 2 * RADIUS + 1].set(kernels)
+    psf_tile, warped = lax.optimization_barrier((psf_tile, warped))
     rows = exchange(warped, ("core", "region"))
-    at_visit = lax.broadcasted_iota(jnp.int32, (8, LANES), 0) == visit_at
-    tile = jnp.where(at_visit, tile[0:1], 0.0)
-    tile = butterfly_sum(tile, "core")
-    pair_sums = lax.dynamic_slice_in_dim(tile, pair_at * cores, cores, 0)[:, :exp_dev]
-    slot_weight = jnp.repeat(1.0 / (pair_sums.reshape(pair_exp) / (extent * width)), slots)
-    tile = butterfly_sum(tile, "y")
+    other = lax.ppermute(psf_tile, "core", [(i, i ^ 1) for i in range(cores)])
+    other = other[:exp_dev, : 2 * RADIUS + 1]
+    col_blur = make_col_matrices(
+        jnp.concatenate(
+            [jnp.where(core_at == 0, kernels, other), jnp.where(core_at == 0, other, kernels)]
+        )
+    )
+    partial = col_warp(
+        rows, count, listed, col_low, col_num, col_from, col_to, col_blur, col_turned, col_key,
+        width, slots, visits, regions, extent * width,
+    )
+    tile = rows[:, -TAIL, : 3 * exp_dev].astype(F32).reshape(cores, regions, 3, exp_dev)
+    tile = jnp.sum(jnp.sum(tile, axis=2), axis=1)
+    own = lax.broadcasted_iota(jnp.int32, (8, LANES), 0) // cores == pair_at
+    placed = jnp.zeros((8, LANES), F32).at[:, :exp_dev].set(jnp.tile(tile, (8 // cores, 1)))
+    tile = butterfly_sum(jnp.where(own, placed, 0.0), "y")
     weight = 1.0 / (tile[:visits, :exp_dev].reshape(exposures) / (extent * width))
     mean_weight = jnp.mean(weight)
-    partial = col_warp(
-        rows, count, listed, col_low, col_num, col_from, col_to, slot_weight, col_blur,
-        col_turned, col_key, width, visits, regions,
-    )
     pieces = exchange(
         partial.reshape((visits * regions,) + partial.shape[2:]), ("y", "core", "region")
     )

time: 187 us -> 185 us (0.989)
  local copies, waits for them, and re-layouts: 9.94 us -> 5.31 us
  waiting for transfers between devices: 66.6 us -> 68.6 us
  Pallas kernels: 36.4 us -> 38.3 us
    ppermute x6 -> x0, waiting for transfers between devices: 39.1 us -> none  [ring_sum(): total = total + lax.ppermute(x, axis, pairs)]
    all_to_all x3, waiting for transfers between devices: 26.3 us -> 56.4 us  [exchange(): return lax.all_to_all(x, axis, split_axis=0, concat_axis=0, tiled=True)]
    ppermute x3 -> x2, waiting for transfers between devices: 1.27 us -> 12.2 us  [butterfly_sum(): x = x + lax.ppermute(x, axis, [(i, i ^ step) for i in range(size)])]
    ppermute x6 -> x0, starting transfers between devices: 9.25 us -> none  [ring_sum(): total = total + lax.ppermute(x, axis, pairs)]
    all_to_all x3, starting transfers between devices: 22.3 us -> 30.6 us  [exchange(): return lax.all_to_all(x, axis, split_axis=0, concat_axis=0, tiled=True)]
    unnamed x19 -> x18, local copies, waits for them, and re-layouts: 4.51 us -> 0.37 us
    pallas_call x1, Pallas kernels: 0.49 us -> 3.98 us  [split_columns(): pl.pallas_call(functools.partial(split_body, parts), out_shape=jax.ShapeD...]
    ppermute x3 -> x2, starting transfers between devices: 4.98 us -> 4.9 us  [butterfly_sum(): x = x + lax.ppermute(x, axis, [(i, i ^ step) for i in range(size)])]
  transfers between devices with their start and end apart: 13 -> 6, of which waited for: 4 -> 3; matrix products, arithmetic and copies ran while one was open for 17% -> 20% of each run, Pallas kernels for 16% -> 15%
where the time goes in v6:
time: 185 us; the launch traced here: 184 us
  waiting for transfers between devices  68.6 us (37%)
  Pallas kernels  38.3 us (21%)
  starting transfers between devices  35.7 us (19%)
  other arithmetic  33.5 us (18%)
  local copies, waits for them, and re-layouts  5.31 us (3%)
    all_to_all x3, waiting for transfers between devices, exchange(): return lax.all_to_all(x, axis, split_axis=0, concat_axis=0, tiled=True)  56.4 us
    all_to_all x3, starting transfers between devices, exchange(): return lax.all_to_all(x, axis, split_axis=0, concat_axis=0, tiled=True)  30.6 us
    pallas_call x1, Pallas kernels, col_warp(): pl.pallas_call(functools.partial(col_body, cols, slots, pixels), out_shap...  17.6 us
    ppermute x2, waiting for transfers between devices, butterfly_sum(): x = x + lax.ppermute(x, axis, [(i, i ^ step) for i in range(size)])  12.2 us
    add x1, other arithmetic, coverage(): running = running + jnp.where(inside, tap, 0.0)  10.2 us
    pallas_call x1, Pallas kernels, make_row_matrices(): pl.pallas_call(functools.partial(row_matrices_body, extent), out_shape=(j...  6.57 us
    pallas_call x1, Pallas kernels, row_warp(): pl.pallas_call(functools.partial(row_body, slots), out_shape=jax.ShapeDty...  6.36 us
    ppermute x2, starting transfers between devices, butterfly_sum(): x = x + lax.ppermute(x, axis, [(i, i ^ step) for i in range(size)])  4.9 us
  transfers between devices with their start and end apart: 6, of which 3 were waited for; matrix products, arithmetic and copies ran while one was open for 20% of the time, Pallas kernels for 15%

profile of v6, /device:TPU:4, one launch (start us, length us, event | category | flops | bytes accessed | tf_op | source)
XLA Modules:
  0.0 184.1 jit_solution(1756325071520367744)
XLA Ops:
  0.6 4.0 %split_columns.1 = bf16[16,256,512]{2,1,0:T(8,128)(2,1)} custom-call(bf16[4,256,2048]{2,1,0:T(8,128)(2,1)} %image_ref.1), custom_call_target="tpu_custom_call" | custom-call | tf_op jit(solution)/shard_map/split_columns/pallas_call | solution.py:451
  4.6 8.3 %all-to-all-start = ((bf16[16,256,512]{2,1,0:T(8,128)(2,1)}), bf16[16,256,512]{2,1,0:T(8,128)(2,1)}, u32[]{:S(2)}, u32[]{:S(2)}) async-start(bf16[16,256,512]{2,1,0:T(8,128)(2,1)} %split_columns.1), calls=%async_computation | async-start | bytes 8388608 | tf_op jit(solution)/shard_map/all_to_all | solution.py:493
  13.0 1.0 constant_dynamic-slice_fusion.4
  14.3 0.7 constant_dynamic-slice_fusion.3
  15.0 0.7 constant_dynamic-slice_fusion.1
  15.7 1.0 constant_dynamic-slice_fusion
  18.0 2.9 %convert_reduce_fusion = f32[4]{0:T(128)S(1)} fusion(bf16[4,256,2048]{2,1,0:T(8,128)(2,1)} %param.16), kind=kLoop, calls=%fused_computation | loop fusion | flops 4194300 | bytes 4194320 | tf_op jit(solution)/shard_map/reduce_sum | solution.py:517
  21.5 6.6 %row_matrices.1 = (bf16[16,256,256]{2,1,0:T(8,128)(2,1)S(1)}, bf16[512,288]{1,0:T(8,128)(2,1)S(1)}) custom-call(f32[1,21]{1,0:T(1,128)S(1)} %constant_dynamic-slice_fusion.2.kernel_ref, s32[16]{0:T(128)S(1)} %get-tuple-element.73.low_ref, f32[16,8,128]{2,1,0:T(8,128)S(1)} %select_add_fusion.1.turned_ref, s32[16,8,128]{2,1,0:T(8,128)S(1)} %and_subtract_fusion.1.key_ref), custom_call_target="tpu_custom_call" | custom-call | tf_op jit(solution)/shard_map/row_matrices/pallas_call | solution.py:148
  28.2 0.8 select_reduce_fusion.list_ref
  29.1 0.6 broadcast_compare_fusion
  29.7 42.4 %all-to-all-done = bf16[16,256,512]{2,1,0:T(8,128)(2,1)} async-done(((bf16[16,256,512]{2,1,0:T(8,128)(2,1)}), bf16[16,256,512]{2,1,0:T(8,128)(2,1)}, u32[]{:S(2)}, u32[]{:S(2)}) %all-to-all-start) | async-done | bytes 4194336 | tf_op jit(solution)/shard_map/all_to_all | solution.py:493
  72.1 6.4 %row_warp.1 = bf16[32,272,128]{2,1,0:T(8,128)(2,1)} custom-call(s32[16]{0:T(128)S(1)} %get-tuple-element.73.low_ref, s32[16]{0:T(128)S(1)} %get-tuple-element.72.num_ref, bf16[4096,512]{1,0:T(8,128)(2,1)} %bitcast.2.x_ref, bf16[16,256,256]{2,1,0:T(8,128)(2,1)S(1)} %get-tuple-element.54.rows_ref, bf16[512,288]{1,0:T(8,128)(2,1)S(1)} %get-tuple-element.55.blur_ref, ...), custom_call_target="tpu_custom_call" | custom-call | flops 2000000000 | bytes 8388608 | tf_op jit(solution)/shard_map/row_warp/pallas_call | solution.py:230
  78.5 14.1 %all-to-all-start.1 = ((bf16[32,272,128]{2,1,0:T(8,128)(2,1)}), bf16[32,272,128]{2,1,0:T(8,128)(2,1)S(1)}, u32[]{:S(2)}, u32[]{:S(2)}) async-start(bf16[32,272,128]{2,1,0:T(8,128)(2,1)} %row_warp.1), calls=%async_computation.1 | async-start | bytes 4456448 | tf_op jit(solution)/shard_map/all_to_all | solution.py:493
  92.6 0.7 select_reduce_fusion.2
  93.3 1.6 and_subtract_fusion.key_hbm
  94.9 2.1 %divide_reduce-precision_fusion.5 = (f32[16,32,128]{2,1,0:T(8,128)S(1)}, f32[16,32,128]{2,1,0:T(8,128)S(1)}) fusion(f32[16,32,128]{2,1,0:T(8,128)S(1)} %reshape.642), kind=kLoop, calls=%fused_computation.61 | loop fusion | flops 2555904 | bytes 786432 | tf_op jit(solution)/shard_map/reduce_precision | solution.py:62
  97.0 2.1 %divide_reduce-precision_fusion.4 = (f32[16,32,128]{2,1,0:T(8,128)S(1)}, f32[16,32,128]{2,1,0:T(8,128)S(1)}, f32[16,32,128]{2,1,0:T(8,128)S(1)}, f32[16,32,128]{2,1,0:T(8,128)S(1)}, f32[16,32,128]{2,1,0:T(8,128)S(1)}) fusion(f32[16,32,128]{2,1,0:T(8,128)S(1)} %get-tuple-element.69, f32[16,32,128]{2,1,0:T(8,128)S(1)} %reshape.642), kind=kLoop, calls=%fused_computation.60 | loop fusion | flops 2424832 | bytes 1835008 | tf_op jit(solution)/shard_map/reduce_precision | solution.py:62
  99.1 2.6 %select_add_fusion.turned_hbm = f32[16,32,8,128]{3,2,1,0:T(8,128)} fusion(f32[16,32,128]{2,1,0:T(8,128)S(1)} %get-tuple-element.80, f32[16,32,128]{2,1,0:T(8,128)S(1)} %get-tuple-element.77, f32[16,32,128]{2,1,0:T(8,128)S(1)} %get-tuple-element.78, f32[16,32,128]{2,1,0:T(8,128)S(1)} %get-tuple-element.79, f32[16,32,128]{2,1,0:T(8,128)S(1)} %get-tuple-element.76, ...), kind=kLoop, calls=%fused_computation.9 | loop fusion | flops 9961472 | bytes 3932160 | tf_op jit(solution)/shard_map/add | solution.py:80
  101.8 0.7 fusion.52.count_ref
  103.1 0.7 compare_reduce_fusion
  104.5 3.9 %col_matrices.1.blur_hbm = bf16[8,2,288,256]{3,2,1,0:T(8,128)(2,1)} custom-call(f32[8,21]{1,0:T(8,128)} %pad_maximum_fusion.kernel_ref), custom_call_target="tpu_custom_call" | custom-call | tf_op jit(solution)/shard_map/col_matrices/pallas_call | solution.py:172
  108.4 14.0 %all-to-all-done.1.z_hbm = bf16[32,272,128]{2,1,0:T(8,128)(2,1)S(1)} async-done(((bf16[32,272,128]{2,1,0:T(8,128)(2,1)}), bf16[32,272,128]{2,1,0:T(8,128)(2,1)S(1)}, u32[]{:S(2)}, u32[]{:S(2)}) %all-to-all-start.1) | async-done | bytes 2228256 | tf_op jit(solution)/shard_map/all_to_all | solution.py:493
  122.6 0.7 broadcast_select_fusion
  123.4 1.8 collective-permute-start.1
  125.2 17.6 %col_warp.1 = bf16[8,16,32,256]{3,2,1,0:T(8,128)(2,1)} custom-call(s32[8]{0:T(128)} %fusion.52.count_ref, s32[8,16]{1,0:T(8,128)} %select_reduce_fusion.list_ref, s32[16,32]{1,0:T(8,128)} %get-tuple-element.95.low_ref, s32[16,32]{1,0:T(8,128)} %get-tuple-element.75.num_ref, s32[16]{0:T(128)} %min.41.from_ref, s32[16]{0:T(128)} %copy-done.6, ...), custom_call_target="tpu_custom_call" | custom-call | flops 8000000000 | bytes 16777216 | tf_op jit(solution)/shard_map/col_warp/pallas_call | solution.py:395
  142.8 8.2 %all-to-all-start.2 = ((bf16[128,32,256]{2,1,0:T(8,128)(2,1)}), bf16[128,32,256]{2,1,0:T(8,128)(2,1)S(1)}, u32[]{:S(2)}, u32[]{:S(2)}) async-start(bf16[128,32,256]{2,1,0:T(8,128)(2,1)} %bitcast.50), calls=%async_computation.2 | async-start | bytes 4194304 | tf_op jit(solution)/shard_map/all_to_all | solution.py:493
  151.3 3.1 %collective-permute-start.2 = (f32[8,128]{1,0:T(8,128)S(1)}, f32[8,128]{1,0:T(8,128)S(1)}, u32[]{:S(2)}, u32[]{:S(2)}) collective-permute-start(f32[8,128]{1,0:T(8,128)S(1)} %add.736), channel_id=1, source_target_pairs={{0,64},{32,96},{64,0},{96,32},{1,65},{33,97},{65,1},{97,33},{2,66}... | collective-permute-start | bytes 12296 | tf_op jit(solution)/shard_map/ppermute | solution.py:470
  154.4 10.2 %fusion.12 = f32[32,2,1024]{2,1,0:T(2,128)S(1)} fusion(s32[32,2,1024]{2,1,0:T(2,128)S(1)} %copy-done.2, f32[32,2,1024]{2,1,0:T(2,128)S(1)} %copy-done.3), kind=kLoop, calls=%fused_computation.37 | loop fusion | flops 5636096 | bytes 786432 | tf_op jit(solution)/shard_map/add | solution.py:70
  164.6 12.2 %collective-permute-done.2 = f32[8,128]{1,0:T(8,128)S(1)} collective-permute-done((f32[8,128]{1,0:T(8,128)S(1)}, f32[8,128]{1,0:T(8,128)S(1)}, u32[]{:S(2)}, u32[]{:S(2)}) %collective-permute-start.2) | collective-permute-done | bytes 4128 | tf_op jit(solution)/shard_map/ppermute | solution.py:470
  178.2 3.4 %fusion.31 = f32[32,2,256]{2,1,0:T(2,128)S(1)} fusion(f32[32,2,4096]{2,1,0:T(2,128)} %param.22, s32[]{:T(128)S(6)} %select_n.324, s32[32,2,4096]{2,1,0:T(2,128)} %param.21, f32[32,2]{1,0:T(8,128)S(1)} %copy.54), kind=kLoop, calls=%fused_computation.119 | loop fusion | flops 1425408 | bytes 196868 | tf_op jit(solution)/shard_map/mul | solution.py:603
  181.6 1.0 fusion.13
  183.0 1.2 fusion.1
  (72 shorter events, 5.5 us)
Async XLA Ops:
  4.6 67.5 %all-to-all-start = ((bf16[16,256,512]{2,1,0:T(8,128)(2,1)}), bf16[16,256,512]{2,1,0:T(8,128)(2,1)}, u32[]{:S(2)}, u32[]{:S(2)}) async-start(bf16[16,256,512]{2,1,0:T(8,128)(2,1)} %split_columns.1), calls=%async_computation | async-start | bytes 8388608 | tf_op jit(solution)/shard_map/all_to_all | solution.py:493
  12.9 3.8 %copy-start.4 = (s32[32,2]{0,1:T(2,128)S(1)}, s32[32,2]{0,1:T(2,128)}, u32[]{:S(2)}) copy-start(s32[32,2]{0,1:T(2,128)} %param.18) | copy-start | bytes 772
  12.9 4.4 %copy-start.5 = (f32[4,3]{1,0:T(4,128)S(1)}, f32[4,3]{1,0:T(4,128)}, u32[]{:S(2)}) copy-start(f32[4,3]{1,0:T(4,128)} %param.17) | copy-start | bytes 148
  12.9 4.7 %copy-start.7 = (f32[3]{0:T(128)S(1)}, f32[3]{0:T(128)}, u32[]{:S(2)}) copy-start(f32[3]{0:T(128)} %constant.303) | copy-start | bytes 40
  78.5 43.9 %all-to-all-start.1 = ((bf16[32,272,128]{2,1,0:T(8,128)(2,1)}), bf16[32,272,128]{2,1,0:T(8,128)(2,1)S(1)}, u32[]{:S(2)}, u32[]{:S(2)}) async-start(bf16[32,272,128]{2,1,0:T(8,128)(2,1)} %row_warp.1), calls=%async_computation.1 | async-start | bytes 4456448 | tf_op jit(solution)/shard_map/all_to_all | solution.py:493
  93.3 9.2 %copy-start.6 = (s32[16]{0:T(128)}, s32[16]{0:T(128)S(1)}, u32[]{:S(2)}) copy-start(s32[16]{0:T(128)S(1)} %get-tuple-element.64.to_ref) | copy-start | bytes 196
  101.7 2.1 %collective-permute-start = (f32[8,128]{1,0:T(8,128)S(1)}, f32[8,128]{1,0:T(8,128)S(1)}, u32[]{:S(2)}, u32[]{:S(2)}) collective-permute-start(f32[8,128]{1,0:T(8,128)S(1)} %scatter.6), channel_id=1, source_target_pairs={{0,16},{16,0},{1,17},{17,1},{2,18},{18,2},{3,19},{19,3},{4,20},{20... | collective-permute-start | bytes 12296 | tf_op jit(solution)/shard_map/ppermute | solution.py:559
  122.3 2.9 %copy-start.1 = (bf16[32,272,128]{2,1,0:T(8,128)(2,1)}, bf16[32,272,128]{2,1,0:T(8,128)(2,1)S(1)}, u32[]{:S(2)}) copy-start(bf16[32,272,128]{2,1,0:T(8,128)(2,1)S(1)} %all-to-all-done.1.z_hbm) | copy-start | bytes 6684676
  123.4 27.7 %collective-permute-start.1 = (f32[8,128]{1,0:T(8,128)S(1)}, f32[8,128]{1,0:T(8,128)S(1)}, u32[]{:S(2)}, u32[]{:S(2)}) collective-permute-start(f32[8,128]{1,0:T(8,128)S(1)} %select_n.336), channel_id=1, source_target_pairs={{0,32},{32,0},{64,96},{96,64},{1,33},{33,1},{65,97},{97,65},{2,34}... | collective-permute-start | bytes 12296 | tf_op jit(solution)/shard_map/ppermute | solution.py:470
  142.8 11.6 %copy-start.2 = (s32[32,2,1024]{2,1,0:T(2,128)S(1)}, s32[32,2,1024]{2,1,0:T(2,128)}, u32[]{:S(2)}) copy-start(s32[32,2,1024]{2,1,0:T(2,128)} %param.19) | copy-start | bytes 786436
  142.8 11.6 %copy-start.3 = (f32[32,2,1024]{2,1,0:T(2,128)S(1)}, f32[32,2,1024]{2,1,0:T(2,128)}, u32[]{:S(2)}) copy-start(f32[32,2,1024]{2,1,0:T(2,128)} %param.20) | copy-start | bytes 786436
  142.8 39.8 %all-to-all-start.2 = ((bf16[128,32,256]{2,1,0:T(8,128)(2,1)}), bf16[128,32,256]{2,1,0:T(8,128)(2,1)S(1)}, u32[]{:S(2)}, u32[]{:S(2)}) async-start(bf16[128,32,256]{2,1,0:T(8,128)(2,1)} %bitcast.50), calls=%async_computation.2 | async-start | bytes 4194304 | tf_op jit(solution)/shard_map/all_to_all | solution.py:493
  151.3 25.5 %collective-permute-start.2 = (f32[8,128]{1,0:T(8,128)S(1)}, f32[8,128]{1,0:T(8,128)S(1)}, u32[]{:S(2)}, u32[]{:S(2)}) collective-permute-start(f32[8,128]{1,0:T(8,128)S(1)} %add.736), channel_id=1, source_target_pairs={{0,64},{32,96},{64,0},{96,32},{1,65},{33,97},{65,1},{97,33},{2,66}... | collective-permute-start | bytes 12296 | tf_op jit(solution)/shard_map/ppermute | solution.py:470
  182.6 1.5 copy-start

commit v7 on v6

--- a/solution.py
+++ b/solution.py
@@ -27,6 +27,7 @@
 LANES = 128
 TAIL = 16
 LIMIT = 14 * 1024 * 1024
+ROW_LIMIT = 24 * 1024 * 1024
 COL_LIMIT = 56 * 1024 * 1024
 
 
@@ -181,15 +182,29 @@
     )(kernels)
 
 
-def row_body(slots, low_ref, num_ref, x_ref, rows_ref, blur_ref, turned_ref, key_ref, tail_ref,
-             out_ref):
+def row_body(slots, pieces, low_ref, num_ref, from_ref, *refs):
+    piece_refs = refs[:pieces]
+    rows_ref, blur_ref, turned_ref, key_ref, tail_ref, out_ref, x_ref, sems = refs[pieces:]
     extent, width = x_ref.shape
+    height = extent // pieces
+    copies = [
+        pltpu.make_async_copy(
+            piece_ref,
+            x_ref.at[pl.ds(pl.multiple_of(from_ref[at] * height, height), height)],
+            sems.at[at],
+        )
+        for at, piece_ref in enumerate(piece_refs)
+    ]
+    for copy in copies:
+        copy.start()
     owners = out_ref.shape[0]
     blocks = turned_ref.shape[0] // slots
     owner_rows = blocks * ROW_BLOCK // owners
     data_rows = out_ref.shape[1] - TAIL
     for owner in range(owners):
         out_ref[owner, data_rows : data_rows + TAIL, :] = tail_ref[...]
+    for copy in copies:
+        copy.wait()
 
     def times(matrix, start):
         first = pl.multiple_of(jnp.minimum(start, extent - ROW_STEP), 16)
@@ -222,24 +237,28 @@
     lax.fori_loop(0, blocks, block, 0)
 
 
-def row_warp(x, low, num, matrices, blur, turned, key, tail, slots, owners):
-    width = x.shape[1]
+def row_warp(pieces, sources, low, num, matrices, blur, turned, key, tail, slots, owners):
+    height, width = pieces[0].shape
     owner_rows = turned.shape[0] // slots * ROW_BLOCK // owners
     vmem = pl.BlockSpec(memory_space=pltpu.VMEM)
     smem = pl.BlockSpec(memory_space=pltpu.SMEM)
     return pl.pallas_call(
-        functools.partial(row_body, slots),
+        functools.partial(row_body, slots, len(pieces)),
         out_shape=jax.ShapeDtypeStruct(
             (owners, width // LANES * slots * owner_rows + TAIL, LANES), BF16
         ),
-        in_specs=[smem, smem] + [vmem] * 6,
+        in_specs=[smem] * 3 + [pl.BlockSpec(memory_space=pl.ANY)] * len(pieces) + [vmem] * 5,
         out_specs=vmem,
-        compiler_params=pltpu.CompilerParams(vmem_limit_bytes=LIMIT),
+        scratch_shapes=[
+            pltpu.VMEM((len(pieces) * height, width), BF16),
+            pltpu.SemaphoreType.DMA((len(pieces),)),
+        ],
+        compiler_params=pltpu.CompilerParams(vmem_limit_bytes=ROW_LIMIT),
         cost_estimate=pl.CostEstimate(
             flops=2_000_000_000, bytes_accessed=8 * 1024 * 1024, transcendentals=0
         ),
         name="row_warp",
-    )(low, num, x, matrices, blur, turned, key, tail)
+    )(low, num, sources, *pieces, matrices, blur, turned, key, tail)
 
 
 def col_body(cols, slots, pixels, count_ref, list_ref, low_ref, num_ref, from_ref, to_ref, z_hbm,
@@ -421,19 +440,23 @@
     )(count, listed, low, num, begin, end, z, blur, turned, key)
 
 
-def split_body(parts, image_ref, out_ref, held, in_sems, out_sems):
-    total, _, width = out_ref.shape
-    reads = [
-        pltpu.make_async_copy(
-            image_ref.at[at // parts, :, pl.ds(at % parts * width, width)],
-            held.at[at],
-            in_sems.at[at],
+def split_body(parts, to_ref, image_ref, *refs):
+    total = len(refs) - 3
+    out_refs = refs[:total]
+    held, in_sems, out_sems = refs[total:]
+    width = held.shape[2]
+    reads = []
+    for at in range(total):
+        lane = pl.multiple_of(to_ref[at] % parts * width, width)
+        reads.append(
+            pltpu.make_async_copy(
+                image_ref.at[to_ref[at] // parts, :, pl.ds(lane, width)],
+                held.at[at],
+                in_sems.at[at],
+            )
         )
-        for at in range(total)
-    ]
     writes = [
-        pltpu.make_async_copy(held.at[at], out_ref.at[at], out_sems.at[at])
-        for at in range(total)
+        pltpu.make_async_copy(held.at[at], out_refs[at], out_sems.at[at]) for at in range(total)
     ]
     for read in reads:
         read.start()
@@ -444,23 +467,58 @@
         write.wait()
 
 
-def split_columns(image, parts):
+def split_columns(image, targets, parts):
     exposures, height, width = image.shape
     total = exposures * parts
-    shape = (total, height, width // parts)
+    shape = (height, width // parts)
     return pl.pallas_call(
         functools.partial(split_body, parts),
-        out_shape=jax.ShapeDtypeStruct(shape, image.dtype),
-        in_specs=[pl.BlockSpec(memory_space=pl.ANY)],
-        out_specs=pl.BlockSpec(memory_space=pl.ANY),
+        out_shape=[jax.ShapeDtypeStruct(shape, image.dtype)] * total,
+        in_specs=[
+            pl.BlockSpec(memory_space=pltpu.SMEM),
+            pl.BlockSpec(memory_space=pl.ANY),
+        ],
+        out_specs=[pl.BlockSpec(memory_space=pl.ANY)] * total,
         scratch_shapes=[
-            pltpu.VMEM(shape, image.dtype),
+            pltpu.VMEM((total,) + shape, image.dtype),
             pltpu.SemaphoreType.DMA((total,)),
             pltpu.SemaphoreType.DMA((total,)),
         ],
         compiler_params=pltpu.CompilerParams(vmem_limit_bytes=COL_LIMIT),
         name="split_columns",
-    )(image)
+    )(targets, image)
+
+
+RING = 4
+
+TWO_STEPS = {
+    (2, 0): ((1, 0), (1, 0)),
+    (2, 3): ((1, 0), (1, -1)),
+    (2, 1): ((-1, 0), (-1, 1)),
+    (2, 2): ((-1, 1), (-1, 1)),
+    (0, 2): ((0, 1), (0, 1)),
+    (1, 2): ((0, -1), (1, -1)),
+    (3, 2): ((0, -1), (-1, -1)),
+}
+
+
+def region_shifts(regions):
+    outer = regions // RING
+    shifts = [(dx, dz) for dx in range(outer) for dz in range(RING)]
+    return sorted(shifts, key=lambda s: (s == (0, 0), s not in TWO_STEPS))
+
+
+def shifted(at, shift, regions):
+    outer = regions // RING
+    return (at // RING + shift[0]) % outer * RING + (at % RING + shift[1]) % RING
+
+
+def send_shifted(x, shift, regions):
+    if shift == (0, 0):
+        return x
+    for step in TWO_STEPS.get(shift, (shift,)):
+        x = lax.ppermute(x, "region", [(i, shifted(i, step, regions)) for i in range(regions)])
+    return x
 
 
 def butterfly_sum(x, axis):
@@ -492,11 +550,15 @@
     def exchange(x, axis):
         return lax.all_to_all(x, axis, split_axis=0, concat_axis=0, tiled=True)
 
-    sent = split_columns(image, parts)
-    (sent, variance, psf_coef, row_start, row_frac, col_start, col_frac) = lax.optimization_barrier(
-        (sent, variance, psf_coef, row_start, row_frac, col_start, col_frac)
-    )
-    columns = exchange(sent, "region").reshape(extent, part_cols)
+    shifts = region_shifts(regions)
+    targets = jnp.stack([shifted(region_at, shift, regions) for shift in shifts])
+    sources = jnp.stack([shifted(region_at, (-dx, -dz), regions) for dx, dz in shifts])
+    sent = split_columns(image, targets.astype(jnp.int32), parts)
+    (first, variance, psf_coef, row_start, row_frac, col_start, col_frac) = lax.optimization_barrier(
+        (sent[0], variance, psf_coef, row_start, row_frac, col_start, col_frac)
+    )
+    sent = [first] + list(sent[1:])
+    columns = [send_shifted(x, shift, regions) for x, shift in zip(sent, shifts)]
 
     kernels = psf_kernel(psf_coef)
 
@@ -550,7 +612,7 @@
     )
 
     warped = row_warp(
-        columns, row_low, row_num, row_matrices, row_blur, row_turned, row_key, tail, slots,
+        columns, sources.astype(jnp.int32), row_low, row_num, row_matrices, row_blur, row_turned, row_key, tail, slots,
         cores * regions,
     )
     psf_tile = jnp.zeros((8, LANES), F32).at[:exp_dev, : 2 * RADIUS + 1].set(kernels)

time: 185 us -> 190 us (1.027)
  waiting for transfers between devices: 68.6 us -> 30.5 us
  starting transfers between devices: 35.7 us -> 61.2 us
  local copies, waits for them, and re-layouts: 5.31 us -> 22.4 us
    all_to_all x3 -> x2, waiting for transfers between devices: 56.4 us -> 14.1 us  [exchange(): return lax.all_to_all(x, axis, split_axis=0, concat_axis=0, tiled=True)]
    ppermute x0 -> x22, starting transfers between devices: none -> 39.6 us  [send_shifted(): lax.ppermute(x, 'region', [(i, shifted(i, step, regions)) for i in range(...]
    all_to_all x3 -> x2, starting transfers between devices: 30.6 us -> 16.5 us  [exchange(): return lax.all_to_all(x, axis, split_axis=0, concat_axis=0, tiled=True)]
    unnamed x18 -> x80, local copies, waits for them, and re-layouts: 0.37 us -> 11.9 us
    ppermute x0 -> x22, waiting for transfers between devices: none -> 4.15 us  [send_shifted(): lax.ppermute(x, 'region', [(i, shifted(i, step, regions)) for i in range(...]
  transfers between devices with their start and end apart: 6 -> 27, of which waited for: 3 -> 5; matrix products, arithmetic and copies ran while one was open for 20% -> 23% of each run, Pallas kernels for 15% -> 15%
where the time goes in v7:
time: 190 us
  starting transfers between devices  61.2 us (32%)
  Pallas kernels  38.8 us (20%)
  other arithmetic  33.5 us (18%)
  waiting for transfers between devices  30.5 us (16%)
  local copies, waits for them, and re-layouts  22.4 us (12%)
  between operations  2.09 us (1%)
    ppermute x22, starting transfers between devices, send_shifted(): lax.ppermute(x, 'region', [(i, shifted(i, step, regions)) for i in range(...  39.6 us
    pallas_call x1, Pallas kernels, col_warp(): pl.pallas_call(functools.partial(col_body, cols, slots, pixels), out_shap...  17.5 us
    all_to_all x2, starting transfers between devices, exchange(): return lax.all_to_all(x, axis, split_axis=0, concat_axis=0, tiled=True)  16.5 us
    all_to_all x2, waiting for transfers between devices, exchange(): return lax.all_to_all(x, axis, split_axis=0, concat_axis=0, tiled=True)  14.1 us
    ppermute x2, waiting for transfers between devices, butterfly_sum(): x = x + lax.ppermute(x, axis, [(i, i ^ step) for i in range(size)])  12.2 us
    unnamed x80, local copies, waits for them, and re-layouts  11.9 us
    add x1, other arithmetic, coverage(): running = running + jnp.where(inside, tap, 0.0)  10.2 us
    pallas_call x1, Pallas kernels, make_row_matrices(): pl.pallas_call(functools.partial(row_matrices_body, extent), out_shape=(j...  6.57 us
  transfers between devices with their start and end apart: 27, of which 5 were waited for; matrix products, arithmetic and copies ran while one was open for 23% of the time, Pallas kernels for 15%

profile of v7, /device:TPU:4, one launch (start us, length us, event | category | flops | bytes accessed | tf_op | source)
XLA Modules:
  0.0 189.6 jit_solution(16584630427503891445)
XLA Ops:
  1.4 4.8 %split_columns.1 = (bf16[256,512]{1,0:T(8,128)(2,1)}, bf16[256,512]{1,0:T(8,128)(2,1)}, bf16[256,512]{1,0:T(8,128)(2,1)}, bf16[256,512]{1,0:T(8,128)(2,1)}, bf16...) custom-call(s32[16]{0:T(128)} %stack.116.to_ref, ...), custom_call_target="tpu_custom_call" | custom-call | tf_op jit(solution)/shard_map/split_columns/pallas_call | solution.py:474
  6.2 2.0 %collective-permute-start = (bf16[256,512]{1,0:T(8,128)(2,1)}, bf16[256,512]{1,0:T(8,128)(2,1)}, u32[]{:S(2)}, u32[]{:S(2)}) collective-permute-start(bf16[256,512]{1,0:T(8,128)(2,1)} %get-tuple-element.69), channel_id=1, source_target_pairs={{0,1},{1,2},{2,3},{3,0},{4,5},{5,6},{6,7},{7,4},{8,9},{9,10},{10,1... | collective-permute-start | bytes 786440 | tf_op jit(solution)/shard_map/ppermute | solution.py:520
  8.2 2.2 %collective-permute-start.2 = (bf16[256,512]{1,0:T(8,128)(2,1)}, bf16[256,512]{1,0:T(8,128)(2,1)}, u32[]{:S(2)}, u32[]{:S(2)}) collective-permute-start(bf16[256,512]{1,0:T(8,128)(2,1)} %get-tuple-element.70), channel_id=1, source_target_pairs={{0,3},{1,0},{2,1},{3,2},{4,7},{5,4},{6,5},{7,6},{8,11},{9,8},{10,9... | collective-permute-start | bytes 786440 | tf_op jit(solution)/shard_map/ppermute | solution.py:520
  12.7 1.7 constant_dynamic-slice_fusion.4
  16.3 3.0 %convert_reduce_fusion = f32[4]{0:T(128)S(1)} fusion(bf16[4,256,2048]{2,1,0:T(8,128)(2,1)} %param.16), kind=kLoop, calls=%fused_computation | loop fusion | flops 4194300 | bytes 4194320 | tf_op jit(solution)/shard_map/reduce_sum | solution.py:579
  19.3 1.7 constant_dynamic-slice_fusion
  22.9 3.4 %collective-permute-start.12 = (bf16[256,512]{1,0:T(8,128)(2,1)S(1)}, bf16[256,512]{1,0:T(8,128)(2,1)S(1)}, u32[]{:S(2)}, u32[]{:S(2)}) collective-permute-start(bf16[256,512]{1,0:T(8,128)(2,1)S(1)} %copy-done.37), channel_id=1, source_target_pairs={{0,3},{1,0},{2,1},{3,2},{4,7},{5,4},{6,5},{7,6},{8,11},{9,8},{10,9... | collective-permute-start | bytes 786440 | tf_op jit(solution)/shard_map/ppermute | solution.py:520
  27.3 3.2 %collective-permute-start.15 = (bf16[256,512]{1,0:T(8,128)(2,1)S(1)}, bf16[256,512]{1,0:T(8,128)(2,1)S(1)}, u32[]{:S(2)}, u32[]{:S(2)}) collective-permute-start(bf16[256,512]{1,0:T(8,128)(2,1)S(1)} %copy-done.36), channel_id=1, source_target_pairs={{0,3},{1,0},{2,1},{3,2},{4,7},{5,4},{6,5},{7,6},{8,11},{9,8},{10,9... | collective-permute-start | bytes 786440 | tf_op jit(solution)/shard_map/ppermute | solution.py:520
  30.5 2.5 %collective-permute-start.16 = (bf16[256,512]{1,0:T(8,128)(2,1)S(1)}, bf16[256,512]{1,0:T(8,128)(2,1)S(1)}, u32[]{:S(2)}, u32[]{:S(2)}) collective-permute-start(bf16[256,512]{1,0:T(8,128)(2,1)S(1)} %copy-done.35), channel_id=1, source_target_pairs={{0,4},{1,5},{2,6},{3,7},{4,8},{5,9},{6,10},{7,11},{8,12},{9,13},{1... | collective-permute-start | bytes 786440 | tf_op jit(solution)/shard_map/ppermute | solution.py:520
  33.7 4.5 %collective-permute-start.18 = (bf16[256,512]{1,0:T(8,128)(2,1)S(1)}, bf16[256,512]{1,0:T(8,128)(2,1)S(1)}, u32[]{:S(2)}, u32[]{:S(2)}) collective-permute-start(bf16[256,512]{1,0:T(8,128)(2,1)S(1)} %copy-done.33), channel_id=1, source_target_pairs={{0,7},{1,4},{2,5},{3,6},{4,11},{5,8},{6,9},{7,10},{8,15},{9,12},{1... | collective-permute-start | bytes 786440 | tf_op jit(solution)/shard_map/ppermute | solution.py:520
  39.8 4.6 %collective-permute-start.21 = (bf16[256,512]{1,0:T(8,128)(2,1)}, bf16[256,512]{1,0:T(8,128)(2,1)S(1)}, u32[]{:S(2)}, u32[]{:S(2)}) collective-permute-start(bf16[256,512]{1,0:T(8,128)(2,1)} %get-tuple-element.83), channel_id=1, source_target_pairs={{0,15},{1,12},{2,13},{3,14},{4,3},{5,0},{6,1},{7,2},{8,7},{9,4},{1... | collective-permute-start | bytes 786440 | tf_op jit(solution)/shard_map/ppermute | solution.py:520
  47.0 2.4 %collective-permute-done.18.refs_11_ = bf16[256,512]{1,0:T(8,128)(2,1)S(1)} collective-permute-done((bf16[256,512]{1,0:T(8,128)(2,1)S(1)}, bf16[256,512]{1,0:T(8,128)(2,1)S(1)}, u32[]{:S(2)}, u32[]{:S(2)}) %collective-permute-start.18) | collective-permute-done | bytes 262176 | tf_op jit(solution)/shard_map/ppermute | solution.py:520
  49.4 5.1 %collective-permute-start.3 = (bf16[256,512]{1,0:T(8,128)(2,1)}, bf16[256,512]{1,0:T(8,128)(2,1)S(1)}, u32[]{:S(2)}, u32[]{:S(2)}) collective-permute-start(bf16[256,512]{1,0:T(8,128)(2,1)} %collective-permute-done.2), channel_id=1, source_target_pairs={{0,7},{1,4},{2,5},{3,6},{4,11},{5,8},{6,9},{7,10},{8,15},{9,12},{1... | collective-permute-start | bytes 786440 | tf_op jit(solution)/shard_map/ppermute | solution.py:520
  58.4 3.3 %collective-permute-start.11 = (bf16[256,512]{1,0:T(8,128)(2,1)}, bf16[256,512]{1,0:T(8,128)(2,1)}, u32[]{:S(2)}, u32[]{:S(2)}) collective-permute-start(bf16[256,512]{1,0:T(8,128)(2,1)} %copy-done.31), channel_id=1, source_target_pairs={{0,7},{1,4},{2,5},{3,6},{4,11},{5,8},{6,9},{7,10},{8,15},{9,12},{1... | collective-permute-start | bytes 786440 | tf_op jit(solution)/shard_map/ppermute | solution.py:520
  62.4 1.9 %collective-permute-start.13 = (bf16[256,512]{1,0:T(8,128)(2,1)}, bf16[256,512]{1,0:T(8,128)(2,1)}, u32[]{:S(2)}, u32[]{:S(2)}) collective-permute-start(bf16[256,512]{1,0:T(8,128)(2,1)} %copy-done.32), channel_id=1, source_target_pairs={{0,15},{1,12},{2,13},{3,14},{4,3},{5,0},{6,1},{7,2},{8,7},{9,4},{1... | collective-permute-start | bytes 786440 | tf_op jit(solution)/shard_map/ppermute | solution.py:520
  66.6 1.9 reshape.638
  68.6 6.6 %row_matrices.1 = (bf16[16,256,256]{2,1,0:T(8,128)(2,1)S(1)}, bf16[512,288]{1,0:T(8,128)(2,1)S(1)}) custom-call(f32[1,21]{1,0:T(1,128)S(1)} %constant_dynamic-slice_fusion.2.kernel_ref, s32[16]{0:T(128)S(1)} %get-tuple-element.105.low_ref, f32[16,8,128]{2,1,0:T(8,128)S(1)} %select_add_fusion.1.turned_ref.refs_18_, ...), custom_call_target="tpu_custom_call" | custom-call | tf_op jit(solution)/shard_map/row_matrices/pallas_call | solution.py:149
  83.5 6.1 %row_warp.1 = bf16[32,272,128]{2,1,0:T(8,128)(2,1)} custom-call(s32[16]{0:T(128)S(1)} %get-tuple-element.105.low_ref, s32[16]{0:T(128)S(1)} %get-tuple-element.104.num_ref, s32[16]{0:T(128)S(1)} %stack.132.from_ref, bf16[256,512]{1,0:T(8,128)(2,1)S(1)} %copy-done.14, bf16[256,512]{1,0:T(8,128)(2,1)S(1)} %copy-done.16, ...), custom_call_target="tpu_custom_call" | custom-call | flops 2000000000 | bytes 8388608 | tf_op jit(solution)/shard_map/row_warp/pallas_call | solution.py:245
  89.7 8.5 %all-to-all-start = ((bf16[32,272,128]{2,1,0:T(8,128)(2,1)}), bf16[32,272,128]{2,1,0:T(8,128)(2,1)S(1)}, u32[]{:S(2)}, u32[]{:S(2)}) async-start(bf16[32,272,128]{2,1,0:T(8,128)(2,1)} %row_warp.1), calls=%async_computation | async-start | bytes 4456448 | tf_op jit(solution)/shard_map/all_to_all | solution.py:551
  99.0 1.7 and_subtract_fusion.key_hbm
  100.6 2.1 %divide_reduce-precision_fusion.5 = (f32[16,32,128]{2,1,0:T(8,128)S(1)}, f32[16,32,128]{2,1,0:T(8,128)S(1)}) fusion(f32[16,32,128]{2,1,0:T(8,128)S(1)} %copy-done.20), kind=kLoop, calls=%fused_computation.61 | loop fusion | flops 2555904 | bytes 786432 | tf_op jit(solution)/shard_map/reduce_precision | solution.py:63
  102.7 2.1 %divide_reduce-precision_fusion.4 = (f32[16,32,128]{2,1,0:T(8,128)S(1)}, f32[16,32,128]{2,1,0:T(8,128)S(1)}, f32[16,32,128]{2,1,0:T(8,128)S(1)}, f32[16,32,128]{2,1,0:T(8,128)S(1)}, f32[16,32,128]{2,1,0:T(8,128)S(1)}) fusion(f32[16,32,128]{2,1,0:T(8,128)S(1)} %get-tuple-element.101, f32[16,32,128]{2,1,0:T(8,128)S(1)} %copy-done.20), kind=kLoop, calls=%fused_computation.60 | loop fusion | flops 2424832 | bytes 1835008 | tf_op jit(solution)/shard_map/reduce_precision | solution.py:63
  104.8 2.5 %select_add_fusion.turned_hbm = f32[16,32,8,128]{3,2,1,0:T(8,128)} fusion(f32[16,32,128]{2,1,0:T(8,128)S(1)} %get-tuple-element.112, f32[16,32,128]{2,1,0:T(8,128)S(1)} %get-tuple-element.109, f32[16,32,128]{2,1,0:T(8,128)S(1)} %get-tuple-element.110, f32[16,32,128]{2,1,0:T(8,128)S(1)} %get-tuple-element.111, f32[16,32,128]{2,1,0:T(8,128)S(1)} %get-tuple-element.108, ...), kind=kLoop, calls=%fused_computation.9 | loop fusion | flops 9961472 | bytes 3932160 | tf_op jit(solution)/shard_map/add | solution.py:81
  110.1 3.9 %col_matrices.1.blur_hbm = bf16[8,2,288,256]{3,2,1,0:T(8,128)(2,1)} custom-call(f32[8,21]{1,0:T(8,128)} %pad_maximum_fusion.kernel_ref), custom_call_target="tpu_custom_call" | custom-call | tf_op jit(solution)/shard_map/col_matrices/pallas_call | solution.py:173
  114.0 14.1 %all-to-all-done.z_hbm = bf16[32,272,128]{2,1,0:T(8,128)(2,1)S(1)} async-done(((bf16[32,272,128]{2,1,0:T(8,128)(2,1)}), bf16[32,272,128]{2,1,0:T(8,128)(2,1)S(1)}, u32[]{:S(2)}, u32[]{:S(2)}) %all-to-all-start) | async-done | bytes 2228256 | tf_op jit(solution)/shard_map/all_to_all | solution.py:551
  129.2 1.9 collective-permute-start.23
  131.0 17.5 %col_warp.1 = bf16[8,16,32,256]{3,2,1,0:T(8,128)(2,1)} custom-call(s32[8]{0:T(128)} %fusion.52.count_ref, s32[8,16]{1,0:T(8,128)} %select_reduce_fusion.list_ref, s32[16,32]{1,0:T(8,128)} %get-tuple-element.127.low_ref, s32[16,32]{1,0:T(8,128)} %get-tuple-element.107.num_ref, s32[16]{0:T(128)} %min.41.from_ref, s32[16]{0:T(128)} %copy-done.26, ...), custom_call_target="tpu_custom_call" | custom-call | flops 8000000000 | bytes 16777216 | tf_op jit(solution)/shard_map/col_warp/pallas_call | solution.py:414
  148.6 8.0 %all-to-all-start.1 = ((bf16[128,32,256]{2,1,0:T(8,128)(2,1)}), bf16[128,32,256]{2,1,0:T(8,128)(2,1)S(1)}, u32[]{:S(2)}, u32[]{:S(2)}) async-start(bf16[128,32,256]{2,1,0:T(8,128)(2,1)} %bitcast.80), calls=%async_computation.1 | async-start | bytes 4194304 | tf_op jit(solution)/shard_map/all_to_all | solution.py:551
  156.8 3.1 %collective-permute-start.24 = (f32[8,128]{1,0:T(8,128)S(1)}, f32[8,128]{1,0:T(8,128)S(1)}, u32[]{:S(2)}, u32[]{:S(2)}) collective-permute-start(f32[8,128]{1,0:T(8,128)S(1)} %add.1087), channel_id=1, source_target_pairs={{0,64},{32,96},{64,0},{96,32},{1,65},{33,97},{65,1},{97,33},{2,66}... | collective-permute-start | bytes 12296 | tf_op jit(solution)/shard_map/ppermute | solution.py:528
  159.9 10.2 %fusion.12 = f32[32,2,1024]{2,1,0:T(2,128)S(1)} fusion(s32[32,2,1024]{2,1,0:T(2,128)S(1)} %copy-done.22, f32[32,2,1024]{2,1,0:T(2,128)S(1)} %copy-done.23), kind=kLoop, calls=%fused_computation.37 | loop fusion | flops 5636096 | bytes 786432 | tf_op jit(solution)/shard_map/add | solution.py:71
  170.0 12.2 %collective-permute-done.24 = f32[8,128]{1,0:T(8,128)S(1)} collective-permute-done((f32[8,128]{1,0:T(8,128)S(1)}, f32[8,128]{1,0:T(8,128)S(1)}, u32[]{:S(2)}, u32[]{:S(2)}) %collective-permute-start.24) | collective-permute-done | bytes 4128 | tf_op jit(solution)/shard_map/ppermute | solution.py:528
  183.7 3.4 %fusion.31 = f32[32,2,256]{2,1,0:T(2,128)S(1)} fusion(f32[32,2,4096]{2,1,0:T(2,128)} %param.22, s32[]{:T(128)S(6)} %select_n.595, s32[32,2,4096]{2,1,0:T(2,128)} %param.21, f32[32,2]{1,0:T(8,128)S(1)} %copy.54), kind=kLoop, calls=%fused_computation.119 | loop fusion | flops 1425408 | bytes 196868 | tf_op jit(solution)/shard_map/mul | solution.py:665
  (178 shorter events, 35.7 us)
Async XLA Ops:
  6.2 15.3 %collective-permute-start = (bf16[256,512]{1,0:T(8,128)(2,1)}, bf16[256,512]{1,0:T(8,128)(2,1)}, u32[]{:S(2)}, u32[]{:S(2)}) collective-permute-start(bf16[256,512]{1,0:T(8,128)(2,1)} %get-tuple-element.69), channel_id=1, source_target_pairs={{0,1},{1,2},{2,3},{3,0},{4,5},{5,6},{6,7},{7,4},{8,9},{9,10},{10,1... | collective-permute-start | bytes 786440 | tf_op jit(solution)/shard_map/ppermute | solution.py:520
  8.2 14.7 %collective-permute-start.2 = (bf16[256,512]{1,0:T(8,128)(2,1)}, bf16[256,512]{1,0:T(8,128)(2,1)}, u32[]{:S(2)}, u32[]{:S(2)}) collective-permute-start(bf16[256,512]{1,0:T(8,128)(2,1)} %get-tuple-element.70), channel_id=1, source_target_pairs={{0,3},{1,0},{2,1},{3,2},{4,7},{5,4},{6,5},{7,6},{8,11},{9,8},{10,9... | collective-permute-start | bytes 786440 | tf_op jit(solution)/shard_map/ppermute | solution.py:520
  10.4 16.0 %collective-permute-start.4 = (bf16[256,512]{1,0:T(8,128)(2,1)}, bf16[256,512]{1,0:T(8,128)(2,1)S(1)}, u32[]{:S(2)}, u32[]{:S(2)}) collective-permute-start(bf16[256,512]{1,0:T(8,128)(2,1)} %get-tuple-element.71), channel_id=1, source_target_pairs={{0,4},{1,5},{2,6},{3,7},{4,8},{5,9},{6,10},{7,11},{8,12},{9,13},{1... | collective-permute-start | bytes 786440 | tf_op jit(solution)/shard_map/ppermute | solution.py:520
  11.6 14.9 %collective-permute-start.6 = (bf16[256,512]{1,0:T(8,128)(2,1)}, bf16[256,512]{1,0:T(8,128)(2,1)S(1)}, u32[]{:S(2)}, u32[]{:S(2)}) collective-permute-start(bf16[256,512]{1,0:T(8,128)(2,1)} %get-tuple-element.72), channel_id=1, source_target_pairs={{0,12},{1,13},{2,14},{3,15},{4,0},{5,1},{6,2},{7,3},{8,4},{9,5},{1... | collective-permute-start | bytes 786440 | tf_op jit(solution)/shard_map/ppermute | solution.py:520
  12.4 18.0 %collective-permute-start.8 = (bf16[256,512]{1,0:T(8,128)(2,1)}, bf16[256,512]{1,0:T(8,128)(2,1)S(1)}, u32[]{:S(2)}, u32[]{:S(2)}) collective-permute-start(bf16[256,512]{1,0:T(8,128)(2,1)} %get-tuple-element.73), channel_id=1, source_target_pairs={{0,13},{1,14},{2,15},{3,12},{4,1},{5,2},{6,3},{7,0},{8,5},{9,6},{1... | collective-permute-start | bytes 786440 | tf_op jit(solution)/shard_map/ppermute | solution.py:520
  16.3 17.4 %copy-start.33 = (bf16[256,512]{1,0:T(8,128)(2,1)S(1)}, bf16[256,512]{1,0:T(8,128)(2,1)}, u32[]{:S(2)}) copy-start(bf16[256,512]{1,0:T(8,128)(2,1)} %get-tuple-element.80) | copy-start | bytes 786436
  19.3 56.6 %copy-start = (bf16[256,512]{1,0:T(8,128)(2,1)S(1)}, bf16[256,512]{1,0:T(8,128)(2,1)}, u32[]{:S(2)}) copy-start(bf16[256,512]{1,0:T(8,128)(2,1)} %get-tuple-element.84.refs_15_) | copy-start | bytes 786436
  21.6 11.4 %collective-permute-start.10 = (bf16[256,512]{1,0:T(8,128)(2,1)S(1)}, bf16[256,512]{1,0:T(8,128)(2,1)S(1)}, u32[]{:S(2)}, u32[]{:S(2)}) collective-permute-start(bf16[256,512]{1,0:T(8,128)(2,1)S(1)} %copy-done.38), channel_id=1, source_target_pairs={{0,4},{1,5},{2,6},{3,7},{4,8},{5,9},{6,10},{7,11},{8,12},{9,13},{1... | collective-permute-start | bytes 786440 | tf_op jit(solution)/shard_map/ppermute | solution.py:520
  22.9 10.1 %collective-permute-start.12 = (bf16[256,512]{1,0:T(8,128)(2,1)S(1)}, bf16[256,512]{1,0:T(8,128)(2,1)S(1)}, u32[]{:S(2)}, u32[]{:S(2)}) collective-permute-start(bf16[256,512]{1,0:T(8,128)(2,1)S(1)} %copy-done.37), channel_id=1, source_target_pairs={{0,3},{1,0},{2,1},{3,2},{4,7},{5,4},{6,5},{7,6},{8,11},{9,8},{10,9... | collective-permute-start | bytes 786440 | tf_op jit(solution)/shard_map/ppermute | solution.py:520
  26.5 12.5 %collective-permute-start.14 = (bf16[256,512]{1,0:T(8,128)(2,1)}, bf16[256,512]{1,0:T(8,128)(2,1)S(1)}, u32[]{:S(2)}, u32[]{:S(2)}) collective-permute-start(bf16[256,512]{1,0:T(8,128)(2,1)} %get-tuple-element.76), channel_id=1, source_target_pairs={{0,1},{1,2},{2,3},{3,0},{4,5},{5,6},{6,7},{7,4},{8,9},{9,10},{10,1... | collective-permute-start | bytes 786440 | tf_op jit(solution)/shard_map/ppermute | solution.py:520
  27.3 11.8 %collective-permute-start.15 = (bf16[256,512]{1,0:T(8,128)(2,1)S(1)}, bf16[256,512]{1,0:T(8,128)(2,1)S(1)}, u32[]{:S(2)}, u32[]{:S(2)}) collective-permute-start(bf16[256,512]{1,0:T(8,128)(2,1)S(1)} %copy-done.36), channel_id=1, source_target_pairs={{0,3},{1,0},{2,1},{3,2},{4,7},{5,4},{6,5},{7,6},{8,11},{9,8},{10,9... | collective-permute-start | bytes 786440 | tf_op jit(solution)/shard_map/ppermute | solution.py:520
  30.5 9.3 %collective-permute-start.16 = (bf16[256,512]{1,0:T(8,128)(2,1)S(1)}, bf16[256,512]{1,0:T(8,128)(2,1)S(1)}, u32[]{:S(2)}, u32[]{:S(2)}) collective-permute-start(bf16[256,512]{1,0:T(8,128)(2,1)S(1)} %copy-done.35), channel_id=1, source_target_pairs={{0,4},{1,5},{2,6},{3,7},{4,8},{5,9},{6,10},{7,11},{8,12},{9,13},{1... | collective-permute-start | bytes 786440 | tf_op jit(solution)/shard_map/ppermute | solution.py:520
  33.0 12.5 %collective-permute-start.17 = (bf16[256,512]{1,0:T(8,128)(2,1)S(1)}, bf16[256,512]{1,0:T(8,128)(2,1)S(1)}, u32[]{:S(2)}, u32[]{:S(2)}) collective-permute-start(bf16[256,512]{1,0:T(8,128)(2,1)S(1)} %copy-done.34), channel_id=1, source_target_pairs={{0,5},{1,6},{2,7},{3,4},{4,9},{5,10},{6,11},{7,8},{8,13},{9,14},{1... | collective-permute-start | bytes 786440 | tf_op jit(solution)/shard_map/ppermute | solution.py:520
  33.7 15.8 %collective-permute-start.18 = (bf16[256,512]{1,0:T(8,128)(2,1)S(1)}, bf16[256,512]{1,0:T(8,128)(2,1)S(1)}, u32[]{:S(2)}, u32[]{:S(2)}) collective-permute-start(bf16[256,512]{1,0:T(8,128)(2,1)S(1)} %copy-done.33), channel_id=1, source_target_pairs={{0,7},{1,4},{2,5},{3,6},{4,11},{5,8},{6,9},{7,10},{8,15},{9,12},{1... | collective-permute-start | bytes 786440 | tf_op jit(solution)/shard_map/ppermute | solution.py:520
  39.0 17.6 %collective-permute-start.19 = (bf16[256,512]{1,0:T(8,128)(2,1)}, bf16[256,512]{1,0:T(8,128)(2,1)S(1)}, u32[]{:S(2)}, u32[]{:S(2)}) collective-permute-start(bf16[256,512]{1,0:T(8,128)(2,1)} %get-tuple-element.81), channel_id=1, source_target_pairs={{0,12},{1,13},{2,14},{3,15},{4,0},{5,1},{6,2},{7,3},{8,4},{9,5},{1... | collective-permute-start | bytes 786440 | tf_op jit(solution)/shard_map/ppermute | solution.py:520
  39.1 18.3 %collective-permute-start.20 = (bf16[256,512]{1,0:T(8,128)(2,1)}, bf16[256,512]{1,0:T(8,128)(2,1)S(1)}, u32[]{:S(2)}, u32[]{:S(2)}) collective-permute-start(bf16[256,512]{1,0:T(8,128)(2,1)} %get-tuple-element.82), channel_id=1, source_target_pairs={{0,13},{1,14},{2,15},{3,12},{4,1},{5,2},{6,3},{7,0},{8,5},{9,6},{1... | collective-permute-start | bytes 786440 | tf_op jit(solution)/shard_map/ppermute | solution.py:520
  39.8 28.7 %copy-start.1 = (bf16[256,512]{1,0:T(8,128)(2,1)}, bf16[256,512]{1,0:T(8,128)(2,1)S(1)}, u32[]{:S(2)}) copy-start(bf16[256,512]{1,0:T(8,128)(2,1)S(1)} %collective-permute-done.16.refs_9_) | copy-start | bytes 786436
  39.8 17.6 %collective-permute-start.21 = (bf16[256,512]{1,0:T(8,128)(2,1)}, bf16[256,512]{1,0:T(8,128)(2,1)S(1)}, u32[]{:S(2)}, u32[]{:S(2)}) collective-permute-start(bf16[256,512]{1,0:T(8,128)(2,1)} %get-tuple-element.83), channel_id=1, source_target_pairs={{0,15},{1,12},{2,13},{3,14},{4,3},{5,0},{6,1},{7,2},{8,7},{9,4},{1... | collective-permute-start | bytes 786440 | tf_op jit(solution)/shard_map/ppermute | solution.py:520
  45.4 23.1 %copy-start.3 = (bf16[256,512]{1,0:T(8,128)(2,1)}, bf16[256,512]{1,0:T(8,128)(2,1)S(1)}, u32[]{:S(2)}) copy-start(bf16[256,512]{1,0:T(8,128)(2,1)S(1)} %collective-permute-done.17.refs_10_) | copy-start | bytes 786436
  45.4 13.0 %collective-permute-start.1 = (bf16[256,512]{1,0:T(8,128)(2,1)}, bf16[256,512]{1,0:T(8,128)(2,1)S(1)}, u32[]{:S(2)}, u32[]{:S(2)}) collective-permute-start(bf16[256,512]{1,0:T(8,128)(2,1)} %collective-permute-done), channel_id=1, source_target_pairs={{0,1},{1,2},{2,3},{3,0},{4,5},{5,6},{6,7},{7,4},{8,9},{9,10},{10,1... | collective-permute-start | bytes 786440 | tf_op jit(solution)/shard_map/ppermute | solution.py:520
  49.4 19.1 %copy-start.5 = (bf16[256,512]{1,0:T(8,128)(2,1)}, bf16[256,512]{1,0:T(8,128)(2,1)S(1)}, u32[]{:S(2)}) copy-start(bf16[256,512]{1,0:T(8,128)(2,1)S(1)} %collective-permute-done.18.refs_11_) | copy-start | bytes 786436
  49.4 12.2 %collective-permute-start.3 = (bf16[256,512]{1,0:T(8,128)(2,1)}, bf16[256,512]{1,0:T(8,128)(2,1)S(1)}, u32[]{:S(2)}, u32[]{:S(2)}) collective-permute-start(bf16[256,512]{1,0:T(8,128)(2,1)} %collective-permute-done.2), channel_id=1, source_target_pairs={{0,7},{1,4},{2,5},{3,6},{4,11},{5,8},{6,9},{7,10},{8,15},{9,12},{1... | collective-permute-start | bytes 786440 | tf_op jit(solution)/shard_map/ppermute | solution.py:520
  56.6 19.3 %collective-permute-start.5 = (bf16[256,512]{1,0:T(8,128)(2,1)}, bf16[256,512]{1,0:T(8,128)(2,1)}, u32[]{:S(2)}, u32[]{:S(2)}) collective-permute-start(bf16[256,512]{1,0:T(8,128)(2,1)} %copy-done.28), channel_id=1, source_target_pairs={{0,4},{1,5},{2,6},{3,7},{4,8},{5,9},{6,10},{7,11},{8,12},{9,13},{1... | collective-permute-start | bytes 786440 | tf_op jit(solution)/shard_map/ppermute | solution.py:520
  57.4 18.5 %collective-permute-start.7 = (bf16[256,512]{1,0:T(8,128)(2,1)}, bf16[256,512]{1,0:T(8,128)(2,1)}, u32[]{:S(2)}, u32[]{:S(2)}) collective-permute-start(bf16[256,512]{1,0:T(8,128)(2,1)} %copy-done.29), channel_id=1, source_target_pairs={{0,13},{1,14},{2,15},{3,12},{4,1},{5,2},{6,3},{7,0},{8,5},{9,6},{1... | collective-permute-start | bytes 786440 | tf_op jit(solution)/shard_map/ppermute | solution.py:520
  57.4 18.5 %collective-permute-start.9 = (bf16[256,512]{1,0:T(8,128)(2,1)}, bf16[256,512]{1,0:T(8,128)(2,1)}, u32[]{:S(2)}, u32[]{:S(2)}) collective-permute-start(bf16[256,512]{1,0:T(8,128)(2,1)} %copy-done.30), channel_id=1, source_target_pairs={{0,13},{1,14},{2,15},{3,12},{4,1},{5,2},{6,3},{7,0},{8,5},{9,6},{1... | collective-permute-start | bytes 786440 | tf_op jit(solution)/shard_map/ppermute | solution.py:520
  58.4 17.5 %collective-permute-start.11 = (bf16[256,512]{1,0:T(8,128)(2,1)}, bf16[256,512]{1,0:T(8,128)(2,1)}, u32[]{:S(2)}, u32[]{:S(2)}) collective-permute-start(bf16[256,512]{1,0:T(8,128)(2,1)} %copy-done.31), channel_id=1, source_target_pairs={{0,7},{1,4},{2,5},{3,6},{4,11},{5,8},{6,9},{7,10},{8,15},{9,12},{1... | collective-permute-start | bytes 786440 | tf_op jit(solution)/shard_map/ppermute | solution.py:520
  62.4 13.6 %collective-permute-start.13 = (bf16[256,512]{1,0:T(8,128)(2,1)}, bf16[256,512]{1,0:T(8,128)(2,1)}, u32[]{:S(2)}, u32[]{:S(2)}) collective-permute-start(bf16[256,512]{1,0:T(8,128)(2,1)} %copy-done.32), channel_id=1, source_target_pairs={{0,15},{1,12},{2,13},{3,14},{4,3},{5,0},{6,1},{7,2},{8,7},{9,4},{1... | collective-permute-start | bytes 786440 | tf_op jit(solution)/shard_map/ppermute | solution.py:520
  89.7 38.5 %all-to-all-start = ((bf16[32,272,128]{2,1,0:T(8,128)(2,1)}), bf16[32,272,128]{2,1,0:T(8,128)(2,1)S(1)}, u32[]{:S(2)}, u32[]{:S(2)}) async-start(bf16[32,272,128]{2,1,0:T(8,128)(2,1)} %row_warp.1), calls=%async_computation | async-start | bytes 4456448 | tf_op jit(solution)/shard_map/all_to_all | solution.py:551
  107.4 2.1 %collective-permute-start.22 = (f32[8,128]{1,0:T(8,128)S(1)}, f32[8,128]{1,0:T(8,128)S(1)}, u32[]{:S(2)}, u32[]{:S(2)}) collective-permute-start(f32[8,128]{1,0:T(8,128)S(1)} %scatter.6), channel_id=1, source_target_pairs={{0,16},{16,0},{1,17},{17,1},{2,18},{18,2},{3,19},{19,3},{4,20},{20... | collective-permute-start | bytes 12296 | tf_op jit(solution)/shard_map/ppermute | solution.py:621
  129.2 27.4 %collective-permute-start.23 = (f32[8,128]{1,0:T(8,128)S(1)}, f32[8,128]{1,0:T(8,128)S(1)}, u32[]{:S(2)}, u32[]{:S(2)}) collective-permute-start(f32[8,128]{1,0:T(8,128)S(1)} %select_n.607), channel_id=1, source_target_pairs={{0,32},{32,0},{64,96},{96,64},{1,33},{33,1},{65,97},{97,65},{2,34}... | collective-permute-start | bytes 12296 | tf_op jit(solution)/shard_map/ppermute | solution.py:528
  148.6 39.5 %all-to-all-start.1 = ((bf16[128,32,256]{2,1,0:T(8,128)(2,1)}), bf16[128,32,256]{2,1,0:T(8,128)(2,1)S(1)}, u32[]{:S(2)}, u32[]{:S(2)}) async-start(bf16[128,32,256]{2,1,0:T(8,128)(2,1)} %bitcast.80), calls=%async_computation.1 | async-start | bytes 4194304 | tf_op jit(solution)/shard_map/all_to_all | solution.py:551
  156.8 25.5 %collective-permute-start.24 = (f32[8,128]{1,0:T(8,128)S(1)}, f32[8,128]{1,0:T(8,128)S(1)}, u32[]{:S(2)}, u32[]{:S(2)}) collective-permute-start(f32[8,128]{1,0:T(8,128)S(1)} %add.1087), channel_id=1, source_target_pairs={{0,64},{32,96},{64,0},{96,32},{1,65},{33,97},{65,1},{97,33},{2,66}... | collective-permute-start | bytes 12296 | tf_op jit(solution)/shard_map/ppermute | solution.py:528
  (34 other events, 209.6 us)

commit v8 on v7

--- a/solution.py
+++ b/solution.py
@@ -26,8 +26,6 @@
 BLUR_BAND = (112, 400)
 LANES = 128
 TAIL = 16
-LIMIT = 14 * 1024 * 1024
-ROW_LIMIT = 24 * 1024 * 1024
 COL_LIMIT = 56 * 1024 * 1024
 
 
@@ -154,7 +152,7 @@
         ),
         in_specs=[smem, smem, vmem, vmem],
         out_specs=(vmem, vmem),
-        compiler_params=pltpu.CompilerParams(vmem_limit_bytes=LIMIT),
+        compiler_params=pltpu.CompilerParams(vmem_limit_bytes=COL_LIMIT),
         name="row_matrices",
     )(kernel, low, turned, key)
 
@@ -247,13 +245,13 @@
         out_shape=jax.ShapeDtypeStruct(
             (owners, width // LANES * slots * owner_rows + TAIL, LANES), BF16
         ),
-        in_specs=[smem] * 3 + [pl.BlockSpec(memory_space=pl.ANY)] * len(pieces) + [vmem] * 5,
+        in_specs=[smem] * 3 + [pl.BlockSpec(memory_space=pltpu.HBM)] * len(pieces) + [vmem] * 5,
         out_specs=vmem,
         scratch_shapes=[
             pltpu.VMEM((len(pieces) * height, width), BF16),
             pltpu.SemaphoreType.DMA((len(pieces),)),
         ],
-        compiler_params=pltpu.CompilerParams(vmem_limit_bytes=ROW_LIMIT),
+        compiler_params=pltpu.CompilerParams(vmem_limit_bytes=COL_LIMIT),
         cost_estimate=pl.CostEstimate(
             flops=2_000_000_000, bytes_accessed=8 * 1024 * 1024, transcendentals=0
         ),
@@ -415,7 +413,7 @@
         functools.partial(col_body, cols, slots, pixels),
         out_shape=jax.ShapeDtypeStruct((patches, owners, rows, own_cols), BF16),
         grid=(patches,),
-        in_specs=[smem] * 6 + [pl.BlockSpec(memory_space=pl.ANY)] * 4,
+        in_specs=[smem] * 6 + [pl.BlockSpec(memory_space=pltpu.HBM)] * 4,
         out_specs=pl.BlockSpec((1, owners, rows, own_cols), lambda k: (k, 0, 0, 0)),
         scratch_shapes=[
             pltpu.VMEM((exposures, (cols // LANES + 2) * tile_rows, LANES), BF16),
@@ -478,7 +476,7 @@
             pl.BlockSpec(memory_space=pltpu.SMEM),
             pl.BlockSpec(memory_space=pl.ANY),
         ],
-        out_specs=[pl.BlockSpec(memory_space=pl.ANY)] * total,
+        out_specs=[pl.BlockSpec(memory_space=pltpu.HBM)] * total,
         scratch_shapes=[
             pltpu.VMEM((total,) + shape, image.dtype),
             pltpu.SemaphoreType.DMA((total,)),
@@ -554,11 +552,10 @@
     targets = jnp.stack([shifted(region_at, shift, regions) for shift in shifts])
     sources = jnp.stack([shifted(region_at, (-dx, -dz), regions) for dx, dz in shifts])
     sent = split_columns(image, targets.astype(jnp.int32), parts)
-    (first, variance, psf_coef, row_start, row_frac, col_start, col_frac) = lax.optimization_barrier(
-        (sent[0], variance, psf_coef, row_start, row_frac, col_start, col_frac)
+    first, variance, psf_coef, row_start, row_frac = lax.optimization_barrier(
+        (sent[0], variance, psf_coef, row_start, row_frac)
     )
     sent = [first] + list(sent[1:])
-    columns = [send_shifted(x, shift, regions) for x, shift in zip(sent, shifts)]
 
     kernels = psf_kernel(psf_coef)
 
@@ -576,6 +573,13 @@
         lax.dynamic_slice_in_dim(kernels, own_exp, 1, 0), row_low, row_turned, row_key, extent
     )
 
+    late = min(4, regions - 1)
+    *held_back, row_matrices = lax.optimization_barrier(
+        (*sent[regions - 1 - late : regions - 1], row_matrices)
+    )
+    sent[regions - 1 - late : regions - 1] = held_back
+    columns = [send_shifted(x, shift, regions) for x, shift in zip(sent, shifts)]
+
     rest = jnp.sum(variance.astype(F32), axis=(1, 2))
     sum_parts = []
     for _ in range(3):
@@ -586,6 +590,22 @@
     pair_exp = cores * exp_dev
     first_exp = pair_at * pair_exp
 
+    warped = row_warp(
+        columns, sources.astype(jnp.int32), row_low, row_num, row_matrices, row_blur, row_turned,
+        row_key, tail, slots, cores * regions,
+    )
+    psf_tile = jnp.zeros((8, LANES), F32).at[:exp_dev, : 2 * RADIUS + 1].set(kernels)
+    psf_tile, warped, col_start, col_frac, correlations = lax.optimization_barrier(
+        (psf_tile, warped, col_start, col_frac, correlations)
+    )
+    rows = exchange(warped, ("core", "region"))
+    other = lax.ppermute(psf_tile, "core", [(i, i ^ 1) for i in range(cores)])
+    other = other[:exp_dev, : 2 * RADIUS + 1]
+    col_blur = make_col_matrices(
+        jnp.concatenate(
+            [jnp.where(core_at == 0, kernels, other), jnp.where(core_at == 0, other, kernels)]
+        )
+    )
     slot_total = pair_exp * slots
     col_blocks = patch_cols // COL_BLOCK
     own_starts = lax.dynamic_slice_in_dim(col_start, first_exp, pair_exp, 0)
@@ -611,20 +631,6 @@
         axis=2,
     )
 
-    warped = row_warp(
-        columns, sources.astype(jnp.int32), row_low, row_num, row_matrices, row_blur, row_turned, row_key, tail, slots,
-        cores * regions,
-    )
-    psf_tile = jnp.zeros((8, LANES), F32).at[:exp_dev, : 2 * RADIUS + 1].set(kernels)
-    psf_tile, warped = lax.optimization_barrier((psf_tile, warped))
-    rows = exchange(warped, ("core", "region"))
-    other = lax.ppermute(psf_tile, "core", [(i, i ^ 1) for i in range(cores)])
-    other = other[:exp_dev, : 2 * RADIUS + 1]
-    col_blur = make_col_matrices(
-        jnp.concatenate(
-            [jnp.where(core_at == 0, kernels, other), jnp.where(core_at == 0, other, kernels)]
-        )
-    )
     partial = col_warp(
         rows, count, listed, col_low, col_num, col_from, col_to, col_blur, col_turned, col_key,
         width, slots, visits, regions, extent * width,
@@ -657,6 +663,7 @@
         ),
         width,
     )
+    row_cover, col_cover = lax.optimization_barrier((row_cover, col_cover))
     scale = jnp.where(
         correlations.reshape(total_slots) == visit_at, jnp.repeat(weight, slots), 0.0
     )

time: 190 us -> 195 us (1.026)
  local copies, waits for them, and re-layouts: 22.4 us -> 15.6 us
  starting transfers between devices: 61.2 us -> 66.2 us
  waiting for transfers between devices: 30.5 us -> 34.2 us
  Pallas kernels: 38.8 us -> 42.2 us
    unnamed x80 -> x46, local copies, waits for them, and re-layouts: 11.9 us -> 1.34 us
    and x0 -> x12, local copies, waits for them, and re-layouts: none -> 7.25 us  [coverage(): inside = (position >= 0) & (position < extent)]
    add x1 -> x2, other arithmetic: 10.2 us -> 3.87 us  [coverage(): running = running + jnp.where(inside, tap, 0.0)]
    ppermute x22, waiting for transfers between devices: 4.15 us -> 8.51 us  [send_shifted(): lax.ppermute(x, 'region', [(i, shifted(i, step, regions)) for i in range(...]
    ppermute x22, starting transfers between devices: 39.6 us -> 43.3 us  [send_shifted(): lax.ppermute(x, 'region', [(i, shifted(i, step, regions)) for i in range(...]
    mul x1 -> x0, other arithmetic: 3.36 us -> none  [local(): col_cover * scale[:, None]]
    and x0 -> x2, other arithmetic: none -> 3.26 us  [coverage(): inside = (position >= 0) & (position < extent)]
    pallas_call x1, Pallas kernels: 6.12 us -> 8.17 us  [row_warp(): pl.pallas_call(functools.partial(row_body, slots, len(pieces)), out_shape...]
  transfers between devices with their start and end apart: 27 -> 27, of which waited for: 5 -> 8; matrix products, arithmetic and copies ran while one was open for 23% -> 23% of each run, Pallas kernels for 15% -> 6%
where the time goes in v8:
time: 195 us; the launch traced here: 194 us
  starting transfers between devices  66.2 us (34%)
  Pallas kernels  42.2 us (22%)
  waiting for transfers between devices  34.2 us (18%)
  other arithmetic  31.6 us (16%)
  local copies, waits for them, and re-layouts  15.6 us (8%)
  matrix products  2.02 us (1%)
  between operations  2.01 us (1%)
    ppermute x22, starting transfers between devices, send_shifted(): lax.ppermute(x, 'region', [(i, shifted(i, step, regions)) for i in range(...  43.3 us
    all_to_all x2, starting transfers between devices, exchange(): return lax.all_to_all(x, axis, split_axis=0, concat_axis=0, tiled=True)  18.5 us
    pallas_call x1, Pallas kernels, col_warp(): pl.pallas_call(functools.partial(col_body, cols, slots, pixels), out_shap...  17.2 us
    all_to_all x2, waiting for transfers between devices, exchange(): return lax.all_to_all(x, axis, split_axis=0, concat_axis=0, tiled=True)  13 us
    ppermute x2, waiting for transfers between devices, butterfly_sum(): x = x + lax.ppermute(x, axis, [(i, i ^ step) for i in range(size)])  12.7 us
    ppermute x22, waiting for transfers between devices, send_shifted(): lax.ppermute(x, 'region', [(i, shifted(i, step, regions)) for i in range(...  8.51 us
    pallas_call x1, Pallas kernels, make_row_matrices(): pl.pallas_call(functools.partial(row_matrices_body, extent), out_shape=(j...  8.26 us
    pallas_call x1, Pallas kernels, row_warp(): pl.pallas_call(functools.partial(row_body, slots, len(pieces)), out_shape...  8.17 us
  transfers between devices with their start and end apart: 27, of which 8 were waited for; matrix products, arithmetic and copies ran while one was open for 23% of the time, Pallas kernels for 6%

profile of v8, /device:TPU:4, one launch (start us, length us, event | category | flops | bytes accessed | tf_op | source)
XLA Modules:
  0.0 193.9 jit_solution(3906590550494305783)
XLA Ops:
  1.5 4.8 %split_columns.1 = (bf16[256,512]{1,0:T(8,128)(2,1)}, bf16[256,512]{1,0:T(8,128)(2,1)}, bf16[256,512]{1,0:T(8,128)(2,1)}, bf16[256,512]{1,0:T(8,128)(2,1)}, bf16...) custom-call(s32[16]{0:T(128)} %stack.116.to_ref, ...), custom_call_target="tpu_custom_call" | custom-call | tf_op jit(solution)/shard_map/split_columns/pallas_call | solution.py:472
  6.3 2.0 %collective-permute-start = (bf16[256,512]{1,0:T(8,128)(2,1)}, bf16[256,512]{1,0:T(8,128)(2,1)}, u32[]{:S(2)}, u32[]{:S(2)}) collective-permute-start(bf16[256,512]{1,0:T(8,128)(2,1)} %get-tuple-element.76), channel_id=1, source_target_pairs={{0,1},{1,2},{2,3},{3,0},{4,5},{5,6},{6,7},{7,4},{8,9},{9,10},{10,1... | collective-permute-start | bytes 786440 | tf_op jit(solution)/shard_map/ppermute | solution.py:518
  8.3 2.2 %collective-permute-start.2 = (bf16[256,512]{1,0:T(8,128)(2,1)}, bf16[256,512]{1,0:T(8,128)(2,1)}, u32[]{:S(2)}, u32[]{:S(2)}) collective-permute-start(bf16[256,512]{1,0:T(8,128)(2,1)} %get-tuple-element.77), channel_id=1, source_target_pairs={{0,3},{1,0},{2,1},{3,2},{4,7},{5,4},{6,5},{7,6},{8,11},{9,8},{10,9... | collective-permute-start | bytes 786440 | tf_op jit(solution)/shard_map/ppermute | solution.py:518
  16.5 2.5 %select_add_fusion.1 = f32[64,1024]{1,0:T(8,128)S(1)} fusion(pred[64,1024]{1,0:T(8,128)(4,1)S(1)} %and.345, pred[64,1024]{1,0:T(8,128)(4,1)S(1)} %and.343, pred[64,1024]{1,0:T(8,128)(4,1)S(1)} %and.341, pred[64,1024]{1,0:T(8,128)(4,1)S(1)} %and.339, pred[64,1024]{1,0:T(8,128)(4,1)S(1)} %and.337, pred[64,1024]{1,0:T(8,128)(4,1)S(1)} %and.335, ...), kind=kLoop, calls=%fused_computation.36 | loop fusion | flops 4128768 | bytes 917504 | tf_op jit(solution)/shard_map/add | solution.py:69
  21.1 3.4 %collective-permute-start.12 = (bf16[256,512]{1,0:T(8,128)(2,1)}, bf16[256,512]{1,0:T(8,128)(2,1)}, u32[]{:S(2)}, u32[]{:S(2)}) collective-permute-start(bf16[256,512]{1,0:T(8,128)(2,1)} %get-tuple-element.82), channel_id=1, source_target_pairs={{0,3},{1,0},{2,1},{3,2},{4,7},{5,4},{6,5},{7,6},{8,11},{9,8},{10,9... | collective-permute-start | bytes 786440 | tf_op jit(solution)/shard_map/ppermute | solution.py:518
  25.6 8.3 %row_matrices.1 = (bf16[16,256,256]{2,1,0:T(8,128)(2,1)}, bf16[512,288]{1,0:T(8,128)(2,1)}) custom-call(f32[1,21]{1,0:T(1,128)} %constant_dynamic-slice_fusion.6.kernel_ref, s32[16]{0:T(128)} %get-tuple-element.123.low_ref, f32[16,8,128]{2,1,0:T(8,128)} %select_add_fusion.3.turned_ref.refs_18_, s32[16,8,128]{2,1,0:T(8,128)} %and_subtract_fusion.1.key_ref.refs_19_), custom_call_target="tpu_custom_call" | custom-call | tf_op jit(solution)/shard_map/row_matrices/pallas_call | solution.py:147
  34.0 3.2 %collective-permute-start.15 = (bf16[256,512]{1,0:T(8,128)(2,1)}, bf16[256,512]{1,0:T(8,128)(2,1)S(1)}, u32[]{:S(2)}, u32[]{:S(2)}) collective-permute-start(bf16[256,512]{1,0:T(8,128)(2,1)} %get-tuple-element.84), channel_id=1, source_target_pairs={{0,3},{1,0},{2,1},{3,2},{4,7},{5,4},{6,5},{7,6},{8,11},{9,8},{10,9... | collective-permute-start | bytes 786440 | tf_op jit(solution)/shard_map/ppermute | solution.py:518
  37.2 2.4 %collective-permute-start.16 = (bf16[256,512]{1,0:T(8,128)(2,1)}, bf16[256,512]{1,0:T(8,128)(2,1)S(1)}, u32[]{:S(2)}, u32[]{:S(2)}) collective-permute-start(bf16[256,512]{1,0:T(8,128)(2,1)} %get-tuple-element.85), channel_id=1, source_target_pairs={{0,4},{1,5},{2,6},{3,7},{4,8},{5,9},{6,10},{7,11},{8,12},{9,13},{1... | collective-permute-start | bytes 786440 | tf_op jit(solution)/shard_map/ppermute | solution.py:518
  39.7 2.8 %collective-permute-start.18 = (bf16[256,512]{1,0:T(8,128)(2,1)}, bf16[256,512]{1,0:T(8,128)(2,1)S(1)}, u32[]{:S(2)}, u32[]{:S(2)}) collective-permute-start(bf16[256,512]{1,0:T(8,128)(2,1)} %get-tuple-element.93), channel_id=1, source_target_pairs={{0,7},{1,4},{2,5},{3,6},{4,11},{5,8},{6,9},{7,10},{8,15},{9,12},{1... | collective-permute-start | bytes 786440 | tf_op jit(solution)/shard_map/ppermute | solution.py:518
  42.5 2.9 %convert_reduce_fusion = f32[4]{0:T(128)S(1)} fusion(bf16[4,256,2048]{2,1,0:T(8,128)(2,1)} %param.16), kind=kLoop, calls=%fused_computation | loop fusion | flops 4194300 | bytes 4194320 | tf_op jit(solution)/shard_map/reduce_sum | solution.py:583
  45.4 1.8 collective-permute-start.19
  47.4 4.5 %collective-permute-start.21 = (bf16[256,512]{1,0:T(8,128)(2,1)S(1)}, bf16[256,512]{1,0:T(8,128)(2,1)S(1)}, u32[]{:S(2)}, u32[]{:S(2)}) collective-permute-start(bf16[256,512]{1,0:T(8,128)(2,1)S(1)} %copy-done.19), channel_id=1, source_target_pairs={{0,15},{1,12},{2,13},{3,14},{4,3},{5,0},{6,1},{7,2},{8,7},{9,4},{1... | collective-permute-start | bytes 786440 | tf_op jit(solution)/shard_map/ppermute | solution.py:518
  52.1 2.1 %collective-permute-start.1 = (bf16[256,512]{1,0:T(8,128)(2,1)}, bf16[256,512]{1,0:T(8,128)(2,1)}, u32[]{:S(2)}, u32[]{:S(2)}) collective-permute-start(bf16[256,512]{1,0:T(8,128)(2,1)} %collective-permute-done), channel_id=1, source_target_pairs={{0,1},{1,2},{2,3},{3,0},{4,5},{5,6},{6,7},{7,4},{8,9},{9,10},{10,1... | collective-permute-start | bytes 786440 | tf_op jit(solution)/shard_map/ppermute | solution.py:518
  55.9 5.3 %collective-permute-start.3 = (bf16[256,512]{1,0:T(8,128)(2,1)}, bf16[256,512]{1,0:T(8,128)(2,1)}, u32[]{:S(2)}, u32[]{:S(2)}) collective-permute-start(bf16[256,512]{1,0:T(8,128)(2,1)} %collective-permute-done.2), channel_id=1, source_target_pairs={{0,7},{1,4},{2,5},{3,6},{4,11},{5,8},{6,9},{7,10},{8,15},{9,12},{1... | collective-permute-start | bytes 786440 | tf_op jit(solution)/shard_map/ppermute | solution.py:518
  62.9 2.2 %collective-permute-done.21.refs_14_ = bf16[256,512]{1,0:T(8,128)(2,1)S(1)} collective-permute-done((bf16[256,512]{1,0:T(8,128)(2,1)S(1)}, bf16[256,512]{1,0:T(8,128)(2,1)S(1)}, u32[]{:S(2)}, u32[]{:S(2)}) %collective-permute-start.21) | collective-permute-done | bytes 262176 | tf_op jit(solution)/shard_map/ppermute | solution.py:518
  65.1 6.5 %collective-permute-start.11 = (bf16[256,512]{1,0:T(8,128)(2,1)}, bf16[256,512]{1,0:T(8,128)(2,1)}, u32[]{:S(2)}, u32[]{:S(2)}) collective-permute-start(bf16[256,512]{1,0:T(8,128)(2,1)} %collective-permute-done.10), channel_id=1, source_target_pairs={{0,7},{1,4},{2,5},{3,6},{4,11},{5,8},{6,9},{7,10},{8,15},{9,12},{1... | collective-permute-start | bytes 786440 | tf_op jit(solution)/shard_map/ppermute | solution.py:518
  71.6 1.8 collective-permute-start.13
  74.8 2.6 %collective-permute-done.9.refs_4_ = bf16[256,512]{1,0:T(8,128)(2,1)} collective-permute-done((bf16[256,512]{1,0:T(8,128)(2,1)}, bf16[256,512]{1,0:T(8,128)(2,1)}, u32[]{:S(2)}, u32[]{:S(2)}) %collective-permute-start.9) | collective-permute-done | bytes 262176 | tf_op jit(solution)/shard_map/ppermute | solution.py:518
  77.4 1.8 collective-permute-done.13.refs_6_
  79.3 8.2 %row_warp.1 = bf16[32,272,128]{2,1,0:T(8,128)(2,1)} custom-call(s32[16]{0:T(128)} %get-tuple-element.123.low_ref, s32[16]{0:T(128)} %get-tuple-element.122.num_ref, s32[16]{0:T(128)} %stack.132.from_ref, bf16[256,512]{1,0:T(8,128)(2,1)} %collective-permute-done.1.refs_0_, bf16[256,512]{1,0:T(8,128)(2,1)} %collective-permute-done.3.refs_1_, ...), custom_call_target="tpu_custom_call" | custom-call | flops 2000000000 | bytes 8388608 | tf_op jit(solution)/shard_map/row_warp/pallas_call | solution.py:243
  89.4 10.0 %all-to-all-start = ((bf16[32,272,128]{2,1,0:T(8,128)(2,1)}), bf16[32,272,128]{2,1,0:T(8,128)(2,1)}, u32[]{:S(2)}, u32[]{:S(2)}) async-start(bf16[32,272,128]{2,1,0:T(8,128)(2,1)} %row_warp.1), calls=%async_computation | async-start | bytes 4456448 | tf_op jit(solution)/shard_map/all_to_all | solution.py:549
  103.8 2.1 %divide_reduce-precision_fusion.5 = (f32[16,32,128]{2,1,0:T(8,128)S(1)}, f32[16,32,128]{2,1,0:T(8,128)S(1)}) fusion(f32[16,32,128]{2,1,0:T(8,128)S(1)} %reshape.721), kind=kLoop, calls=%fused_computation.46 | loop fusion | flops 2555904 | bytes 786432 | tf_op jit(solution)/shard_map/reduce_precision | solution.py:61
  105.9 2.1 %divide_reduce-precision_fusion.4 = (f32[16,32,128]{2,1,0:T(8,128)S(1)}, f32[16,32,128]{2,1,0:T(8,128)S(1)}, f32[16,32,128]{2,1,0:T(8,128)S(1)}, f32[16,32,128]{2,1,0:T(8,128)S(1)}, f32[16,32,128]{2,1,0:T(8,128)S(1)}) fusion(f32[16,32,128]{2,1,0:T(8,128)S(1)} %get-tuple-element.117, f32[16,32,128]{2,1,0:T(8,128)S(1)} %reshape.721), kind=kLoop, calls=%fused_computation.45 | loop fusion | flops 2424832 | bytes 1835008 | tf_op jit(solution)/shard_map/reduce_precision | solution.py:61
  108.0 2.6 %select_add_fusion.turned_hbm = f32[16,32,8,128]{3,2,1,0:T(8,128)} fusion(f32[16,32,128]{2,1,0:T(8,128)S(1)} %get-tuple-element.134, f32[16,32,128]{2,1,0:T(8,128)S(1)} %get-tuple-element.131, f32[16,32,128]{2,1,0:T(8,128)S(1)} %get-tuple-element.132, f32[16,32,128]{2,1,0:T(8,128)S(1)} %get-tuple-element.133, f32[16,32,128]{2,1,0:T(8,128)S(1)} %get-tuple-element.130, ...), kind=kLoop, calls=%fused_computation.9 | loop fusion | flops 9961472 | bytes 3932160 | tf_op jit(solution)/shard_map/add | solution.py:79
  112.4 3.9 %col_matrices.1.blur_hbm = bf16[8,2,288,256]{3,2,1,0:T(8,128)(2,1)} custom-call(f32[8,21]{1,0:T(8,128)} %pad_maximum_fusion.kernel_ref), custom_call_target="tpu_custom_call" | custom-call | tf_op jit(solution)/shard_map/col_matrices/pallas_call | solution.py:171
  116.3 13.0 %all-to-all-done.z_hbm = bf16[32,272,128]{2,1,0:T(8,128)(2,1)} async-done(((bf16[32,272,128]{2,1,0:T(8,128)(2,1)}), bf16[32,272,128]{2,1,0:T(8,128)(2,1)}, u32[]{:S(2)}, u32[]{:S(2)}) %all-to-all-start) | async-done | bytes 2228256 | tf_op jit(solution)/shard_map/all_to_all | solution.py:549
  129.3 17.2 %col_warp.1 = bf16[8,16,32,256]{3,2,1,0:T(8,128)(2,1)} custom-call(s32[8]{0:T(128)} %fusion.45.count_ref, s32[8,16]{1,0:T(8,128)} %select_reduce_fusion.list_ref, s32[16,32]{1,0:T(8,128)} %get-tuple-element.155.low_ref, s32[16,32]{1,0:T(8,128)} %get-tuple-element.119.num_ref, s32[16]{0:T(128)} %min.46.from_ref, s32[16]{0:T(128)} %copy-done.15, ...), custom_call_target="tpu_custom_call" | custom-call | flops 8000000000 | bytes 16777216 | tf_op jit(solution)/shard_map/col_warp/pallas_call | solution.py:412
  146.4 8.4 %all-to-all-start.1 = ((bf16[128,32,256]{2,1,0:T(8,128)(2,1)}), bf16[128,32,256]{2,1,0:T(8,128)(2,1)S(1)}, u32[]{:S(2)}, u32[]{:S(2)}) async-start(bf16[128,32,256]{2,1,0:T(8,128)(2,1)} %bitcast.75), calls=%async_computation.1 | async-start | bytes 4194304 | tf_op jit(solution)/shard_map/all_to_all | solution.py:549
  155.7 1.8 compare_and_fusion.11
  167.8 11.6 %collective-permute-done.23 = f32[8,128]{1,0:T(8,128)} collective-permute-done((f32[8,128]{1,0:T(8,128)}, f32[8,128]{1,0:T(8,128)}, u32[]{:S(2)}, u32[]{:S(2)}) %collective-permute-start.23) | collective-permute-done | bytes 4128 | tf_op jit(solution)/shard_map/ppermute | solution.py:526
  181.3 2.7 %collective-permute-start.24 = (f32[8,128]{1,0:T(8,128)}, f32[8,128]{1,0:T(8,128)S(1)}, u32[]{:S(2)}, u32[]{:S(2)}) collective-permute-start(f32[8,128]{1,0:T(8,128)} %add.1061), channel_id=1, source_target_pairs={{0,64},{32,96},{64,0},{96,32},{1,65},{33,97},{65,1},{97,33},{2,66}... | collective-permute-start | bytes 12296 | tf_op jit(solution)/shard_map/ppermute | solution.py:526
  189.6 2.0 %fusion.18 = f32[1024,256]{1,0:T(8,128)} fusion(f32[64,1024]{1,0:T(8,128)S(1)} %select_add_fusion.1, f32[64,256]{1,0:T(8,128)S(1)} %select_add_fusion.2, f32[64]{0:T(128)S(1)} %select_n.597), kind=kOutput, calls=%fused_computation.78 | convolution fusion | flops 201342976 | bytes 1376512 | tf_op jit(solution)/shard_map/dot_general | solution.py:670
  (162 shorter events, 43.2 us)
Async XLA Ops:
  0.6 99.1 %copy-start = (f32[32,2,4096]{2,1,0:T(2,128)S(1)}, f32[32,2,4096]{2,1,0:T(2,128)}, u32[]{:S(2)}) copy-start(f32[32,2,4096]{2,1,0:T(2,128)} %param.22) | copy-start | bytes 3145732
  6.3 13.5 %collective-permute-start = (bf16[256,512]{1,0:T(8,128)(2,1)}, bf16[256,512]{1,0:T(8,128)(2,1)}, u32[]{:S(2)}, u32[]{:S(2)}) collective-permute-start(bf16[256,512]{1,0:T(8,128)(2,1)} %get-tuple-element.76), channel_id=1, source_target_pairs={{0,1},{1,2},{2,3},{3,0},{4,5},{5,6},{6,7},{7,4},{8,9},{9,10},{10,1... | collective-permute-start | bytes 786440 | tf_op jit(solution)/shard_map/ppermute | solution.py:518
  8.3 12.8 %collective-permute-start.2 = (bf16[256,512]{1,0:T(8,128)(2,1)}, bf16[256,512]{1,0:T(8,128)(2,1)}, u32[]{:S(2)}, u32[]{:S(2)}) collective-permute-start(bf16[256,512]{1,0:T(8,128)(2,1)} %get-tuple-element.77), channel_id=1, source_target_pairs={{0,3},{1,0},{2,1},{3,2},{4,7},{5,4},{6,5},{7,6},{8,11},{9,8},{10,9... | collective-permute-start | bytes 786440 | tf_op jit(solution)/shard_map/ppermute | solution.py:518
  10.5 23.4 %collective-permute-start.4 = (bf16[256,512]{1,0:T(8,128)(2,1)}, bf16[256,512]{1,0:T(8,128)(2,1)S(1)}, u32[]{:S(2)}, u32[]{:S(2)}) collective-permute-start(bf16[256,512]{1,0:T(8,128)(2,1)} %get-tuple-element.78), channel_id=1, source_target_pairs={{0,4},{1,5},{2,6},{3,7},{4,8},{5,9},{6,10},{7,11},{8,12},{9,13},{1... | collective-permute-start | bytes 786440 | tf_op jit(solution)/shard_map/ppermute | solution.py:518
  11.7 22.3 %collective-permute-start.6 = (bf16[256,512]{1,0:T(8,128)(2,1)}, bf16[256,512]{1,0:T(8,128)(2,1)S(1)}, u32[]{:S(2)}, u32[]{:S(2)}) collective-permute-start(bf16[256,512]{1,0:T(8,128)(2,1)} %get-tuple-element.79), channel_id=1, source_target_pairs={{0,12},{1,13},{2,14},{3,15},{4,0},{5,1},{6,2},{7,3},{8,4},{9,5},{1... | collective-permute-start | bytes 786440 | tf_op jit(solution)/shard_map/ppermute | solution.py:518
  12.5 24.7 %collective-permute-start.8 = (bf16[256,512]{1,0:T(8,128)(2,1)}, bf16[256,512]{1,0:T(8,128)(2,1)}, u32[]{:S(2)}, u32[]{:S(2)}) collective-permute-start(bf16[256,512]{1,0:T(8,128)(2,1)} %get-tuple-element.80), channel_id=1, source_target_pairs={{0,13},{1,14},{2,15},{3,12},{4,1},{5,2},{6,3},{7,0},{8,5},{9,6},{1... | collective-permute-start | bytes 786440 | tf_op jit(solution)/shard_map/ppermute | solution.py:518
  19.8 19.8 %collective-permute-start.10 = (bf16[256,512]{1,0:T(8,128)(2,1)}, bf16[256,512]{1,0:T(8,128)(2,1)}, u32[]{:S(2)}, u32[]{:S(2)}) collective-permute-start(bf16[256,512]{1,0:T(8,128)(2,1)} %get-tuple-element.81), channel_id=1, source_target_pairs={{0,4},{1,5},{2,6},{3,7},{4,8},{5,9},{6,10},{7,11},{8,12},{9,13},{1... | collective-permute-start | bytes 786440 | tf_op jit(solution)/shard_map/ppermute | solution.py:518
  21.1 18.6 %collective-permute-start.12 = (bf16[256,512]{1,0:T(8,128)(2,1)}, bf16[256,512]{1,0:T(8,128)(2,1)}, u32[]{:S(2)}, u32[]{:S(2)}) collective-permute-start(bf16[256,512]{1,0:T(8,128)(2,1)} %get-tuple-element.82), channel_id=1, source_target_pairs={{0,3},{1,0},{2,1},{3,2},{4,7},{5,4},{6,5},{7,6},{8,11},{9,8},{10,9... | collective-permute-start | bytes 786440 | tf_op jit(solution)/shard_map/ppermute | solution.py:518
  33.9 11.6 %collective-permute-start.14 = (bf16[256,512]{1,0:T(8,128)(2,1)}, bf16[256,512]{1,0:T(8,128)(2,1)S(1)}, u32[]{:S(2)}, u32[]{:S(2)}) collective-permute-start(bf16[256,512]{1,0:T(8,128)(2,1)} %get-tuple-element.83), channel_id=1, source_target_pairs={{0,1},{1,2},{2,3},{3,0},{4,5},{5,6},{6,7},{7,4},{8,9},{9,10},{10,1... | collective-permute-start | bytes 786440 | tf_op jit(solution)/shard_map/ppermute | solution.py:518
  34.0 13.3 %collective-permute-start.15 = (bf16[256,512]{1,0:T(8,128)(2,1)}, bf16[256,512]{1,0:T(8,128)(2,1)S(1)}, u32[]{:S(2)}, u32[]{:S(2)}) collective-permute-start(bf16[256,512]{1,0:T(8,128)(2,1)} %get-tuple-element.84), channel_id=1, source_target_pairs={{0,3},{1,0},{2,1},{3,2},{4,7},{5,4},{6,5},{7,6},{8,11},{9,8},{10,9... | collective-permute-start | bytes 786440 | tf_op jit(solution)/shard_map/ppermute | solution.py:518
  37.2 10.2 %collective-permute-start.16 = (bf16[256,512]{1,0:T(8,128)(2,1)}, bf16[256,512]{1,0:T(8,128)(2,1)S(1)}, u32[]{:S(2)}, u32[]{:S(2)}) collective-permute-start(bf16[256,512]{1,0:T(8,128)(2,1)} %get-tuple-element.85), channel_id=1, source_target_pairs={{0,4},{1,5},{2,6},{3,7},{4,8},{5,9},{6,10},{7,11},{8,12},{9,13},{1... | collective-permute-start | bytes 786440 | tf_op jit(solution)/shard_map/ppermute | solution.py:518
  39.6 12.5 %collective-permute-start.17 = (bf16[256,512]{1,0:T(8,128)(2,1)}, bf16[256,512]{1,0:T(8,128)(2,1)S(1)}, u32[]{:S(2)}, u32[]{:S(2)}) collective-permute-start(bf16[256,512]{1,0:T(8,128)(2,1)} %get-tuple-element.86), channel_id=1, source_target_pairs={{0,5},{1,6},{2,7},{3,4},{4,9},{5,10},{6,11},{7,8},{8,13},{9,14},{1... | collective-permute-start | bytes 786440 | tf_op jit(solution)/shard_map/ppermute | solution.py:518
  39.7 16.3 %collective-permute-start.18 = (bf16[256,512]{1,0:T(8,128)(2,1)}, bf16[256,512]{1,0:T(8,128)(2,1)S(1)}, u32[]{:S(2)}, u32[]{:S(2)}) collective-permute-start(bf16[256,512]{1,0:T(8,128)(2,1)} %get-tuple-element.93), channel_id=1, source_target_pairs={{0,7},{1,4},{2,5},{3,6},{4,11},{5,8},{6,9},{7,10},{8,15},{9,12},{1... | collective-permute-start | bytes 786440 | tf_op jit(solution)/shard_map/ppermute | solution.py:518
  45.4 33.8 %copy-start.4 = (bf16[256,512]{1,0:T(8,128)(2,1)}, bf16[256,512]{1,0:T(8,128)(2,1)S(1)}, u32[]{:S(2)}) copy-start(bf16[256,512]{1,0:T(8,128)(2,1)S(1)} %collective-permute-done.14.refs_7_) | copy-start | bytes 786436
  45.4 15.9 %collective-permute-start.19 = (bf16[256,512]{1,0:T(8,128)(2,1)S(1)}, bf16[256,512]{1,0:T(8,128)(2,1)S(1)}, u32[]{:S(2)}, u32[]{:S(2)}) collective-permute-start(bf16[256,512]{1,0:T(8,128)(2,1)S(1)} %copy-done.21), channel_id=1, source_target_pairs={{0,12},{1,13},{2,14},{3,15},{4,0},{5,1},{6,2},{7,3},{8,4},{9,5},{1... | collective-permute-start | bytes 786440 | tf_op jit(solution)/shard_map/ppermute | solution.py:518
  47.3 31.9 %copy-start.5 = (bf16[256,512]{1,0:T(8,128)(2,1)}, bf16[256,512]{1,0:T(8,128)(2,1)S(1)}, u32[]{:S(2)}) copy-start(bf16[256,512]{1,0:T(8,128)(2,1)S(1)} %collective-permute-done.15.refs_8_) | copy-start | bytes 786436
  47.3 14.8 %collective-permute-start.20 = (bf16[256,512]{1,0:T(8,128)(2,1)S(1)}, bf16[256,512]{1,0:T(8,128)(2,1)S(1)}, u32[]{:S(2)}, u32[]{:S(2)}) collective-permute-start(bf16[256,512]{1,0:T(8,128)(2,1)S(1)} %copy-done.20), channel_id=1, source_target_pairs={{0,13},{1,14},{2,15},{3,12},{4,1},{5,2},{6,3},{7,0},{8,5},{9,6},{1... | collective-permute-start | bytes 786440 | tf_op jit(solution)/shard_map/ppermute | solution.py:518
  47.4 31.8 %copy-start.6 = (bf16[256,512]{1,0:T(8,128)(2,1)}, bf16[256,512]{1,0:T(8,128)(2,1)S(1)}, u32[]{:S(2)}) copy-start(bf16[256,512]{1,0:T(8,128)(2,1)S(1)} %collective-permute-done.16.refs_9_) | copy-start | bytes 786436
  47.4 17.7 %collective-permute-start.21 = (bf16[256,512]{1,0:T(8,128)(2,1)S(1)}, bf16[256,512]{1,0:T(8,128)(2,1)S(1)}, u32[]{:S(2)}, u32[]{:S(2)}) collective-permute-start(bf16[256,512]{1,0:T(8,128)(2,1)S(1)} %copy-done.19), channel_id=1, source_target_pairs={{0,15},{1,12},{2,13},{3,14},{4,3},{5,0},{6,1},{7,2},{8,7},{9,4},{1... | collective-permute-start | bytes 786440 | tf_op jit(solution)/shard_map/ppermute | solution.py:518
  52.1 27.1 %copy-start.7 = (bf16[256,512]{1,0:T(8,128)(2,1)}, bf16[256,512]{1,0:T(8,128)(2,1)S(1)}, u32[]{:S(2)}) copy-start(bf16[256,512]{1,0:T(8,128)(2,1)S(1)} %collective-permute-done.17.refs_10_) | copy-start | bytes 786436
  52.1 13.0 %collective-permute-start.1 = (bf16[256,512]{1,0:T(8,128)(2,1)}, bf16[256,512]{1,0:T(8,128)(2,1)}, u32[]{:S(2)}, u32[]{:S(2)}) collective-permute-start(bf16[256,512]{1,0:T(8,128)(2,1)} %collective-permute-done), channel_id=1, source_target_pairs={{0,1},{1,2},{2,3},{3,0},{4,5},{5,6},{6,7},{7,4},{8,9},{9,10},{10,1... | collective-permute-start | bytes 786440 | tf_op jit(solution)/shard_map/ppermute | solution.py:518
  55.9 15.7 %collective-permute-start.3 = (bf16[256,512]{1,0:T(8,128)(2,1)}, bf16[256,512]{1,0:T(8,128)(2,1)}, u32[]{:S(2)}, u32[]{:S(2)}) collective-permute-start(bf16[256,512]{1,0:T(8,128)(2,1)} %collective-permute-done.2), channel_id=1, source_target_pairs={{0,7},{1,4},{2,5},{3,6},{4,11},{5,8},{6,9},{7,10},{8,15},{9,12},{1... | collective-permute-start | bytes 786440 | tf_op jit(solution)/shard_map/ppermute | solution.py:518
  61.3 13.5 %collective-permute-start.5 = (bf16[256,512]{1,0:T(8,128)(2,1)}, bf16[256,512]{1,0:T(8,128)(2,1)}, u32[]{:S(2)}, u32[]{:S(2)}) collective-permute-start(bf16[256,512]{1,0:T(8,128)(2,1)} %copy-done.17), channel_id=1, source_target_pairs={{0,4},{1,5},{2,6},{3,7},{4,8},{5,9},{6,10},{7,11},{8,12},{9,13},{1... | collective-permute-start | bytes 786440 | tf_op jit(solution)/shard_map/ppermute | solution.py:518
  62.1 12.7 %collective-permute-start.7 = (bf16[256,512]{1,0:T(8,128)(2,1)}, bf16[256,512]{1,0:T(8,128)(2,1)}, u32[]{:S(2)}, u32[]{:S(2)}) collective-permute-start(bf16[256,512]{1,0:T(8,128)(2,1)} %copy-done.18), channel_id=1, source_target_pairs={{0,13},{1,14},{2,15},{3,12},{4,1},{5,2},{6,3},{7,0},{8,5},{9,6},{1... | collective-permute-start | bytes 786440 | tf_op jit(solution)/shard_map/ppermute | solution.py:518
  65.1 12.3 %collective-permute-start.9 = (bf16[256,512]{1,0:T(8,128)(2,1)}, bf16[256,512]{1,0:T(8,128)(2,1)}, u32[]{:S(2)}, u32[]{:S(2)}) collective-permute-start(bf16[256,512]{1,0:T(8,128)(2,1)} %collective-permute-done.8), channel_id=1, source_target_pairs={{0,13},{1,14},{2,15},{3,12},{4,1},{5,2},{6,3},{7,0},{8,5},{9,6},{1... | collective-permute-start | bytes 786440 | tf_op jit(solution)/shard_map/ppermute | solution.py:518
  65.1 12.3 %collective-permute-start.11 = (bf16[256,512]{1,0:T(8,128)(2,1)}, bf16[256,512]{1,0:T(8,128)(2,1)}, u32[]{:S(2)}, u32[]{:S(2)}) collective-permute-start(bf16[256,512]{1,0:T(8,128)(2,1)} %collective-permute-done.10), channel_id=1, source_target_pairs={{0,7},{1,4},{2,5},{3,6},{4,11},{5,8},{6,9},{7,10},{8,15},{9,12},{1... | collective-permute-start | bytes 786440 | tf_op jit(solution)/shard_map/ppermute | solution.py:518
  71.6 7.6 %collective-permute-start.13 = (bf16[256,512]{1,0:T(8,128)(2,1)}, bf16[256,512]{1,0:T(8,128)(2,1)}, u32[]{:S(2)}, u32[]{:S(2)}) collective-permute-start(bf16[256,512]{1,0:T(8,128)(2,1)} %collective-permute-done.12), channel_id=1, source_target_pairs={{0,15},{1,12},{2,13},{3,14},{4,3},{5,0},{6,1},{7,2},{8,7},{9,4},{1... | collective-permute-start | bytes 786440 | tf_op jit(solution)/shard_map/ppermute | solution.py:518
  89.4 39.9 %all-to-all-start = ((bf16[32,272,128]{2,1,0:T(8,128)(2,1)}), bf16[32,272,128]{2,1,0:T(8,128)(2,1)}, u32[]{:S(2)}, u32[]{:S(2)}) async-start(bf16[32,272,128]{2,1,0:T(8,128)(2,1)} %row_warp.1), calls=%async_computation | async-start | bytes 4456448 | tf_op jit(solution)/shard_map/all_to_all | solution.py:549
  99.4 12.3 %collective-permute-start.22 = (f32[8,128]{1,0:T(8,128)S(1)}, f32[8,128]{1,0:T(8,128)S(1)}, u32[]{:S(2)}, u32[]{:S(2)}) collective-permute-start(f32[8,128]{1,0:T(8,128)S(1)} %scatter.6), channel_id=1, source_target_pairs={{0,16},{16,0},{1,17},{17,1},{2,18},{18,2},{3,19},{19,3},{4,20},{20... | collective-permute-start | bytes 12296 | tf_op jit(solution)/shard_map/ppermute | solution.py:602
  146.4 45.2 %all-to-all-start.1 = ((bf16[128,32,256]{2,1,0:T(8,128)(2,1)}), bf16[128,32,256]{2,1,0:T(8,128)(2,1)S(1)}, u32[]{:S(2)}, u32[]{:S(2)}) async-start(bf16[128,32,256]{2,1,0:T(8,128)(2,1)} %bitcast.75), calls=%async_computation.1 | async-start | bytes 4194304 | tf_op jit(solution)/shard_map/all_to_all | solution.py:549
  160.0 19.4 %collective-permute-start.23 = (f32[8,128]{1,0:T(8,128)}, f32[8,128]{1,0:T(8,128)}, u32[]{:S(2)}, u32[]{:S(2)}) collective-permute-start(f32[8,128]{1,0:T(8,128)} %select_n.594), channel_id=1, source_target_pairs={{0,32},{32,0},{64,96},{96,64},{1,33},{33,1},{65,97},{97,65},{2,34}... | collective-permute-start | bytes 12296 | tf_op jit(solution)/shard_map/ppermute | solution.py:526
  181.3 5.3 %collective-permute-start.24 = (f32[8,128]{1,0:T(8,128)}, f32[8,128]{1,0:T(8,128)S(1)}, u32[]{:S(2)}, u32[]{:S(2)}) collective-permute-start(f32[8,128]{1,0:T(8,128)} %add.1061), channel_id=1, source_target_pairs={{0,64},{32,96},{64,0},{96,32},{1,65},{33,97},{65,1},{97,33},{2,66}... | collective-permute-start | bytes 12296 | tf_op jit(solution)/shard_map/ppermute | solution.py:526
  (17 other events, 182.0 us)

commit v9 on v6

--- a/solution.py
+++ b/solution.py
@@ -292,7 +292,7 @@
                 blur[e, n, end:BLUR_STEP] = jnp.zeros((BLUR_STEP - end, BLUR_BLOCK), BF16)
             for j in range(slots):
                 blurred[e * slots + j, :, cols : cols + COL_STEP] = jnp.zeros(
-                    (2 * rows, COL_STEP), BF16
+                    (rows, COL_STEP), BF16
                 )
         for e in range(exposures):
             for copy in waits[e]:
@@ -312,13 +312,12 @@
                 ],
                 axis=0,
             )
-            high, rest = two_parts(dot(windows, blur[e, 0]) + dot(windows, blur[e, 1]))
+            matched = (dot(windows, blur[e, 0]) + dot(windows, blur[e, 1])).astype(BF16)
             for b in range(cols // BLUR_BLOCK):
                 for j in range(slots):
                     at = (b * slots + j) * rows
                     span = slice(b * BLUR_BLOCK, (b + 1) * BLUR_BLOCK)
-                    blurred[e * slots + j, 0:rows, span] = high[at : at + rows]
-                    blurred[e * slots + j, rows : 2 * rows, span] = rest[at : at + rows]
+                    blurred[e * slots + j, :, span] = matched[at : at + rows]
         for copy in tables:
             copy.wait()
         sums = jnp.sum(tails[...].astype(F32), axis=1)
@@ -345,7 +344,7 @@
         first = pl.multiple_of(jnp.minimum(low_ref[slot, b] + n * COL_STEP, cols), LANES)
         band = band_of(turned_ref[slot, b], key_ref[slot, b], first, COL_STEP // 8)
         band = jnp.concatenate(band, axis=0).astype(BF16)
-        return halves_sum(dot(blurred[slot, :, pl.ds(first, COL_STEP)], band))
+        return dot(blurred[slot, :, pl.ds(first, COL_STEP)], band)
 
     def add_slot(i, carry):
         slot = list_ref[patch, i]
@@ -404,7 +403,7 @@
             pltpu.VMEM(turned.shape, F32),
             pltpu.VMEM(key.shape, jnp.int32),
             pltpu.VMEM((z.shape[0], TAIL, LANES), BF16),
-            pltpu.VMEM((slot_total, 2 * rows, cols + COL_STEP), BF16),
+            pltpu.VMEM((slot_total, rows, cols + COL_STEP), BF16),
             pltpu.VMEM((rows, owners * own_cols), F32),
             pltpu.SMEM((slot_total,), F32),
             pltpu.SemaphoreType.DMA((exposures, sources)),

time: 185 us -> 184 us (level)
  no operation moved by 1% of the time
where the time goes in v9:
time: 184 us; the launch traced here: 183 us
  waiting for transfers between devices  68.6 us (37%)
  Pallas kernels  37.3 us (20%)
  starting transfers between devices  36 us (20%)
  other arithmetic  33.5 us (18%)
  local copies, waits for them, and re-layouts  5.31 us (3%)
    all_to_all x3, waiting for transfers between devices, exchange(): return lax.all_to_all(x, axis, split_axis=0, concat_axis=0, tiled=True)  56.4 us
    all_to_all x3, starting transfers between devices, exchange(): return lax.all_to_all(x, axis, split_axis=0, concat_axis=0, tiled=True)  30.9 us
    pallas_call x1, Pallas kernels, col_warp(): pl.pallas_call(functools.partial(col_body, cols, slots, pixels), out_shap...  16.6 us
    ppermute x2, waiting for transfers between devices, butterfly_sum(): x = x + lax.ppermute(x, axis, [(i, i ^ step) for i in range(size)])  12.2 us
    add x1, other arithmetic, coverage(): running = running + jnp.where(inside, tap, 0.0)  10.2 us
    pallas_call x1, Pallas kernels, make_row_matrices(): pl.pallas_call(functools.partial(row_matrices_body, extent), out_shape=(j...  6.57 us
    pallas_call x1, Pallas kernels, row_warp(): pl.pallas_call(functools.partial(row_body, slots), out_shape=jax.ShapeDty...  6.36 us
    ppermute x2, starting transfers between devices, butterfly_sum(): x = x + lax.ppermute(x, axis, [(i, i ^ step) for i in range(size)])  4.9 us
  transfers between devices with their start and end apart: 6, of which 3 were waited for; matrix products, arithmetic and copies ran while one was open for 20% of the time, Pallas kernels for 15%

profile of v9, /device:TPU:4, one launch (start us, length us, event | category | flops | bytes accessed | tf_op | source)
XLA Modules:
  0.0 183.4 jit_solution(9660086478769515168)
XLA Ops:
  0.6 4.0 %split_columns.1 = bf16[16,256,512]{2,1,0:T(8,128)(2,1)} custom-call(bf16[4,256,2048]{2,1,0:T(8,128)(2,1)} %image_ref.1), custom_call_target="tpu_custom_call" | custom-call | tf_op jit(solution)/shard_map/split_columns/pallas_call | solution.py:450
  4.6 8.3 %all-to-all-start = ((bf16[16,256,512]{2,1,0:T(8,128)(2,1)}), bf16[16,256,512]{2,1,0:T(8,128)(2,1)}, u32[]{:S(2)}, u32[]{:S(2)}) async-start(bf16[16,256,512]{2,1,0:T(8,128)(2,1)} %split_columns.1), calls=%async_computation | async-start | bytes 8388608 | tf_op jit(solution)/shard_map/all_to_all | solution.py:492
  13.0 1.0 constant_dynamic-slice_fusion.4
  14.3 0.7 constant_dynamic-slice_fusion.3
  15.0 0.7 constant_dynamic-slice_fusion.1
  15.7 1.0 constant_dynamic-slice_fusion
  18.0 2.9 %convert_reduce_fusion = f32[4]{0:T(128)S(1)} fusion(bf16[4,256,2048]{2,1,0:T(8,128)(2,1)} %param.16), kind=kLoop, calls=%fused_computation | loop fusion | flops 4194300 | bytes 4194320 | tf_op jit(solution)/shard_map/reduce_sum | solution.py:516
  21.5 6.6 %row_matrices.1 = (bf16[16,256,256]{2,1,0:T(8,128)(2,1)S(1)}, bf16[512,288]{1,0:T(8,128)(2,1)S(1)}) custom-call(f32[1,21]{1,0:T(1,128)S(1)} %constant_dynamic-slice_fusion.2.kernel_ref, s32[16]{0:T(128)S(1)} %get-tuple-element.73.low_ref, f32[16,8,128]{2,1,0:T(8,128)S(1)} %select_add_fusion.1.turned_ref, s32[16,8,128]{2,1,0:T(8,128)S(1)} %and_subtract_fusion.1.key_ref), custom_call_target="tpu_custom_call" | custom-call | tf_op jit(solution)/shard_map/row_matrices/pallas_call | solution.py:148
  28.2 0.8 select_reduce_fusion.list_ref
  29.1 0.6 broadcast_compare_fusion
  29.7 42.4 %all-to-all-done = bf16[16,256,512]{2,1,0:T(8,128)(2,1)} async-done(((bf16[16,256,512]{2,1,0:T(8,128)(2,1)}), bf16[16,256,512]{2,1,0:T(8,128)(2,1)}, u32[]{:S(2)}, u32[]{:S(2)}) %all-to-all-start) | async-done | bytes 4194336 | tf_op jit(solution)/shard_map/all_to_all | solution.py:492
  72.1 6.4 %row_warp.1 = bf16[32,272,128]{2,1,0:T(8,128)(2,1)} custom-call(s32[16]{0:T(128)S(1)} %get-tuple-element.73.low_ref, s32[16]{0:T(128)S(1)} %get-tuple-element.72.num_ref, bf16[4096,512]{1,0:T(8,128)(2,1)} %bitcast.2.x_ref, bf16[16,256,256]{2,1,0:T(8,128)(2,1)S(1)} %get-tuple-element.54.rows_ref, bf16[512,288]{1,0:T(8,128)(2,1)S(1)} %get-tuple-element.55.blur_ref, ...), custom_call_target="tpu_custom_call" | custom-call | flops 2000000000 | bytes 8388608 | tf_op jit(solution)/shard_map/row_warp/pallas_call | solution.py:230
  78.5 14.1 %all-to-all-start.1 = ((bf16[32,272,128]{2,1,0:T(8,128)(2,1)}), bf16[32,272,128]{2,1,0:T(8,128)(2,1)S(1)}, u32[]{:S(2)}, u32[]{:S(2)}) async-start(bf16[32,272,128]{2,1,0:T(8,128)(2,1)} %row_warp.1), calls=%async_computation.1 | async-start | bytes 4456448 | tf_op jit(solution)/shard_map/all_to_all | solution.py:492
  92.6 0.7 select_reduce_fusion.2
  93.3 1.6 and_subtract_fusion.key_hbm
  94.9 2.1 %divide_reduce-precision_fusion.5 = (f32[16,32,128]{2,1,0:T(8,128)S(1)}, f32[16,32,128]{2,1,0:T(8,128)S(1)}) fusion(f32[16,32,128]{2,1,0:T(8,128)S(1)} %reshape.642), kind=kLoop, calls=%fused_computation.61 | loop fusion | flops 2555904 | bytes 786432 | tf_op jit(solution)/shard_map/reduce_precision | solution.py:62
  97.0 2.1 %divide_reduce-precision_fusion.4 = (f32[16,32,128]{2,1,0:T(8,128)S(1)}, f32[16,32,128]{2,1,0:T(8,128)S(1)}, f32[16,32,128]{2,1,0:T(8,128)S(1)}, f32[16,32,128]{2,1,0:T(8,128)S(1)}, f32[16,32,128]{2,1,0:T(8,128)S(1)}) fusion(f32[16,32,128]{2,1,0:T(8,128)S(1)} %get-tuple-element.69, f32[16,32,128]{2,1,0:T(8,128)S(1)} %reshape.642), kind=kLoop, calls=%fused_computation.60 | loop fusion | flops 2424832 | bytes 1835008 | tf_op jit(solution)/shard_map/reduce_precision | solution.py:62
  99.1 2.6 %select_add_fusion.turned_hbm = f32[16,32,8,128]{3,2,1,0:T(8,128)} fusion(f32[16,32,128]{2,1,0:T(8,128)S(1)} %get-tuple-element.80, f32[16,32,128]{2,1,0:T(8,128)S(1)} %get-tuple-element.77, f32[16,32,128]{2,1,0:T(8,128)S(1)} %get-tuple-element.78, f32[16,32,128]{2,1,0:T(8,128)S(1)} %get-tuple-element.79, f32[16,32,128]{2,1,0:T(8,128)S(1)} %get-tuple-element.76, ...), kind=kLoop, calls=%fused_computation.9 | loop fusion | flops 9961472 | bytes 3932160 | tf_op jit(solution)/shard_map/add | solution.py:80
  101.8 0.7 fusion.52.count_ref
  103.1 0.7 compare_reduce_fusion
  104.5 3.9 %col_matrices.1.blur_hbm = bf16[8,2,288,256]{3,2,1,0:T(8,128)(2,1)} custom-call(f32[8,21]{1,0:T(8,128)} %pad_maximum_fusion.kernel_ref), custom_call_target="tpu_custom_call" | custom-call | tf_op jit(solution)/shard_map/col_matrices/pallas_call | solution.py:172
  108.4 14.0 %all-to-all-done.1.z_hbm = bf16[32,272,128]{2,1,0:T(8,128)(2,1)S(1)} async-done(((bf16[32,272,128]{2,1,0:T(8,128)(2,1)}), bf16[32,272,128]{2,1,0:T(8,128)(2,1)S(1)}, u32[]{:S(2)}, u32[]{:S(2)}) %all-to-all-start.1) | async-done | bytes 2228256 | tf_op jit(solution)/shard_map/all_to_all | solution.py:492
  122.6 0.7 broadcast_select_fusion
  123.4 1.8 collective-permute-start.1
  125.2 16.6 %col_warp.1 = bf16[8,16,32,256]{3,2,1,0:T(8,128)(2,1)} custom-call(s32[8]{0:T(128)} %fusion.52.count_ref, s32[8,16]{1,0:T(8,128)} %select_reduce_fusion.list_ref, s32[16,32]{1,0:T(8,128)} %get-tuple-element.95.low_ref, s32[16,32]{1,0:T(8,128)} %get-tuple-element.75.num_ref, s32[16]{0:T(128)} %min.41.from_ref, s32[16]{0:T(128)} %copy-done.6, ...), custom_call_target="tpu_custom_call" | custom-call | flops 8000000000 | bytes 16777216 | tf_op jit(solution)/shard_map/col_warp/pallas_call | solution.py:394
  141.8 8.5 %all-to-all-start.2 = ((bf16[128,32,256]{2,1,0:T(8,128)(2,1)}), bf16[128,32,256]{2,1,0:T(8,128)(2,1)S(1)}, u32[]{:S(2)}, u32[]{:S(2)}) async-start(bf16[128,32,256]{2,1,0:T(8,128)(2,1)} %bitcast.50), calls=%async_computation.2 | async-start | bytes 4194304 | tf_op jit(solution)/shard_map/all_to_all | solution.py:492
  150.6 3.1 %collective-permute-start.2 = (f32[8,128]{1,0:T(8,128)S(1)}, f32[8,128]{1,0:T(8,128)S(1)}, u32[]{:S(2)}, u32[]{:S(2)}) collective-permute-start(f32[8,128]{1,0:T(8,128)S(1)} %add.736), channel_id=1, source_target_pairs={{0,64},{32,96},{64,0},{96,32},{1,65},{33,97},{65,1},{97,33},{2,66}... | collective-permute-start | bytes 12296 | tf_op jit(solution)/shard_map/ppermute | solution.py:469
  153.7 10.2 %fusion.12 = f32[32,2,1024]{2,1,0:T(2,128)S(1)} fusion(s32[32,2,1024]{2,1,0:T(2,128)S(1)} %copy-done.2, f32[32,2,1024]{2,1,0:T(2,128)S(1)} %copy-done.3), kind=kLoop, calls=%fused_computation.37 | loop fusion | flops 5636096 | bytes 786432 | tf_op jit(solution)/shard_map/add | solution.py:70
  163.8 12.2 %collective-permute-done.2 = f32[8,128]{1,0:T(8,128)S(1)} collective-permute-done((f32[8,128]{1,0:T(8,128)S(1)}, f32[8,128]{1,0:T(8,128)S(1)}, u32[]{:S(2)}, u32[]{:S(2)}) %collective-permute-start.2) | collective-permute-done | bytes 4128 | tf_op jit(solution)/shard_map/ppermute | solution.py:469
  177.5 3.4 %fusion.31 = f32[32,2,256]{2,1,0:T(2,128)S(1)} fusion(f32[32,2,4096]{2,1,0:T(2,128)} %param.22, s32[]{:T(128)S(6)} %select_n.324, s32[32,2,4096]{2,1,0:T(2,128)} %param.21, f32[32,2]{1,0:T(8,128)S(1)} %copy.54), kind=kLoop, calls=%fused_computation.119 | loop fusion | flops 1425408 | bytes 196868 | tf_op jit(solution)/shard_map/mul | solution.py:602
  180.9 1.0 fusion.13
  182.2 1.2 fusion.1
  (72 shorter events, 5.5 us)
Async XLA Ops:
  4.6 67.5 %all-to-all-start = ((bf16[16,256,512]{2,1,0:T(8,128)(2,1)}), bf16[16,256,512]{2,1,0:T(8,128)(2,1)}, u32[]{:S(2)}, u32[]{:S(2)}) async-start(bf16[16,256,512]{2,1,0:T(8,128)(2,1)} %split_columns.1), calls=%async_computation | async-start | bytes 8388608 | tf_op jit(solution)/shard_map/all_to_all | solution.py:492
  12.9 3.8 %copy-start.4 = (s32[32,2]{0,1:T(2,128)S(1)}, s32[32,2]{0,1:T(2,128)}, u32[]{:S(2)}) copy-start(s32[32,2]{0,1:T(2,128)} %param.18) | copy-start | bytes 772
  12.9 4.4 %copy-start.5 = (f32[4,3]{1,0:T(4,128)S(1)}, f32[4,3]{1,0:T(4,128)}, u32[]{:S(2)}) copy-start(f32[4,3]{1,0:T(4,128)} %param.17) | copy-start | bytes 148
  12.9 4.7 %copy-start.7 = (f32[3]{0:T(128)S(1)}, f32[3]{0:T(128)}, u32[]{:S(2)}) copy-start(f32[3]{0:T(128)} %constant.303) | copy-start | bytes 40
  78.5 43.9 %all-to-all-start.1 = ((bf16[32,272,128]{2,1,0:T(8,128)(2,1)}), bf16[32,272,128]{2,1,0:T(8,128)(2,1)S(1)}, u32[]{:S(2)}, u32[]{:S(2)}) async-start(bf16[32,272,128]{2,1,0:T(8,128)(2,1)} %row_warp.1), calls=%async_computation.1 | async-start | bytes 4456448 | tf_op jit(solution)/shard_map/all_to_all | solution.py:492
  93.3 9.2 %copy-start.6 = (s32[16]{0:T(128)}, s32[16]{0:T(128)S(1)}, u32[]{:S(2)}) copy-start(s32[16]{0:T(128)S(1)} %get-tuple-element.64.to_ref) | copy-start | bytes 196
  101.7 2.1 %collective-permute-start = (f32[8,128]{1,0:T(8,128)S(1)}, f32[8,128]{1,0:T(8,128)S(1)}, u32[]{:S(2)}, u32[]{:S(2)}) collective-permute-start(f32[8,128]{1,0:T(8,128)S(1)} %scatter.6), channel_id=1, source_target_pairs={{0,16},{16,0},{1,17},{17,1},{2,18},{18,2},{3,19},{19,3},{4,20},{20... | collective-permute-start | bytes 12296 | tf_op jit(solution)/shard_map/ppermute | solution.py:558
  122.3 2.9 %copy-start.1 = (bf16[32,272,128]{2,1,0:T(8,128)(2,1)}, bf16[32,272,128]{2,1,0:T(8,128)(2,1)S(1)}, u32[]{:S(2)}) copy-start(bf16[32,272,128]{2,1,0:T(8,128)(2,1)S(1)} %all-to-all-done.1.z_hbm) | copy-start | bytes 6684676
  123.4 27.0 %collective-permute-start.1 = (f32[8,128]{1,0:T(8,128)S(1)}, f32[8,128]{1,0:T(8,128)S(1)}, u32[]{:S(2)}, u32[]{:S(2)}) collective-permute-start(f32[8,128]{1,0:T(8,128)S(1)} %select_n.336), channel_id=1, source_target_pairs={{0,32},{32,0},{64,96},{96,64},{1,33},{33,1},{65,97},{97,65},{2,34}... | collective-permute-start | bytes 12296 | tf_op jit(solution)/shard_map/ppermute | solution.py:469
  141.8 11.8 %copy-start.2 = (s32[32,2,1024]{2,1,0:T(2,128)S(1)}, s32[32,2,1024]{2,1,0:T(2,128)}, u32[]{:S(2)}) copy-start(s32[32,2,1024]{2,1,0:T(2,128)} %param.19) | copy-start | bytes 786436
  141.8 11.8 %copy-start.3 = (f32[32,2,1024]{2,1,0:T(2,128)S(1)}, f32[32,2,1024]{2,1,0:T(2,128)}, u32[]{:S(2)}) copy-start(f32[32,2,1024]{2,1,0:T(2,128)} %param.20) | copy-start | bytes 786436
  141.8 40.1 %all-to-all-start.2 = ((bf16[128,32,256]{2,1,0:T(8,128)(2,1)}), bf16[128,32,256]{2,1,0:T(8,128)(2,1)S(1)}, u32[]{:S(2)}, u32[]{:S(2)}) async-start(bf16[128,32,256]{2,1,0:T(8,128)(2,1)} %bitcast.50), calls=%async_computation.2 | async-start | bytes 4194304 | tf_op jit(solution)/shard_map/all_to_all | solution.py:492
  150.6 25.5 %collective-permute-start.2 = (f32[8,128]{1,0:T(8,128)S(1)}, f32[8,128]{1,0:T(8,128)S(1)}, u32[]{:S(2)}, u32[]{:S(2)}) collective-permute-start(f32[8,128]{1,0:T(8,128)S(1)} %add.736), channel_id=1, source_target_pairs={{0,64},{32,96},{64,0},{96,32},{1,65},{33,97},{65,1},{97,33},{2,66}... | collective-permute-start | bytes 12296 | tf_op jit(solution)/shard_map/ppermute | solution.py:469
  181.9 1.5 copy-start

commit v10 on v9

--- a/solution.py
+++ b/solution.py
@@ -462,13 +462,12 @@
     )(image)
 
 
-def butterfly_sum(x, axis):
+def ring_sum(x, axis):
     size = lax.axis_size(axis)
-    step = 1
-    while step < size:
-        x = x + lax.ppermute(x, axis, [(i, i ^ step) for i in range(size)])
-        step *= 2
-    return x
+    return x + sum(
+        lax.ppermute(x, axis, [(i, (i + step) % size) for i in range(size)])
+        for step in range(1, size)
+    )
 
 
 def local(image, variance, psf_coef, correlations, row_start, row_frac, col_start, col_frac):
@@ -570,7 +569,7 @@
     tile = jnp.sum(jnp.sum(tile, axis=2), axis=1)
     own = lax.broadcasted_iota(jnp.int32, (8, LANES), 0) // cores == pair_at
     placed = jnp.zeros((8, LANES), F32).at[:, :exp_dev].set(jnp.tile(tile, (8 // cores, 1)))
-    tile = butterfly_sum(jnp.where(own, placed, 0.0), "y")
+    tile = ring_sum(jnp.where(own, placed, 0.0), "y")
     weight = 1.0 / (tile[:visits, :exp_dev].reshape(exposures) / (extent * width))
     mean_weight = jnp.mean(weight)
     pieces = exchange(

time: 184 us -> 185 us (level)
  starting transfers between devices: 36 us -> 33.9 us
    all_to_all x3, waiting for transfers between devices: 56.4 us -> 69.2 us  [exchange(): return lax.all_to_all(x, axis, split_axis=0, concat_axis=0, tiled=True)]
    ppermute x2 -> x3, waiting for transfers between devices: 12.2 us -> 0.01 us  [ring_sum(): lax.ppermute(x, axis, [(i, (i + step) % size) for i in range(size)])]
    all_to_all x3, starting transfers between devices: 30.9 us -> 28.4 us  [exchange(): return lax.all_to_all(x, axis, split_axis=0, concat_axis=0, tiled=True)]
    ppermute x2 -> x3, starting transfers between devices: 4.9 us -> 5.29 us  [ring_sum(): lax.ppermute(x, axis, [(i, (i + step) % size) for i in range(size)])]
  transfers between devices with their start and end apart: 6 -> 7, of which waited for: 3 -> 3; matrix products, arithmetic and copies ran while one was open for 20% -> 20% of each run, Pallas kernels for 15% -> 15%
where the time goes in v10:
time: 185 us; the launch traced here: 183 us
  waiting for transfers between devices  69.2 us (37%)
  Pallas kernels  38.3 us (21%)
  starting transfers between devices  33.9 us (18%)
  other arithmetic  33.5 us (18%)
  local copies, waits for them, and re-layouts  5.11 us (3%)
    all_to_all x3, waiting for transfers between devices, exchange(): return lax.all_to_all(x, axis, split_axis=0, concat_axis=0, tiled=True)  69.2 us
    all_to_all x3, starting transfers between devices, exchange(): return lax.all_to_all(x, axis, split_axis=0, concat_axis=0, tiled=True)  28.4 us
    pallas_call x1, Pallas kernels, col_warp(): pl.pallas_call(functools.partial(col_body, cols, slots, pixels), out_shap...  17.5 us
    add x1, other arithmetic, coverage(): running = running + jnp.where(inside, tap, 0.0)  10.2 us
    pallas_call x1, Pallas kernels, make_row_matrices(): pl.pallas_call(functools.partial(row_matrices_body, extent), out_shape=(j...  6.57 us
    pallas_call x1, Pallas kernels, row_warp(): pl.pallas_call(functools.partial(row_body, slots), out_shape=jax.ShapeDty...  6.36 us
    ppermute x3, starting transfers between devices, ring_sum(): lax.ppermute(x, axis, [(i, (i + step) % size) for i in range(size)])  5.29 us
    reduce_precision x4, other arithmetic, lanczos_taps(): return [lax.reduce_precision(value / total, 8, 7) for value in values]  4.39 us
  transfers between devices with their start and end apart: 7, of which 3 were waited for; matrix products, arithmetic and copies ran while one was open for 20% of the time, Pallas kernels for 15%

profile of v10, /device:TPU:4, one launch (start us, length us, event | category | flops | bytes accessed | tf_op | source)
XLA Modules:
  0.0 182.6 jit_solution(11635525434786673623)
XLA Ops:
  0.6 4.0 %split_columns.1 = bf16[16,256,512]{2,1,0:T(8,128)(2,1)} custom-call(bf16[4,256,2048]{2,1,0:T(8,128)(2,1)} %image_ref.1), custom_call_target="tpu_custom_call" | custom-call | tf_op jit(solution)/shard_map/split_columns/pallas_call | solution.py:450
  4.6 8.3 %all-to-all-start = ((bf16[16,256,512]{2,1,0:T(8,128)(2,1)}), bf16[16,256,512]{2,1,0:T(8,128)(2,1)}, u32[]{:S(2)}, u32[]{:S(2)}) async-start(bf16[16,256,512]{2,1,0:T(8,128)(2,1)} %split_columns.1), calls=%async_computation | async-start | bytes 8388608 | tf_op jit(solution)/shard_map/all_to_all | solution.py:491
  13.0 1.0 constant_dynamic-slice_fusion.4
  14.3 0.7 constant_dynamic-slice_fusion.3
  15.0 0.7 constant_dynamic-slice_fusion.1
  15.7 1.0 constant_dynamic-slice_fusion
  18.0 2.9 %convert_reduce_fusion = f32[4]{0:T(128)S(1)} fusion(bf16[4,256,2048]{2,1,0:T(8,128)(2,1)} %param.16), kind=kLoop, calls=%fused_computation | loop fusion | flops 4194300 | bytes 4194320 | tf_op jit(solution)/shard_map/reduce_sum | solution.py:515
  21.5 6.6 %row_matrices.1 = (bf16[16,256,256]{2,1,0:T(8,128)(2,1)S(1)}, bf16[512,288]{1,0:T(8,128)(2,1)S(1)}) custom-call(f32[1,21]{1,0:T(1,128)S(1)} %constant_dynamic-slice_fusion.2.kernel_ref, s32[16]{0:T(128)S(1)} %get-tuple-element.73.low_ref, f32[16,8,128]{2,1,0:T(8,128)S(1)} %select_add_fusion.1.turned_ref, s32[16,8,128]{2,1,0:T(8,128)S(1)} %and_subtract_fusion.1.key_ref), custom_call_target="tpu_custom_call" | custom-call | tf_op jit(solution)/shard_map/row_matrices/pallas_call | solution.py:148
  28.2 0.8 select_reduce_fusion.list_ref
  29.1 0.6 broadcast_compare_fusion
  29.7 42.4 %all-to-all-done = bf16[16,256,512]{2,1,0:T(8,128)(2,1)} async-done(((bf16[16,256,512]{2,1,0:T(8,128)(2,1)}), bf16[16,256,512]{2,1,0:T(8,128)(2,1)}, u32[]{:S(2)}, u32[]{:S(2)}) %all-to-all-start) | async-done | bytes 4194336 | tf_op jit(solution)/shard_map/all_to_all | solution.py:491
  72.1 6.4 %row_warp.1 = bf16[32,272,128]{2,1,0:T(8,128)(2,1)} custom-call(s32[16]{0:T(128)S(1)} %get-tuple-element.73.low_ref, s32[16]{0:T(128)S(1)} %get-tuple-element.72.num_ref, bf16[4096,512]{1,0:T(8,128)(2,1)} %bitcast.2.x_ref, bf16[16,256,256]{2,1,0:T(8,128)(2,1)S(1)} %get-tuple-element.54.rows_ref, bf16[512,288]{1,0:T(8,128)(2,1)S(1)} %get-tuple-element.55.blur_ref, ...), custom_call_target="tpu_custom_call" | custom-call | flops 2000000000 | bytes 8388608 | tf_op jit(solution)/shard_map/row_warp/pallas_call | solution.py:230
  78.5 14.1 %all-to-all-start.1 = ((bf16[32,272,128]{2,1,0:T(8,128)(2,1)}), bf16[32,272,128]{2,1,0:T(8,128)(2,1)S(1)}, u32[]{:S(2)}, u32[]{:S(2)}) async-start(bf16[32,272,128]{2,1,0:T(8,128)(2,1)} %row_warp.1), calls=%async_computation.1 | async-start | bytes 4456448 | tf_op jit(solution)/shard_map/all_to_all | solution.py:491
  92.6 0.7 select_reduce_fusion.2
  93.3 1.6 and_subtract_fusion.key_hbm
  94.9 2.1 %divide_reduce-precision_fusion.5 = (f32[16,32,128]{2,1,0:T(8,128)S(1)}, f32[16,32,128]{2,1,0:T(8,128)S(1)}) fusion(f32[16,32,128]{2,1,0:T(8,128)S(1)} %reshape.642), kind=kLoop, calls=%fused_computation.61 | loop fusion | flops 2555904 | bytes 786432 | tf_op jit(solution)/shard_map/reduce_precision | solution.py:62
  97.0 2.1 %divide_reduce-precision_fusion.4 = (f32[16,32,128]{2,1,0:T(8,128)S(1)}, f32[16,32,128]{2,1,0:T(8,128)S(1)}, f32[16,32,128]{2,1,0:T(8,128)S(1)}, f32[16,32,128]{2,1,0:T(8,128)S(1)}, f32[16,32,128]{2,1,0:T(8,128)S(1)}) fusion(f32[16,32,128]{2,1,0:T(8,128)S(1)} %get-tuple-element.69, f32[16,32,128]{2,1,0:T(8,128)S(1)} %reshape.642), kind=kLoop, calls=%fused_computation.60 | loop fusion | flops 2424832 | bytes 1835008 | tf_op jit(solution)/shard_map/reduce_precision | solution.py:62
  99.1 2.6 %select_add_fusion.turned_hbm = f32[16,32,8,128]{3,2,1,0:T(8,128)} fusion(f32[16,32,128]{2,1,0:T(8,128)S(1)} %get-tuple-element.80, f32[16,32,128]{2,1,0:T(8,128)S(1)} %get-tuple-element.77, f32[16,32,128]{2,1,0:T(8,128)S(1)} %get-tuple-element.78, f32[16,32,128]{2,1,0:T(8,128)S(1)} %get-tuple-element.79, f32[16,32,128]{2,1,0:T(8,128)S(1)} %get-tuple-element.76, ...), kind=kLoop, calls=%fused_computation.9 | loop fusion | flops 9961472 | bytes 3932160 | tf_op jit(solution)/shard_map/add | solution.py:80
  101.8 0.7 fusion.52.count_ref
  103.1 0.7 compare_reduce_fusion
  104.5 3.9 %col_matrices.1.blur_hbm = bf16[8,2,288,256]{3,2,1,0:T(8,128)(2,1)} custom-call(f32[8,21]{1,0:T(8,128)} %pad_maximum_fusion.kernel_ref), custom_call_target="tpu_custom_call" | custom-call | tf_op jit(solution)/shard_map/col_matrices/pallas_call | solution.py:172
  108.4 14.0 %all-to-all-done.1.z_hbm = bf16[32,272,128]{2,1,0:T(8,128)(2,1)S(1)} async-done(((bf16[32,272,128]{2,1,0:T(8,128)(2,1)}), bf16[32,272,128]{2,1,0:T(8,128)(2,1)S(1)}, u32[]{:S(2)}, u32[]{:S(2)}) %all-to-all-start.1) | async-done | bytes 2228256 | tf_op jit(solution)/shard_map/all_to_all | solution.py:491
  122.6 0.7 broadcast_select_fusion
  123.4 3.1 %collective-permute-start.3 = (f32[8,128]{1,0:T(8,128)S(1)}, f32[8,128]{1,0:T(8,128)S(1)}, u32[]{:S(2)}, u32[]{:S(2)}) collective-permute-start(f32[8,128]{1,0:T(8,128)S(1)} %select_n.336), channel_id=1, source_target_pairs={{0,96},{32,0},{64,32},{96,64},{1,97},{33,1},{65,33},{97,65},{2,98}... | collective-permute-start | bytes 12296 | tf_op jit(solution)/shard_map/ppermute | solution.py:468
  126.5 2.2 %collective-permute-start.2 = (f32[8,128]{1,0:T(8,128)S(1)}, f32[8,128]{1,0:T(8,128)S(1)}, u32[]{:S(2)}, u32[]{:S(2)}) collective-permute-start(f32[8,128]{1,0:T(8,128)S(1)} %select_n.336), channel_id=1, source_target_pairs={{0,64},{32,96},{64,0},{96,32},{1,65},{33,97},{65,1},{97,33},{2,66}... | collective-permute-start | bytes 12296 | tf_op jit(solution)/shard_map/ppermute | solution.py:468
  128.7 17.5 %col_warp.1 = bf16[8,16,32,256]{3,2,1,0:T(8,128)(2,1)} custom-call(s32[8]{0:T(128)} %fusion.52.count_ref, s32[8,16]{1,0:T(8,128)} %select_reduce_fusion.list_ref, s32[16,32]{1,0:T(8,128)} %get-tuple-element.95.low_ref, s32[16,32]{1,0:T(8,128)} %get-tuple-element.75.num_ref, s32[16]{0:T(128)} %min.41.from_ref, s32[16]{0:T(128)} %copy-done.6, ...), custom_call_target="tpu_custom_call" | custom-call | flops 8000000000 | bytes 16777216 | tf_op jit(solution)/shard_map/col_warp/pallas_call | solution.py:394
  146.2 6.0 %all-to-all-start.2 = ((bf16[128,32,256]{2,1,0:T(8,128)(2,1)}), bf16[128,32,256]{2,1,0:T(8,128)(2,1)S(1)}, u32[]{:S(2)}, u32[]{:S(2)}) async-start(bf16[128,32,256]{2,1,0:T(8,128)(2,1)} %bitcast.50), calls=%async_computation.2 | async-start | bytes 4194304 | tf_op jit(solution)/shard_map/all_to_all | solution.py:491
  152.2 10.2 %fusion.12 = f32[32,2,1024]{2,1,0:T(2,128)S(1)} fusion(s32[32,2,1024]{2,1,0:T(2,128)S(1)} %copy-done.2, f32[32,2,1024]{2,1,0:T(2,128)S(1)} %copy-done.3), kind=kLoop, calls=%fused_computation.37 | loop fusion | flops 5636096 | bytes 786432 | tf_op jit(solution)/shard_map/add | solution.py:70
  163.9 3.4 %fusion.31 = f32[32,2,256]{2,1,0:T(2,128)S(1)} fusion(f32[32,2,4096]{2,1,0:T(2,128)} %param.22, s32[]{:T(128)S(6)} %select_n.324, s32[32,2,4096]{2,1,0:T(2,128)} %param.21, f32[32,2]{1,0:T(8,128)S(1)} %copy.54), kind=kLoop, calls=%fused_computation.119 | loop fusion | flops 1425408 | bytes 196868 | tf_op jit(solution)/shard_map/mul | solution.py:601
  167.3 1.0 fusion.13
  168.3 12.8 %all-to-all-done.2 = bf16[128,32,256]{2,1,0:T(8,128)(2,1)S(1)} async-done(((bf16[128,32,256]{2,1,0:T(8,128)(2,1)}), bf16[128,32,256]{2,1,0:T(8,128)(2,1)S(1)}, u32[]{:S(2)}, u32[]{:S(2)}) %all-to-all-start.2) | async-done | bytes 2097184 | tf_op jit(solution)/shard_map/all_to_all | solution.py:491
  181.4 1.2 fusion.1
  (72 shorter events, 5.3 us)
Async XLA Ops:
  4.6 67.5 %all-to-all-start = ((bf16[16,256,512]{2,1,0:T(8,128)(2,1)}), bf16[16,256,512]{2,1,0:T(8,128)(2,1)}, u32[]{:S(2)}, u32[]{:S(2)}) async-start(bf16[16,256,512]{2,1,0:T(8,128)(2,1)} %split_columns.1), calls=%async_computation | async-start | bytes 8388608 | tf_op jit(solution)/shard_map/all_to_all | solution.py:491
  12.9 3.8 %copy-start.4 = (s32[32,2]{0,1:T(2,128)S(1)}, s32[32,2]{0,1:T(2,128)}, u32[]{:S(2)}) copy-start(s32[32,2]{0,1:T(2,128)} %param.18) | copy-start | bytes 772
  12.9 4.4 %copy-start.5 = (f32[4,3]{1,0:T(4,128)S(1)}, f32[4,3]{1,0:T(4,128)}, u32[]{:S(2)}) copy-start(f32[4,3]{1,0:T(4,128)} %param.17) | copy-start | bytes 148
  12.9 4.7 %copy-start.7 = (f32[3]{0:T(128)S(1)}, f32[3]{0:T(128)}, u32[]{:S(2)}) copy-start(f32[3]{0:T(128)} %constant.303) | copy-start | bytes 40
  78.5 43.9 %all-to-all-start.1 = ((bf16[32,272,128]{2,1,0:T(8,128)(2,1)}), bf16[32,272,128]{2,1,0:T(8,128)(2,1)S(1)}, u32[]{:S(2)}, u32[]{:S(2)}) async-start(bf16[32,272,128]{2,1,0:T(8,128)(2,1)} %row_warp.1), calls=%async_computation.1 | async-start | bytes 4456448 | tf_op jit(solution)/shard_map/all_to_all | solution.py:491
  93.3 9.2 %copy-start.6 = (s32[16]{0:T(128)}, s32[16]{0:T(128)S(1)}, u32[]{:S(2)}) copy-start(s32[16]{0:T(128)S(1)} %get-tuple-element.64.to_ref) | copy-start | bytes 196
  101.7 2.1 %collective-permute-start = (f32[8,128]{1,0:T(8,128)S(1)}, f32[8,128]{1,0:T(8,128)S(1)}, u32[]{:S(2)}, u32[]{:S(2)}) collective-permute-start(f32[8,128]{1,0:T(8,128)S(1)} %scatter.6), channel_id=1, source_target_pairs={{0,16},{16,0},{1,17},{17,1},{2,18},{18,2},{3,19},{19,3},{4,20},{20... | collective-permute-start | bytes 12296 | tf_op jit(solution)/shard_map/ppermute | solution.py:557
  122.3 6.4 %copy-start.1 = (bf16[32,272,128]{2,1,0:T(8,128)(2,1)}, bf16[32,272,128]{2,1,0:T(8,128)(2,1)S(1)}, u32[]{:S(2)}) copy-start(bf16[32,272,128]{2,1,0:T(8,128)(2,1)S(1)} %all-to-all-done.1.z_hbm) | copy-start | bytes 6684676
  123.4 39.0 %collective-permute-start.3 = (f32[8,128]{1,0:T(8,128)S(1)}, f32[8,128]{1,0:T(8,128)S(1)}, u32[]{:S(2)}, u32[]{:S(2)}) collective-permute-start(f32[8,128]{1,0:T(8,128)S(1)} %select_n.336), channel_id=1, source_target_pairs={{0,96},{32,0},{64,32},{96,64},{1,97},{33,1},{65,33},{97,65},{2,98}... | collective-permute-start | bytes 12296 | tf_op jit(solution)/shard_map/ppermute | solution.py:468
  126.5 36.0 %collective-permute-start.1 = (f32[8,128]{1,0:T(8,128)S(1)}, f32[8,128]{1,0:T(8,128)S(1)}, u32[]{:S(2)}, u32[]{:S(2)}) collective-permute-start(f32[8,128]{1,0:T(8,128)S(1)} %select_n.336), channel_id=1, source_target_pairs={{0,32},{32,64},{64,96},{96,0},{1,33},{33,65},{65,97},{97,1},{2,34}... | collective-permute-start | bytes 12296 | tf_op jit(solution)/shard_map/ppermute | solution.py:468
  126.5 36.0 %collective-permute-start.2 = (f32[8,128]{1,0:T(8,128)S(1)}, f32[8,128]{1,0:T(8,128)S(1)}, u32[]{:S(2)}, u32[]{:S(2)}) collective-permute-start(f32[8,128]{1,0:T(8,128)S(1)} %select_n.336), channel_id=1, source_target_pairs={{0,64},{32,96},{64,0},{96,32},{1,65},{33,97},{65,1},{97,33},{2,66}... | collective-permute-start | bytes 12296 | tf_op jit(solution)/shard_map/ppermute | solution.py:468
  146.2 6.0 %copy-start.2 = (s32[32,2,1024]{2,1,0:T(2,128)S(1)}, s32[32,2,1024]{2,1,0:T(2,128)}, u32[]{:S(2)}) copy-start(s32[32,2,1024]{2,1,0:T(2,128)} %param.19) | copy-start | bytes 786436
  146.2 6.0 %copy-start.3 = (f32[32,2,1024]{2,1,0:T(2,128)S(1)}, f32[32,2,1024]{2,1,0:T(2,128)}, u32[]{:S(2)}) copy-start(f32[32,2,1024]{2,1,0:T(2,128)} %param.20) | copy-start | bytes 786436
  146.2 34.9 %all-to-all-start.2 = ((bf16[128,32,256]{2,1,0:T(8,128)(2,1)}), bf16[128,32,256]{2,1,0:T(8,128)(2,1)S(1)}, u32[]{:S(2)}, u32[]{:S(2)}) async-start(bf16[128,32,256]{2,1,0:T(8,128)(2,1)} %bitcast.50), calls=%async_computation.2 | async-start | bytes 4194304 | tf_op jit(solution)/shard_map/all_to_all | solution.py:491
  168.3 14.3 %copy-start = (f32[1024,256,1]{1,0,2:T(8,128)}, f32[1024,256,1]{1,0,2:T(8,128)S(1)}, u32[]{:S(2)}) copy-start(f32[1024,256,1]{1,0,2:T(8,128)S(1)} %fusion.13) | copy-start | bytes 3145732
